TPU v7x, 32 devices: a whole 2x2x4 slice. The times are simulated.
32 devices in a mesh: grp: 2 (over y), row: 4 (over x, core), col: 4 (over z).
Axes of the slice: x: 2, y: 2, z: 4, core: 2. Of those that a mesh axis runs over, the one named last changes fastest.
Arguments:
- activations: bfloat16 [1280, 5120], P(('grp', 'row')), parts along dimension 0, may hold values from -6 to 6
- gradients: bfloat16 [1280, 5120], P(('grp', 'col')), parts along dimension 0, may hold values from -0.625 to 0.625
- input_basis: bfloat16 [10240, 5120], P(('grp', 'row'), 'col'), parts along dimension 0, may hold values from -0.078125 to 0.078125
- output_basis: bfloat16 [10240, 5120], P(('grp', 'col'), 'row'), parts along dimension 0, may hold values from -0.078125 to 0.078125
- seq_ids: int32 [1280], P('grp'), parts along dimension 0, may hold values from 0 to 3, never falling along the last dimension, each value on 1 to 320 neighbouring positions
Outputs:
- corrected: float32 [10240, 5120], P(('grp', 'col'), 'row'), parts along dimension 0
There are 2 independent parts, one for each index of `grp`. A program takes and returns all parts, laid end to end along the dimension named above; each array names one. Nothing has to cross between parts.
Inputs may be any that keep to these rules, and one draw needn't show every extreme that they name: `seq_ids`: sequence ids never fall along the tokens; every sequence has at least one token and at most 320, one exactly 320.
All inputs are finite; a program needn't handle non-finite values.
Results may differ from a plain program's by a relative error of at most 0.0041.
Values may be sent and summed in bfloat16 or wider, within the bound.
No kernel may reach another device: no remote copies, remote signals or barrier semaphores. Data moves between devices by JAX's collectives and lax.ppermute only.
A program may use at most 128 MiB of HBM per device.

v0:
```python
import jax
import jax.numpy as jnp
from jax import lax
from jax.sharding import PartitionSpec as P

SEQS = 4


def add_piece(values, piece):
    return jnp.dot(values, piece, preferred_element_type=jnp.float32)


def outer_sum(left, right):
    return lax.dot_general(
        left, right, (((0,), (0,)), ((), ())), preferred_element_type=jnp.float32
    )


def on_device(activations, gradients, input_basis, output_basis, seq_ids):
    act_proj = add_piece(activations, lax.all_gather(input_basis, "row", axis=0, tiled=True))
    grad_proj = add_piece(gradients, lax.all_gather(output_basis, "col", axis=0, tiled=True))
    act_proj = act_proj.astype(jnp.bfloat16)
    grad_proj = grad_proj.astype(jnp.bfloat16)
    grad_panel = lax.all_gather(grad_proj, "col", axis=0, tiled=True)
    total_rows = seq_ids.shape[0]
    act_panel = lax.all_gather(act_proj, "row", axis=0, tiled=True)
    window = total_rows // 2
    total = jnp.zeros((act_panel.shape[1], grad_panel.shape[1]), jnp.float32)
    for seq in range(SEQS):
        first = jnp.sum((seq_ids < seq).astype(jnp.int32))
        begin = jnp.minimum(first, total_rows - window)
        left = lax.dynamic_slice_in_dim(act_panel, begin, window, 0)
        right = lax.dynamic_slice_in_dim(grad_panel, begin, window, 0)
        ids_here = lax.dynamic_slice_in_dim(seq_ids, begin, window, 0)
        masked = left * (ids_here == seq).astype(jnp.bfloat16)[:, None]
        seq_sum = outer_sum(masked, right)
        total = total + seq_sum * seq_sum
    return total / SEQS


def solution(mesh):
    return jax.shard_map(
        on_device,
        mesh=mesh,
        in_specs=(
            P(("grp", "row"), None),
            P(("grp", "col"), None),
            P(("grp", "row"), "col"),
            P(("grp", "col"), "row"),
            P("grp"),
        ),
        out_specs=P(("grp", "col"), "row"),
        check_vma=False,
    )
```

profile of v0, /device:TPU:0, one launch (start us, length us, event | category | flops | bytes accessed | tf_op | source)
XLA Modules:
  0.0 403.6 jit_solution(5573550312229918936)
XLA Ops:
  6.5 0.0 copy-start
  6.5 0.0 all-gather.5.cloned.1.call-start
  6.5 0.7 all-gather.5.cloned.1.call-update
  7.3 0.0 all-gather.9.cloned.1.call-start
  7.3 0.7 all-gather.9.cloned.1.call-update
  8.0 0.0 copy-start.4
  8.0 0.0 all-gather.7.cloned.1.call-start
  8.1 88.7 %all-gather.5.cloned.1.call-done = bf16[5120,1280]{1,0:T(8,128)(2,1)} async-done(((bf16[1280,1280]{1,0:T(8,128)(2,1)}), bf16[5120,1280]{1,0:T(8,128)(2,1)}) %all-gather.5.cloned.1.call-update) | async-done | bytes 13107216 | tf_op jit(solution)/shard_map/all_gather | solution.py:20
  96.7 0.0 copy-done
  96.7 7.8 %convolution_convert_fusion.1 = bf16[160,1280]{1,0:T(8,128)(2,1)} fusion(bf16[160,5120]{1,0:T(8,128)(2,1)S(1)} %copy-done, bf16[5120,1280]{1,0:T(8,128)(2,1)} %all-gather.5.cloned.1.call-done), kind=kOutput, calls=%fused_computation.9 | convolution fusion | flops 2097356800 | bytes 15155200 | tf_op jit(solution)/shard_map/dot_general | solution.py:10
  104.5 0.0 all-gather.7.cloned.1.call-update
  104.5 0.0 copy-start.3
  104.5 0.2 all-gather.11.cloned.1.call-start
  104.8 220.4 %all-gather.9.cloned.1.call-done = bf16[5120,1280]{1,0:T(8,128)(2,1)} async-done(((bf16[1280,1280]{1,0:T(8,128)(2,1)}), bf16[5120,1280]{1,0:T(8,128)(2,1)}) %all-gather.9.cloned.1.call-update) | async-done | bytes 13107216 | tf_op jit(solution)/shard_map/all_gather | solution.py:21
  325.2 0.0 copy-done.4
  325.2 7.8 %convolution_convert_fusion = bf16[160,1280]{1,0:T(8,128)(2,1)} fusion(bf16[160,5120]{1,0:T(8,128)(2,1)S(1)} %copy-done.4, bf16[5120,1280]{1,0:T(8,128)(2,1)} %all-gather.9.cloned.1.call-done), kind=kOutput, calls=%fused_computation.8 | convolution fusion | flops 2097356800 | bytes 15155200 | tf_op jit(solution)/shard_map/dot_general | solution.py:10
  333.0 0.0 all-gather.11.cloned.1.call-update
  333.0 0.0 copy-done.3
  333.0 0.8 convert_reduce_fusion
  336.3 0.1 fusion.27
  336.4 8.6 %all-gather.7.cloned.1.call-done = bf16[640,1280]{1,0:T(8,128)(2,1)} async-done(((bf16[160,1280]{1,0:T(8,128)(2,1)}), bf16[640,1280]{1,0:T(8,128)(2,1)}) %all-gather.7.cloned.1.call-update) | async-done | bytes 1638416 | tf_op jit(solution)/shard_map/all_gather | solution.py:26
  345.0 39.6 %all-gather.11.cloned.1.call-done = bf16[640,1280]{1,0:T(8,128)(2,1)} async-done(((bf16[160,1280]{1,0:T(8,128)(2,1)}), bf16[640,1280]{1,0:T(8,128)(2,1)}) %all-gather.11.cloned.1.call-update) | async-done | bytes 1638416 | tf_op jit(solution)/shard_map/all_gather | solution.py:24
  384.7 0.0 copy-start.1
  384.7 0.0 copy-start.2
  384.7 3.6 convolution_multiply_fusion.2
  388.2 0.0 copy-done.1
  388.2 0.0 copy-done.2
  388.3 2.0 fusion
  390.3 2.0 fusion.1
  392.3 4.8 %fusion.3 = f32[1280,1280]{1,0:T(8,128)} fusion(f32[1280,1280]{1,0:T(8,128)S(1)} %fusion.1, bf16[640,1280]{1,0:T(8,128)(2,1)S(1)} %copy-done.2, s32[]{:T(128)S(6)} %select_n.11, bf16[640,1280]{1,0:T(8,128)(2,1)S(1)} %copy-done.1, bf16[320]{0:T(512)(128)(2,1)S(1)} %get-tuple-element.9), kind=kOutput, calls=%fused_computation.7 | convolution fusion | flops 1055129600 | bytes 14747648 | tf_op jit(solution)/shard_map/dot_general | solution.py:14
Async XLA Ops:
  6.5 90.2 %copy-start = (bf16[160,5120]{1,0:T(8,128)(2,1)S(1)}, bf16[160,5120]{1,0:T(8,128)(2,1)}, u32[]{:S(2)}) copy-start(bf16[160,5120]{1,0:T(8,128)(2,1)} %param.5) | copy-start | bytes 4915204
  6.5 90.2 %all-gather.5.cloned.1.call-start = ((), (), s32[]{:S(2)}) async-start(), calls=%async_computation | async-start | bytes 16384000 | tf_op jit(solution)/shard_map/all_gather | solution.py:20
  7.3 318.0 %all-gather.9.cloned.1.call-start = ((), (), s32[]{:S(2)}) async-start(), calls=%async_computation.2 | async-start | bytes 16384000 | tf_op jit(solution)/shard_map/all_gather | solution.py:21
  8.0 317.2 %copy-start.4 = (bf16[160,5120]{1,0:T(8,128)(2,1)S(1)}, bf16[160,5120]{1,0:T(8,128)(2,1)}, u32[]{:S(2)}) copy-start(bf16[160,5120]{1,0:T(8,128)(2,1)} %param.6) | copy-start | bytes 4915204
  8.0 337.0 %all-gather.7.cloned.1.call-start = ((), (), s32[]{:S(2)}) async-start(), calls=%async_computation.1 | async-start | bytes 2048000 | tf_op jit(solution)/shard_map/all_gather | solution.py:26
  104.5 228.5 %copy-start.3 = (s32[640]{0:T(1024)S(1)}, s32[640]{0:T(1024)}, u32[]{:S(2)}) copy-start(s32[640]{0:T(1024)} %param.9) | copy-start | bytes 7684
  104.5 280.1 %all-gather.11.cloned.1.call-start = ((), (), s32[]{:S(2)}) async-start(), calls=%async_computation.3 | async-start | bytes 2048000 | tf_op jit(solution)/shard_map/all_gather | solution.py:24
  384.7 3.6 copy-start.1
  384.7 3.6 copy-start.2
Sparse Core Ops, SparseCore 0:
  8.9 87.7 all-gather.4
  98.3 226.8 all-gather.8
  326.8 18.1 all-gather.6
  346.4 38.1 all-gather.10
where the time goes:
time: 404 us
  waiting for transfers between devices  359 us (89%)
  matrix products  28 us (7%)
  between operations  15.7 us (4%)
    all_gather x1, waiting for transfers between devices, on_device(): lax.all_gather(output_basis, 'col', axis=0, tiled=True)  220 us
    all_gather x1, waiting for transfers between devices, on_device(): lax.all_gather(input_basis, 'row', axis=0, tiled=True)  88.7 us
    all_gather x1, waiting for transfers between devices, on_device(): grad_panel = lax.all_gather(grad_proj, 'col', axis=0, tiled=True)  39.6 us
    dot_general x2, matrix products, add_piece(): return jnp.dot(values, piece, preferred_element_type=jnp.float32)  15.6 us
    dot_general x4, matrix products, outer_sum(): lax.dot_general(left, right, (((0,), (0,)), ((), ())), preferred_element_...  12.4 us
    all_gather x1, waiting for transfers between devices, on_device(): act_panel = lax.all_gather(act_proj, 'row', axis=0, tiled=True)  8.61 us
  transfers between devices with their start and end apart: 4, of which 4 were waited for; matrix products, arithmetic and copies ran while one was open for 4% of the time, Pallas kernels for 0%

commit v1 on v0

v1 whole, which is shorter than its diff:
```python
import jax
import jax.numpy as jnp
from jax import lax
from jax.sharding import PartitionSpec as P

SEQS = 4
BF16 = jnp.bfloat16
F32 = jnp.float32


def dot(values, piece):
    return jnp.dot(values, piece, preferred_element_type=F32)


def outer_sum(left, right):
    return lax.dot_general(
        left, right, (((0,), (0,)), ((), ())), preferred_element_type=F32
    )


def project_any(values, basis, axis):
    turned = lax.all_to_all(values, axis, split_axis=1, concat_axis=0, tiled=True)
    total = lax.psum_scatter(dot(turned, basis), axis, scatter_dimension=0, tiled=True)
    return lax.all_gather(total.astype(BF16), axis, axis=0, tiled=True)


def by_xor(values, axis, bits):
    return lax.ppermute(values, axis, [(i, i ^ bits) for i in range(4)])


def columns_of(values, index, width):
    return lax.dynamic_slice_in_dim(values, index * width, width, 1)


def place(blocks, indices, size):
    panel = jnp.zeros((4 * size, blocks[0].shape[1]), BF16)
    for block, index in zip(blocks, indices):
        panel = lax.dynamic_update_slice_in_dim(panel, block, index * size, 0)
    return panel


def project_square(values, basis):
    me = lax.axis_index("row")
    tokens, depth = values.shape[0], basis.shape[0]
    core = me % 2
    mine = columns_of(values, me, depth)
    for_core = columns_of(values, me ^ 1, depth)
    for_chip = columns_of(values, me // 2 ^ 1, 2 * depth)
    from_chip = by_xor(for_chip, "row", 2)
    from_core = by_xor(for_core, "row", 1)
    own = dot(mine, basis)
    part = dot(from_core, basis)
    near = own + by_xor(part, "row", 1)
    near_there = by_xor(near.astype(BF16), "row", 2)
    far_mine = columns_of(from_chip, core, depth)
    far_for_core = columns_of(from_chip, core ^ 1, depth)
    far_from_core = by_xor(far_for_core, "row", 1)
    far_part = dot(far_from_core, basis)
    far = dot(far_mine, basis) + by_xor(far_part, "row", 1)
    far_there = by_xor(far.astype(BF16), "row", 2)
    near = (near + far_there.astype(F32)).astype(BF16)
    far = (far + near_there.astype(F32)).astype(BF16)
    near_other = by_xor(near, "row", 1)
    far_other = by_xor(far, "row", 1)
    return place([near, far, near_other, far_other], [me, me ^ 2, me ^ 1, me ^ 3], tokens)


def project_line(values, basis):
    me = lax.axis_index("col")
    core = lax.axis_index("row") % 2
    tokens, depth = values.shape[0], basis.shape[0]
    half = tokens // 2
    right = me // 2
    inner = (me == 1) | (me == 2)
    own_half = lax.dynamic_slice_in_dim(values, core * half, half, 0)

    def fetch(index, send):
        piece = send(columns_of(own_half, index, depth))
        other = by_xor(piece, "row", 1)
        first = jnp.where(core == 0, piece, other)
        second = jnp.where(core == 0, other, piece)
        return jnp.concatenate([first, second], 0)

    beside = fetch(me ^ 1, lambda v: by_xor(v, "col", 1))
    across = fetch(3 - me, lambda v: by_xor(v, "col", 3))
    twice = fetch(me ^ 2, lambda v: by_xor(v, "col", 2))
    own = columns_of(values, me, depth)
    blocks = [
        jnp.where(inner, beside, own),
        jnp.where(inner, own, beside),
        jnp.where(inner, across, twice),
        jnp.where(inner, twice, across),
    ]
    parts = [dot(block, basis) for block in blocks]

    def step_outer(values, inward, outward):
        pairs = [(0, 1), (3, 2)] * inward + [(1, 0), (2, 3)] * outward
        return lax.ppermute(values, "col", pairs).astype(F32)

    arrived, sums, crossed = [], [], []
    for step in range(6):
        inward, outward = step < 4, step >= 2
        if outward:
            sent = (parts[5 - step] + crossed[step - 2]).astype(BF16)
        if inward:
            sent = jnp.where(inner, sent, parts[step].astype(BF16)) if outward else parts[step].astype(BF16)
        arrived.append(step_outer(sent, inward, outward))
        if inward:
            sums.append(parts[step] + arrived[step])
            crossed.append(
                lax.ppermute(sums[step].astype(BF16), "col", [(1, 2), (2, 1)]).astype(F32)
            )
    done = [
        jnp.where(inner, sums[j] + crossed[3 - j], parts[j] + arrived[5 - j]).astype(BF16)
        for j in range(4)
    ]
    return place(done, [jnp.where(right == 1, 3 - j, j) for j in range(4)], tokens)


def on_device(rows, cols, activations, gradients, input_basis, output_basis, seq_ids):
    if rows == 4 and cols == 4:
        grad_panel = project_line(gradients, output_basis)
        act_panel = project_square(activations, input_basis)
    else:
        act_panel = project_any(activations, input_basis, "row")
        grad_panel = project_any(gradients, output_basis, "col")
    total_rows = seq_ids.shape[0]
    window = total_rows // 2
    total = jnp.zeros((act_panel.shape[1], grad_panel.shape[1]), F32)
    for seq in range(SEQS):
        first = jnp.sum((seq_ids < seq).astype(jnp.int32))
        begin = jnp.minimum(first, total_rows - window)
        left = lax.dynamic_slice_in_dim(act_panel, begin, window, 0)
        right = lax.dynamic_slice_in_dim(grad_panel, begin, window, 0)
        ids_here = lax.dynamic_slice_in_dim(seq_ids, begin, window, 0)
        masked = left * (ids_here == seq).astype(BF16)[:, None]
        seq_sum = outer_sum(masked, right)
        total = total + seq_sum * seq_sum
    return total / SEQS


def solution(mesh):
    def body(*args):
        return on_device(mesh.shape["row"], mesh.shape["col"], *args)

    return jax.shard_map(
        body,
        mesh=mesh,
        in_specs=(
            P(("grp", "row"), None),
            P(("grp", "col"), None),
            P(("grp", "row"), "col"),
            P(("grp", "col"), "row"),
            P("grp"),
        ),
        out_specs=P(("grp", "col"), "row"),
        check_vma=False,
    )
```

time: 404 us -> 125 us (0.31)
  waiting for transfers between devices: 359 us -> 49 us
  starting transfers between devices: 0.3 us -> 38.1 us
  between operations: 15.7 us -> 2.91 us
  local copies, waits for them, and re-layouts: 0.02 us -> 7.64 us
  matrix products: 28 us -> 21.2 us
  other arithmetic: 0.84 us -> 5.25 us
    all_gather x4 -> x0, waiting for transfers between devices: 357 us -> none  [the longest x1 220 us: on_device(): lax.all_gather(output_basis, 'col', axis=0, tiled=True)]
    ppermute x0 -> x25, waiting for transfers between devices: none -> 49 us  [the longest x6 36.3 us: step_outer(): return lax.ppermute(values, 'col', pairs).astype(F32)]
    ppermute x0 -> x25, starting transfers between devices: none -> 38.1 us  [the longest x6 23.1 us: step_outer(): return lax.ppermute(values, 'col', pairs).astype(F32)]
    dynamic_slice x0 -> x4, local copies, waits for them, and re-layouts: none -> 7.34 us  [columns_of(): return lax.dynamic_slice_in_dim(values, index * width, width, 1)]
    dot_general x2 -> x8, matrix products: 15.6 us -> 9.88 us  [dot(): return jnp.dot(values, piece, preferred_element_type=F32)]
  transfers between devices with their start and end apart: 4 -> 25, of which waited for: 4 -> 8; matrix products, arithmetic and copies ran while one was open for 4% -> 17% of each run, Pallas kernels for 0% -> 0%
where the time goes in v1:
time: 125 us; the launch traced here: 124 us
  waiting for transfers between devices  49 us (39%)
  starting transfers between devices  38.1 us (30%)
  matrix products  21.2 us (17%)
  local copies, waits for them, and re-layouts  7.64 us (6%)
  other arithmetic  5.25 us (4%)
  between operations  2.91 us (2%)
    ppermute x6, waiting for transfers between devices, step_outer(): return lax.ppermute(values, 'col', pairs).astype(F32)  36.3 us
    ppermute x6, starting transfers between devices, step_outer(): return lax.ppermute(values, 'col', pairs).astype(F32)  23.1 us
    ppermute x15, waiting for transfers between devices, by_xor(): return lax.ppermute(values, axis, [(i, i ^ bits) for i in range(4)])  12.6 us
    ppermute x15, starting transfers between devices, by_xor(): return lax.ppermute(values, axis, [(i, i ^ bits) for i in range(4)])  12.3 us
    dot_general x4, matrix products, outer_sum(): lax.dot_general(left, right, (((0,), (0,)), ((), ())), preferred_element_...  11.3 us
    dot_general x8, matrix products, dot(): return jnp.dot(values, piece, preferred_element_type=F32)  9.88 us
    dynamic_slice x4, local copies, waits for them, and re-layouts, columns_of(): return lax.dynamic_slice_in_dim(values, index * width, width, 1)  7.34 us
    select_n x3, other arithmetic, fetch(): first = jnp.where(core == 0, piece, other)  2.89 us
  transfers between devices with their start and end apart: 25, of which 8 were waited for; matrix products, arithmetic and copies ran while one was open for 17% of the time, Pallas kernels for 0%

profile of v1, /device:TPU:0, one launch (start us, length us, event | category | flops | bytes accessed | tf_op | source)
XLA Modules:
  0.0 124.1 jit_solution(4199500494705696555)
XLA Ops:
  0.0 1.9 %constant_dynamic-slice_fusion.2 = bf16[160,1280]{1,0:T(8,128)(2,1)} fusion(bf16[160,5120]{1,0:T(8,128)(2,1)} %param.5, s32[]{:T(128)S(6)} %select_n.186), kind=kLoop, calls=%fused_computation.103 | loop fusion | bytes 819204 | tf_op jit(solution)/shard_map/dynamic_slice | solution.py:32
  2.4 2.3 %fusion.75 = (bf16[80,1280]{1,0:T(8,128)(2,1)}, bf16[80,1280]{1,0:T(8,128)(2,1)}, bf16[80,1280]{1,0:T(8,128)(2,1)S(1)}) fusion(bf16[160,5120]{1,0:T(8,128)(2,1)} %param.6, s32[]{:T(128)S(6)} %select_n.200, s32[]{:T(128)S(6)} %select_n.208, s32[]{:T(128)S(6)} %select_n.202, s32[]{:T(128)S(6)} %select_n.212), kind=kLoop, calls=%fused_computation.121 | loop fusion | bytes 1228816 | tf_op jit(solution)/shard_map/dynamic_slice | solution.py:32
  4.7 3.6 %collective-permute-start.12 = (bf16[80,1280]{1,0:T(8,128)(2,1)}, bf16[80,1280]{1,0:T(8,128)(2,1)}, u32[]{:S(2)}, u32[]{:S(2)}) collective-permute-start(bf16[80,1280]{1,0:T(8,128)(2,1)} %get-tuple-element.15), channel_id=1, source_target_pairs={{0,2},{1,3},{2,0},{3,1},{4,6},{5,7},{6,4},{7,5},{8,10},{9,11},{10,... | collective-permute-start | bytes 614408 | tf_op jit(solution)/shard_map/ppermute | solution.py:28
  8.3 1.6 %collective-permute-start.9 = (bf16[80,1280]{1,0:T(8,128)(2,1)}, bf16[80,1280]{1,0:T(8,128)(2,1)}, u32[]{:S(2)}, u32[]{:S(2)}) collective-permute-start(bf16[80,1280]{1,0:T(8,128)(2,1)} %get-tuple-element.16), channel_id=1, source_target_pairs={{0,1},{1,0},{2,3},{3,2},{4,5},{5,4},{6,7},{7,6},{8,9},{9,8},{10,11... | collective-permute-start | bytes 614408 | tf_op jit(solution)/shard_map/ppermute | solution.py:28
  9.9 2.1 %constant_dynamic-slice_fusion.1 = bf16[160,2560]{1,0:T(8,128)(2,1)} fusion(bf16[160,5120]{1,0:T(8,128)(2,1)} %param.5, s32[]{:T(128)S(6)} %select_n.188), kind=kLoop, calls=%fused_computation.102 | loop fusion | bytes 1638404 | tf_op jit(solution)/shard_map/dynamic_slice | solution.py:32
  11.9 1.7 %collective-permute-start.2 = (bf16[160,2560]{1,0:T(8,128)(2,1)}, bf16[160,2560]{1,0:T(8,128)(2,1)}, u32[]{:S(2)}, u32[]{:S(2)}) collective-permute-start(bf16[160,2560]{1,0:T(8,128)(2,1)} %constant_dynamic-slice_fusion.1), channel_id=1, source_target_pairs={{0,8},{4,12},{8,0},{12,4},{1,9},{5,13},{9,1},{13,5},{2,10},{6,14},... | collective-permute-start | bytes 2457608 | tf_op jit(solution)/shard_map/ppermute | solution.py:28
  17.0 2.0 %collective-permute-done.12 = bf16[80,1280]{1,0:T(8,128)(2,1)} collective-permute-done((bf16[80,1280]{1,0:T(8,128)(2,1)}, bf16[80,1280]{1,0:T(8,128)(2,1)}, u32[]{:S(2)}, u32[]{:S(2)}) %collective-permute-start.12) | collective-permute-done | bytes 204832 | tf_op jit(solution)/shard_map/ppermute | solution.py:28
  19.5 4.8 %collective-permute-done.14 = bf16[80,1280]{1,0:T(8,128)(2,1)} collective-permute-done((bf16[80,1280]{1,0:T(8,128)(2,1)S(1)}, bf16[80,1280]{1,0:T(8,128)(2,1)}, u32[]{:S(2)}, u32[]{:S(2)}) %collective-permute-start.14) | collective-permute-done | bytes 204832 | tf_op jit(solution)/shard_map/ppermute | solution.py:28
  24.3 2.8 %fusion.79 = f32[160,1280]{1,0:T(8,128)S(1)} fusion(bf16[160,1280]{1,0:T(8,128)(2,1)} %collective-permute-done, bf16[1280,1280]{1,0:T(8,128)(2,1)} %param.7), kind=kOutput, calls=%fused_computation.125 | convolution fusion | flops 524288000 | bytes 4505600 | tf_op jit(solution)/shard_map/dot_general | solution.py:12
  27.6 1.0 broadcast_select_fusion.5
  29.4 5.7 %collective-permute-start.16 = (bf16[160,1280]{1,0:T(8,128)(2,1)S(1)}, bf16[160,1280]{1,0:T(8,128)(2,1)S(1)}, u32[]{:S(2)}, u32[]{:S(2)}) collective-permute-start(bf16[160,1280]{1,0:T(8,128)(2,1)S(1)} %get-tuple-element.30), channel_id=1, source_target_pairs={{0,1},{3,2},{4,5},{7,6},{8,9},{11,10},{12,13},{15,14},{16,17},{19,... | collective-permute-start | bytes 1228808 | tf_op jit(solution)/shard_map/ppermute | solution.py:98
  35.8 1.3 %collective-permute-start.11 = (bf16[160,1280]{1,0:T(8,128)(2,1)S(1)}, bf16[160,1280]{1,0:T(8,128)(2,1)S(1)}, u32[]{:S(2)}, u32[]{:S(2)}) collective-permute-start(bf16[160,1280]{1,0:T(8,128)(2,1)S(1)} %get-tuple-element.28), channel_id=1, source_target_pairs={{0,1},{3,2},{4,5},{7,6},{8,9},{11,10},{12,13},{15,14},{16,17},{19,... | collective-permute-start | bytes 1228808 | tf_op jit(solution)/shard_map/ppermute | solution.py:98
  37.2 1.0 broadcast_select_fusion.3
  38.1 1.0 broadcast_select_fusion.1
  39.1 5.8 %collective-permute-done.16 = bf16[160,1280]{1,0:T(8,128)(2,1)S(1)} collective-permute-done((bf16[160,1280]{1,0:T(8,128)(2,1)S(1)}, bf16[160,1280]{1,0:T(8,128)(2,1)S(1)}, u32[]{:S(2)}, u32[]{:S(2)}) %collective-permute-start.16) | collective-permute-done | bytes 409632 | tf_op jit(solution)/shard_map/ppermute | solution.py:98
  45.7 7.1 %collective-permute-done.11 = bf16[160,1280]{1,0:T(8,128)(2,1)S(1)} collective-permute-done((bf16[160,1280]{1,0:T(8,128)(2,1)S(1)}, bf16[160,1280]{1,0:T(8,128)(2,1)S(1)}, u32[]{:S(2)}, u32[]{:S(2)}) %collective-permute-start.11) | collective-permute-done | bytes 409632 | tf_op jit(solution)/shard_map/ppermute | solution.py:98
  53.6 1.0 constant_dynamic-slice_fusion
  56.2 13.3 %collective-permute-start.22 = (bf16[160,1280]{1,0:T(8,128)(2,1)S(1)}, bf16[160,1280]{1,0:T(8,128)(2,1)S(1)}, u32[]{:S(2)}, u32[]{:S(2)}) collective-permute-start(bf16[160,1280]{1,0:T(8,128)(2,1)S(1)} %get-tuple-element.13), channel_id=1, source_target_pairs={{0,1},{3,2},{1,0},{2,3},{4,5},{7,6},{5,4},{6,7},{8,9},{11,10},{9,8... | collective-permute-start | bytes 1228808 | tf_op jit(solution)/shard_map/ppermute | solution.py:98
  70.3 1.7 %add_convert_fusion.2 = (bf16[160,1280]{1,0:T(8,128)(2,1)S(1)}, f32[160,1280]{1,0:T(8,128)S(1)}) fusion(f32[160,1280]{1,0:T(8,128)S(1)} %collective-permute-done.1, bf16[1280,1280]{1,0:T(8,128)(2,1)S(1)} %copy-done.1, bf16[160,5120]{1,0:T(8,128)(2,1)} %param.5, s32[]{:T(128)S(6)} %select_n.185), kind=kOutput, calls=%fused_computation.81 | convolution fusion | flops 524697600 | bytes 5734404 | tf_op jit(solution)/shard_map/dot_general | solution.py:12
  72.1 1.6 %collective-permute-start.6 = (bf16[160,1280]{1,0:T(8,128)(2,1)S(1)}, bf16[160,1280]{1,0:T(8,128)(2,1)S(1)}, u32[]{:S(2)}, u32[]{:S(2)}) collective-permute-start(bf16[160,1280]{1,0:T(8,128)(2,1)S(1)} %get-tuple-element.35), channel_id=1, source_target_pairs={{0,8},{4,12},{8,0},{12,4},{1,9},{5,13},{9,1},{13,5},{2,10},{6,14},... | collective-permute-start | bytes 1228808 | tf_op jit(solution)/shard_map/ppermute | solution.py:28
  73.7 5.8 %collective-permute-done.22 = bf16[160,1280]{1,0:T(8,128)(2,1)S(1)} collective-permute-done((bf16[160,1280]{1,0:T(8,128)(2,1)S(1)}, bf16[160,1280]{1,0:T(8,128)(2,1)S(1)}, u32[]{:S(2)}, u32[]{:S(2)}) %collective-permute-start.22) | collective-permute-done | bytes 409632 | tf_op jit(solution)/shard_map/ppermute | solution.py:98
  80.2 6.3 %collective-permute-done.18 = bf16[160,1280]{1,0:T(8,128)(2,1)S(1)} collective-permute-done((bf16[160,1280]{1,0:T(8,128)(2,1)S(1)}, bf16[160,1280]{1,0:T(8,128)(2,1)S(1)}, u32[]{:S(2)}, u32[]{:S(2)}) %collective-permute-start.18) | collective-permute-done | bytes 409632 | tf_op jit(solution)/shard_map/ppermute | solution.py:98
  87.3 1.7 %fusion.78 = (bf16[160,1280]{1,0:T(8,128)(2,1)S(1)}, f32[160,1280]{1,0:T(8,128)S(1)}) fusion(f32[160,1280]{1,0:T(8,128)S(1)} %collective-permute-done.4, bf16[1280,1280]{1,0:T(8,128)(2,1)S(1)} %copy-done.1, bf16[160,2560]{1,0:T(8,128)(2,1)} %collective-permute-done.2, s32[]{:T(128)S(6)} %select_n.190), kind=kOutput, calls=%fused_computation.124 | convolution fusion | flops 524697600 | bytes 5734404 | tf_op jit(solution)/shard_map/dot_general | solution.py:12
  89.0 1.6 %collective-permute-start.5 = (bf16[160,1280]{1,0:T(8,128)(2,1)S(1)}, bf16[160,1280]{1,0:T(8,128)(2,1)S(1)}, u32[]{:S(2)}, u32[]{:S(2)}) collective-permute-start(bf16[160,1280]{1,0:T(8,128)(2,1)S(1)} %get-tuple-element.33), channel_id=1, source_target_pairs={{0,8},{4,12},{8,0},{12,4},{1,9},{5,13},{9,1},{13,5},{2,10},{6,14},... | collective-permute-start | bytes 1228808 | tf_op jit(solution)/shard_map/ppermute | solution.py:28
  90.7 1.3 %collective-permute-start.24 = (bf16[160,1280]{1,0:T(8,128)(2,1)S(1)}, bf16[160,1280]{1,0:T(8,128)(2,1)S(1)}, u32[]{:S(2)}, u32[]{:S(2)}) collective-permute-start(bf16[160,1280]{1,0:T(8,128)(2,1)S(1)} %fusion.15), channel_id=1, source_target_pairs={{1,0},{2,3},{5,4},{6,7},{9,8},{10,11},{13,12},{14,15},{17,16},{18,... | collective-permute-start | bytes 1228808 | tf_op jit(solution)/shard_map/ppermute | solution.py:98
  92.1 1.5 %collective-permute-start.20 = (bf16[160,1280]{1,0:T(8,128)(2,1)S(1)}, bf16[160,1280]{1,0:T(8,128)(2,1)S(1)}, u32[]{:S(2)}, u32[]{:S(2)}) collective-permute-start(bf16[160,1280]{1,0:T(8,128)(2,1)S(1)} %fusion.9), channel_id=1, source_target_pairs={{1,0},{2,3},{5,4},{6,7},{9,8},{10,11},{13,12},{14,15},{17,16},{18,... | collective-permute-start | bytes 1228808 | tf_op jit(solution)/shard_map/ppermute | solution.py:98
  93.6 5.8 %collective-permute-done.5 = bf16[160,1280]{1,0:T(8,128)(2,1)S(1)} collective-permute-done((bf16[160,1280]{1,0:T(8,128)(2,1)S(1)}, bf16[160,1280]{1,0:T(8,128)(2,1)S(1)}, u32[]{:S(2)}, u32[]{:S(2)}) %collective-permute-start.5) | collective-permute-done | bytes 409632 | tf_op jit(solution)/shard_map/ppermute | solution.py:28
  100.2 11.3 %collective-permute-done.20 = bf16[160,1280]{1,0:T(8,128)(2,1)S(1)} collective-permute-done((bf16[160,1280]{1,0:T(8,128)(2,1)S(1)}, bf16[160,1280]{1,0:T(8,128)(2,1)S(1)}, u32[]{:S(2)}, u32[]{:S(2)}) %collective-permute-start.20) | collective-permute-done | bytes 409632 | tf_op jit(solution)/shard_map/ppermute | solution.py:98
  112.7 2.0 %convolution_multiply_fusion = f32[1280,1280]{1,0:T(8,128)S(1)} fusion(bf16[640,1280]{1,0:T(8,128)(2,1)S(1)} %fusion.33, s32[]{:T(128)S(6)} %select_n.235, bf16[640,1280]{1,0:T(8,128)(2,1)S(1)} %constant_dynamic-update-slice_fusion, bf16[320]{0:T(512)(128)(2,1)S(1)} %get-tuple-element.26), kind=kOutput, calls=%fused_computation | convolution fusion | flops 1051852800 | bytes 8194048 | tf_op jit(solution)/shard_map/dot_general | solution.py:16
  114.8 2.0 %convolution_multiply_fusion.1 = f32[1280,1280]{1,0:T(8,128)S(1)} fusion(bf16[640,1280]{1,0:T(8,128)(2,1)S(1)} %fusion.33, s32[]{:T(128)S(6)} %select_n.234, bf16[640,1280]{1,0:T(8,128)(2,1)S(1)} %constant_dynamic-update-slice_fusion, bf16[320]{0:T(512)(128)(2,1)S(1)} %get-tuple-element.25), kind=kOutput, calls=%fused_computation.1 | convolution fusion | flops 1051852800 | bytes 8194048 | tf_op jit(solution)/shard_map/dot_general | solution.py:16
  116.8 2.0 %convolution_multiply_fusion.2 = f32[1280,1280]{1,0:T(8,128)S(1)} fusion(bf16[640,1280]{1,0:T(8,128)(2,1)S(1)} %fusion.33, s32[]{:T(128)S(6)} %select_n.233, bf16[640,1280]{1,0:T(8,128)(2,1)S(1)} %constant_dynamic-update-slice_fusion, bf16[320]{0:T(512)(128)(2,1)S(1)} %get-tuple-element.27), kind=kOutput, calls=%fused_computation.2 | convolution fusion | flops 1051852800 | bytes 8194048 | tf_op jit(solution)/shard_map/dot_general | solution.py:16
  118.8 5.2 %fusion.3 = f32[1280,1280]{1,0:T(8,128)} fusion(f32[1280,1280]{1,0:T(8,128)S(1)} %convolution_multiply_fusion, f32[1280,1280]{1,0:T(8,128)S(1)} %convolution_multiply_fusion.1, f32[1280,1280]{1,0:T(8,128)S(1)} %convolution_multiply_fusion.2, bf16[640,1280]{1,0:T(8,128)(2,1)S(1)} %fusion.33, s32[]{:T(128)S(6)} %select_n.196, ...), kind=kOutput, calls=%fused_computation.7 | convolution fusion | flops 1058406400 | bytes 27854848 | tf_op jit(solution)/shard_map/dot_general | solution.py:16
  (63 shorter events, 11.4 us)
Async XLA Ops:
  0.0 28.6 %copy-start = (bf16[1280,1280]{1,0:T(8,128)(2,1)S(1)}, bf16[1280,1280]{1,0:T(8,128)(2,1)}, u32[]{:S(2)}) copy-start(bf16[1280,1280]{1,0:T(8,128)(2,1)} %param.8) | copy-start | bytes 9830404
  1.9 11.7 %copy-start.3 = (s32[640]{0:T(1024)S(1)}, s32[640]{0:T(1024)}, u32[]{:S(2)}) copy-start(s32[640]{0:T(1024)} %param.9) | copy-start | bytes 7684
  2.0 22.3 %collective-permute-start = (bf16[160,1280]{1,0:T(8,128)(2,1)}, bf16[160,1280]{1,0:T(8,128)(2,1)}, u32[]{:S(2)}, u32[]{:S(2)}) collective-permute-start(bf16[160,1280]{1,0:T(8,128)(2,1)} %constant_dynamic-slice_fusion.2), channel_id=1, source_target_pairs={{0,4},{4,0},{8,12},{12,8},{1,5},{5,1},{9,13},{13,9},{2,6},{6,2},{1... | collective-permute-start | bytes 1228808 | tf_op jit(solution)/shard_map/ppermute | solution.py:28
  4.7 14.3 %collective-permute-start.12 = (bf16[80,1280]{1,0:T(8,128)(2,1)}, bf16[80,1280]{1,0:T(8,128)(2,1)}, u32[]{:S(2)}, u32[]{:S(2)}) collective-permute-start(bf16[80,1280]{1,0:T(8,128)(2,1)} %get-tuple-element.15), channel_id=1, source_target_pairs={{0,2},{1,3},{2,0},{3,1},{4,6},{5,7},{6,4},{7,5},{8,10},{9,11},{10,... | collective-permute-start | bytes 614408 | tf_op jit(solution)/shard_map/ppermute | solution.py:28
  8.3 10.7 %collective-permute-start.9 = (bf16[80,1280]{1,0:T(8,128)(2,1)}, bf16[80,1280]{1,0:T(8,128)(2,1)}, u32[]{:S(2)}, u32[]{:S(2)}) collective-permute-start(bf16[80,1280]{1,0:T(8,128)(2,1)} %get-tuple-element.16), channel_id=1, source_target_pairs={{0,1},{1,0},{2,3},{3,2},{4,5},{5,4},{6,7},{7,6},{8,9},{9,8},{10,11... | collective-permute-start | bytes 614408 | tf_op jit(solution)/shard_map/ppermute | solution.py:28
  9.9 14.4 %collective-permute-start.14 = (bf16[80,1280]{1,0:T(8,128)(2,1)S(1)}, bf16[80,1280]{1,0:T(8,128)(2,1)}, u32[]{:S(2)}, u32[]{:S(2)}) collective-permute-start(bf16[80,1280]{1,0:T(8,128)(2,1)S(1)} %get-tuple-element.17), channel_id=1, source_target_pairs={{0,3},{1,2},{2,1},{3,0},{4,7},{5,6},{6,5},{7,4},{8,11},{9,10},{10,... | collective-permute-start | bytes 614408 | tf_op jit(solution)/shard_map/ppermute | solution.py:28
  11.9 41.6 %collective-permute-start.2 = (bf16[160,2560]{1,0:T(8,128)(2,1)}, bf16[160,2560]{1,0:T(8,128)(2,1)}, u32[]{:S(2)}, u32[]{:S(2)}) collective-permute-start(bf16[160,2560]{1,0:T(8,128)(2,1)} %constant_dynamic-slice_fusion.1), channel_id=1, source_target_pairs={{0,8},{4,12},{8,0},{12,4},{1,9},{5,13},{9,1},{13,5},{2,10},{6,14},... | collective-permute-start | bytes 2457608 | tf_op jit(solution)/shard_map/ppermute | solution.py:28
  17.0 11.6 %copy-start.2 = (bf16[160,5120]{1,0:T(8,128)(2,1)S(1)}, bf16[160,5120]{1,0:T(8,128)(2,1)}, u32[]{:S(2)}) copy-start(bf16[160,5120]{1,0:T(8,128)(2,1)} %param.6) | copy-start | bytes 4915204
  18.9 16.9 %collective-permute-start.13 = (bf16[80,1280]{1,0:T(8,128)(2,1)}, bf16[80,1280]{1,0:T(8,128)(2,1)S(1)}, u32[]{:S(2)}, u32[]{:S(2)}) collective-permute-start(bf16[80,1280]{1,0:T(8,128)(2,1)} %collective-permute-done.12), channel_id=1, source_target_pairs={{0,4},{4,0},{8,12},{12,8},{1,5},{5,1},{9,13},{13,9},{2,6},{6,2},{1... | collective-permute-start | bytes 614408 | tf_op jit(solution)/shard_map/ppermute | solution.py:28
  19.0 8.7 %collective-permute-start.10 = (bf16[80,1280]{1,0:T(8,128)(2,1)}, bf16[80,1280]{1,0:T(8,128)(2,1)S(1)}, u32[]{:S(2)}, u32[]{:S(2)}) collective-permute-start(bf16[80,1280]{1,0:T(8,128)(2,1)} %collective-permute-done.9), channel_id=1, source_target_pairs={{0,4},{4,0},{8,12},{12,8},{1,5},{5,1},{9,13},{13,9},{2,6},{6,2},{1... | collective-permute-start | bytes 614408 | tf_op jit(solution)/shard_map/ppermute | solution.py:28
  24.3 13.8 %collective-permute-start.15 = (bf16[80,1280]{1,0:T(8,128)(2,1)}, bf16[80,1280]{1,0:T(8,128)(2,1)S(1)}, u32[]{:S(2)}, u32[]{:S(2)}) collective-permute-start(bf16[80,1280]{1,0:T(8,128)(2,1)} %collective-permute-done.14), channel_id=1, source_target_pairs={{0,4},{4,0},{8,12},{12,8},{1,5},{5,1},{9,13},{13,9},{2,6},{6,2},{1... | collective-permute-start | bytes 614408 | tf_op jit(solution)/shard_map/ppermute | solution.py:28
  27.1 43.2 %collective-permute-start.1 = (f32[160,1280]{1,0:T(8,128)S(1)}, f32[160,1280]{1,0:T(8,128)S(1)}, u32[]{:S(2)}, u32[]{:S(2)}) collective-permute-start(f32[160,1280]{1,0:T(8,128)S(1)} %fusion.79), channel_id=1, source_target_pairs={{0,4},{4,0},{8,12},{12,8},{1,5},{5,1},{9,13},{13,9},{2,6},{6,2},{1... | collective-permute-start | bytes 2457608 | tf_op jit(solution)/shard_map/ppermute | solution.py:28
  29.4 15.5 %collective-permute-start.16 = (bf16[160,1280]{1,0:T(8,128)(2,1)S(1)}, bf16[160,1280]{1,0:T(8,128)(2,1)S(1)}, u32[]{:S(2)}, u32[]{:S(2)}) collective-permute-start(bf16[160,1280]{1,0:T(8,128)(2,1)S(1)} %get-tuple-element.30), channel_id=1, source_target_pairs={{0,1},{3,2},{4,5},{7,6},{8,9},{11,10},{12,13},{15,14},{16,17},{19,... | collective-permute-start | bytes 1228808 | tf_op jit(solution)/shard_map/ppermute | solution.py:98
  35.8 16.9 %collective-permute-start.11 = (bf16[160,1280]{1,0:T(8,128)(2,1)S(1)}, bf16[160,1280]{1,0:T(8,128)(2,1)S(1)}, u32[]{:S(2)}, u32[]{:S(2)}) collective-permute-start(bf16[160,1280]{1,0:T(8,128)(2,1)S(1)} %get-tuple-element.28), channel_id=1, source_target_pairs={{0,1},{3,2},{4,5},{7,6},{8,9},{11,10},{12,13},{15,14},{16,17},{19,... | collective-permute-start | bytes 1228808 | tf_op jit(solution)/shard_map/ppermute | solution.py:98
  45.0 10.5 %collective-permute-start.17 = (bf16[160,1280]{1,0:T(8,128)(2,1)S(1)}, bf16[160,1280]{1,0:T(8,128)(2,1)S(1)}, u32[]{:S(2)}, u32[]{:S(2)}) collective-permute-start(bf16[160,1280]{1,0:T(8,128)(2,1)S(1)} %fusion.26), channel_id=1, source_target_pairs={{1,2},{2,1},{5,6},{6,5},{9,10},{10,9},{13,14},{14,13},{17,18},{18,... | collective-permute-start | bytes 1228808 | tf_op jit(solution)/shard_map/ppermute | solution.py:111
  52.8 2.6 %collective-permute-start.21 = (bf16[160,1280]{1,0:T(8,128)(2,1)S(1)}, bf16[160,1280]{1,0:T(8,128)(2,1)S(1)}, u32[]{:S(2)}, u32[]{:S(2)}) collective-permute-start(bf16[160,1280]{1,0:T(8,128)(2,1)S(1)} %fusion.27), channel_id=1, source_target_pairs={{1,2},{2,1},{5,6},{6,5},{9,10},{10,9},{13,14},{14,13},{17,18},{18,... | collective-permute-start | bytes 1228808 | tf_op jit(solution)/shard_map/ppermute | solution.py:111
  54.6 14.9 %collective-permute-start.3 = (bf16[160,1280]{1,0:T(8,128)(2,1)S(1)}, bf16[160,1280]{1,0:T(8,128)(2,1)S(1)}, u32[]{:S(2)}, u32[]{:S(2)}) collective-permute-start(bf16[160,1280]{1,0:T(8,128)(2,1)S(1)} %constant_dynamic-slice_fusion), channel_id=1, source_target_pairs={{0,4},{4,0},{8,12},{12,8},{1,5},{5,1},{9,13},{13,9},{2,6},{6,2},{1... | collective-permute-start | bytes 1228808 | tf_op jit(solution)/shard_map/ppermute | solution.py:28
  55.4 14.1 %copy-start.1 = (bf16[1280,1280]{1,0:T(8,128)(2,1)S(1)}, bf16[1280,1280]{1,0:T(8,128)(2,1)}, u32[]{:S(2)}) copy-start(bf16[1280,1280]{1,0:T(8,128)(2,1)} %param.7) | copy-start | bytes 9830404
  56.2 23.2 %collective-permute-start.22 = (bf16[160,1280]{1,0:T(8,128)(2,1)S(1)}, bf16[160,1280]{1,0:T(8,128)(2,1)S(1)}, u32[]{:S(2)}, u32[]{:S(2)}) collective-permute-start(bf16[160,1280]{1,0:T(8,128)(2,1)S(1)} %get-tuple-element.13), channel_id=1, source_target_pairs={{0,1},{3,2},{1,0},{2,3},{4,5},{7,6},{5,4},{6,7},{8,9},{11,10},{9,8... | collective-permute-start | bytes 1228808 | tf_op jit(solution)/shard_map/ppermute | solution.py:98
  70.2 17.0 %collective-permute-start.4 = (f32[160,1280]{1,0:T(8,128)S(1)}, f32[160,1280]{1,0:T(8,128)S(1)}, u32[]{:S(2)}, u32[]{:S(2)}) collective-permute-start(f32[160,1280]{1,0:T(8,128)S(1)} %fusion.80), channel_id=1, source_target_pairs={{0,4},{4,0},{8,12},{12,8},{1,5},{5,1},{9,13},{13,9},{2,6},{6,2},{1... | collective-permute-start | bytes 2457608 | tf_op jit(solution)/shard_map/ppermute | solution.py:28
  72.1 27.5 %collective-permute-start.6 = (bf16[160,1280]{1,0:T(8,128)(2,1)S(1)}, bf16[160,1280]{1,0:T(8,128)(2,1)S(1)}, u32[]{:S(2)}, u32[]{:S(2)}) collective-permute-start(bf16[160,1280]{1,0:T(8,128)(2,1)S(1)} %get-tuple-element.35), channel_id=1, source_target_pairs={{0,8},{4,12},{8,0},{12,4},{1,9},{5,13},{9,1},{13,5},{2,10},{6,14},... | collective-permute-start | bytes 1228808 | tf_op jit(solution)/shard_map/ppermute | solution.py:28
  73.6 12.9 %collective-permute-start.18 = (bf16[160,1280]{1,0:T(8,128)(2,1)S(1)}, bf16[160,1280]{1,0:T(8,128)(2,1)S(1)}, u32[]{:S(2)}, u32[]{:S(2)}) collective-permute-start(bf16[160,1280]{1,0:T(8,128)(2,1)S(1)} %get-tuple-element.14), channel_id=1, source_target_pairs={{0,1},{3,2},{1,0},{2,3},{4,5},{7,6},{5,4},{6,7},{8,9},{11,10},{9,8... | collective-permute-start | bytes 1228808 | tf_op jit(solution)/shard_map/ppermute | solution.py:98
  79.5 11.1 %collective-permute-start.23 = (bf16[160,1280]{1,0:T(8,128)(2,1)S(1)}, bf16[160,1280]{1,0:T(8,128)(2,1)S(1)}, u32[]{:S(2)}, u32[]{:S(2)}) collective-permute-start(bf16[160,1280]{1,0:T(8,128)(2,1)S(1)} %fusion.31), channel_id=1, source_target_pairs={{1,2},{2,1},{5,6},{6,5},{9,10},{10,9},{13,14},{14,13},{17,18},{18,... | collective-permute-start | bytes 1228808 | tf_op jit(solution)/shard_map/ppermute | solution.py:111
  86.6 5.4 %collective-permute-start.19 = (bf16[160,1280]{1,0:T(8,128)(2,1)S(1)}, bf16[160,1280]{1,0:T(8,128)(2,1)S(1)}, u32[]{:S(2)}, u32[]{:S(2)}) collective-permute-start(bf16[160,1280]{1,0:T(8,128)(2,1)S(1)} %fusion.30), channel_id=1, source_target_pairs={{1,2},{2,1},{5,6},{6,5},{9,10},{10,9},{13,14},{14,13},{17,18},{18,... | collective-permute-start | bytes 1228808 | tf_op jit(solution)/shard_map/ppermute | solution.py:111
  89.0 10.3 %collective-permute-start.5 = (bf16[160,1280]{1,0:T(8,128)(2,1)S(1)}, bf16[160,1280]{1,0:T(8,128)(2,1)S(1)}, u32[]{:S(2)}, u32[]{:S(2)}) collective-permute-start(bf16[160,1280]{1,0:T(8,128)(2,1)S(1)} %get-tuple-element.33), channel_id=1, source_target_pairs={{0,8},{4,12},{8,0},{12,4},{1,9},{5,13},{9,1},{13,5},{2,10},{6,14},... | collective-permute-start | bytes 1228808 | tf_op jit(solution)/shard_map/ppermute | solution.py:28
  90.7 21.3 %collective-permute-start.24 = (bf16[160,1280]{1,0:T(8,128)(2,1)S(1)}, bf16[160,1280]{1,0:T(8,128)(2,1)S(1)}, u32[]{:S(2)}, u32[]{:S(2)}) collective-permute-start(bf16[160,1280]{1,0:T(8,128)(2,1)S(1)} %fusion.15), channel_id=1, source_target_pairs={{1,0},{2,3},{5,4},{6,7},{9,8},{10,11},{13,12},{14,15},{17,16},{18,... | collective-permute-start | bytes 1228808 | tf_op jit(solution)/shard_map/ppermute | solution.py:98
  92.1 19.5 %collective-permute-start.20 = (bf16[160,1280]{1,0:T(8,128)(2,1)S(1)}, bf16[160,1280]{1,0:T(8,128)(2,1)S(1)}, u32[]{:S(2)}, u32[]{:S(2)}) collective-permute-start(bf16[160,1280]{1,0:T(8,128)(2,1)S(1)} %fusion.9), channel_id=1, source_target_pairs={{1,0},{2,3},{5,4},{6,7},{9,8},{10,11},{13,12},{14,15},{17,16},{18,... | collective-permute-start | bytes 1228808 | tf_op jit(solution)/shard_map/ppermute | solution.py:98
  99.7 13.0 %collective-permute-start.8 = (bf16[160,1280]{1,0:T(8,128)(2,1)S(1)}, bf16[160,1280]{1,0:T(8,128)(2,1)S(1)}, u32[]{:S(2)}, u32[]{:S(2)}) collective-permute-start(bf16[160,1280]{1,0:T(8,128)(2,1)S(1)} %get-tuple-element.10), channel_id=1, source_target_pairs={{0,4},{4,0},{8,12},{12,8},{1,5},{5,1},{9,13},{13,9},{2,6},{6,2},{1... | collective-permute-start | bytes 1228808 | tf_op jit(solution)/shard_map/ppermute | solution.py:28
  99.7 12.9 %collective-permute-start.7 = (bf16[160,1280]{1,0:T(8,128)(2,1)S(1)}, bf16[160,1280]{1,0:T(8,128)(2,1)S(1)}, u32[]{:S(2)}, u32[]{:S(2)}) collective-permute-start(bf16[160,1280]{1,0:T(8,128)(2,1)S(1)} %get-tuple-element.12), channel_id=1, source_target_pairs={{0,4},{4,0},{8,12},{12,8},{1,5},{5,1},{9,13},{13,9},{2,6},{6,2},{1... | collective-permute-start | bytes 1228808 | tf_op jit(solution)/shard_map/ppermute | solution.py:28

commit v2 on v0

v2 whole, which is shorter than its diff:
```python
import functools

import jax
import jax.numpy as jnp
from jax import lax
from jax.experimental import pallas as pl
from jax.experimental.pallas import tpu as pltpu
from jax.sharding import PartitionSpec as P

SEQS = 4
BF16 = jnp.bfloat16
F32 = jnp.float32
NARROW = 256
VMEM_GRANT = 56 << 20


def dot(values, piece):
    return jnp.dot(values, piece, preferred_element_type=F32)


def outer_sum(left, right):
    return lax.dot_general(
        left, right, (((0,), (0,)), ((), ())), preferred_element_type=F32
    )


def project_any(values, basis, axis):
    turned = lax.all_to_all(values, axis, split_axis=1, concat_axis=0, tiled=True)
    total = lax.psum_scatter(dot(turned, basis), axis, scatter_dimension=0, tiled=True)
    return lax.all_gather(total.astype(BF16), axis, axis=0, tiled=True)


def correct_any(act_panel, grad_panel, seq_ids):
    total_rows = seq_ids.shape[0]
    window = total_rows // 2
    total = jnp.zeros((act_panel.shape[1], grad_panel.shape[1]), F32)
    for seq in range(SEQS):
        first = jnp.sum((seq_ids < seq).astype(jnp.int32))
        begin = jnp.minimum(first, total_rows - window)
        left = lax.dynamic_slice_in_dim(act_panel, begin, window, 0)
        right = lax.dynamic_slice_in_dim(grad_panel, begin, window, 0)
        ids_here = lax.dynamic_slice_in_dim(seq_ids, begin, window, 0)
        masked = left * (ids_here == seq).astype(BF16)[:, None]
        seq_sum = outer_sum(masked, right)
        total = total + seq_sum * seq_sum
    return total / SEQS


VMEM = pl.BlockSpec(memory_space=pltpu.VMEM)
SMEM = pl.BlockSpec(memory_space=pltpu.SMEM)
ANY = pl.BlockSpec(memory_space=pl.ANY)


def shaped(*shape, dtype=BF16):
    return jax.ShapeDtypeStruct(shape, dtype)


def columns_of(ref, rows, index, width):
    return ref.at[rows, pl.ds(pl.multiple_of(index * width, width), width)]


def copy_all(pairs, sems):
    copies = [pltpu.make_async_copy(src, dst, sems.at[i]) for i, (src, dst) in enumerate(pairs)]
    for copy in copies:
        copy.start()
    for copy in copies:
        copy.wait()


def cut_first(gradients, depth):
    tokens = gradients.shape[0]
    half = tokens // 2

    def kernel(grad, beside, own, token, sems):
        core, col = lax.axis_index("row") % 2, lax.axis_index("col")
        part = pl.ds(pl.multiple_of(core * half, half), half)
        token[...] = jnp.zeros_like(token)
        copy_all(
            [
                (columns_of(grad, part, col + 1 - 2 * (col % 2), depth), beside),
                (columns_of(grad, pl.ds(0, tokens), col, depth), own),
            ],
            sems,
        )

    return pl.pallas_call(
        kernel,
        out_shape=[shaped(half, depth), shaped(tokens, depth), shaped(8, 128, dtype=F32)],
        in_specs=[ANY],
        out_specs=[VMEM] * 3,
        scratch_shapes=[pltpu.SemaphoreType.DMA((2,))],
        compiler_params=pltpu.CompilerParams(vmem_limit_bytes=VMEM_GRANT),
    )(gradients)


def cut_rest(activations, gradients, depth, before):
    tokens = activations.shape[0]
    half = tokens // 2

    def kernel(act, grad, before, far, mine, across, twice, token, sems):
        token[...] = before[...]
        row, col = lax.axis_index("row"), lax.axis_index("col")
        core, chip = row % 2, row // 2
        whole = pl.ds(0, tokens)
        part = pl.ds(pl.multiple_of(core * half, half), half)
        left, right = pl.ds(0, depth), pl.ds(depth, depth)
        copy_all(
            [
                (columns_of(grad, part, 3 - col, depth), across),
                (columns_of(grad, part, col + 2 - 4 * (col // 2), depth), twice),
                (columns_of(act, whole, 2 - 2 * chip + core, depth), far.at[:, left]),
                (columns_of(act, whole, 3 - 2 * chip - core, depth), far.at[:, right]),
                (columns_of(act, whole, 2 * chip + core, depth), mine.at[:, left]),
                (columns_of(act, whole, 2 * chip + 1 - core, depth), mine.at[:, right]),
            ],
            sems,
        )

    return pl.pallas_call(
        kernel,
        out_shape=[shaped(tokens, 2 * depth)] * 2
        + [shaped(half, depth)] * 2
        + [shaped(8, 128, dtype=F32)],
        in_specs=[ANY] * 2 + [VMEM],
        out_specs=[VMEM] * 5,
        scratch_shapes=[pltpu.SemaphoreType.DMA((6,))],
        compiler_params=pltpu.CompilerParams(vmem_limit_bytes=48 << 20),
    )(activations, gradients, before)


def step(function, shapes, values, token, after=(), grant=16 << 20, flops=0):
    count, shapes = len(values), list(shapes) + [shaped(8, 128, dtype=F32)]

    def kernel(*refs):
        outs = function(*refs[:count])
        for ref, out in zip(refs[count + 1 + len(after) :], outs):
            ref[...] = out
        refs[-1][...] = refs[count][...]

    return pl.pallas_call(
        kernel,
        out_shape=shapes,
        in_specs=[VMEM] * (count + 1) + [ANY] * len(after),
        out_specs=[VMEM] * len(shapes),
        cost_estimate=pl.CostEstimate(flops=flops, bytes_accessed=0, transcendentals=0),
        compiler_params=pltpu.CompilerParams(vmem_limit_bytes=grant),
    )(*values, token, *after)


def is_inner():
    col = lax.axis_index("col")
    return (col == 1) | (col == 2)


def both_halves(here, there):
    first = lax.axis_index("row") % 2 == 0
    return jnp.concatenate([jnp.where(first, here, there), jnp.where(first, there, here)], 0)


def turn(blocks, seq_ids, token):
    tokens, width = blocks[0].shape
    rows = 4 * tokens
    wide = 2 * NARROW

    def kernel(ids_ref, own, other_chip, other_core, both, before, out_ref, place_ref, token_ref, act_ref):
        token_ref[...] = before[...]
        row = lax.axis_index("row")
        chip, core = row // 2, row % 2
        homes = [row, 2 - 2 * chip + core, 2 * chip + 1 - core, 3 - 2 * chip - core]
        for ref, home in zip((own, other_chip, other_core, both), homes):
            act_ref[pl.ds(pl.multiple_of(home * tokens, tokens), tokens), :] = ref[...]
        ids = ids_ref[...]
        for seq in range(SEQS):
            begin = jnp.sum((ids < seq).astype(jnp.int32))
            end = jnp.sum((ids <= seq).astype(jnp.int32))
            floor = begin // 16 * 16
            narrow = jnp.minimum(floor, rows - NARROW)
            is_wide = end - narrow > NARROW
            start = jnp.where(is_wide, jnp.minimum(floor, rows - wide), narrow)
            place_ref[2 * seq] = start
            place_ref[2 * seq + 1] = is_wide.astype(jnp.int32)

            def put(offset):
                here = pl.multiple_of(start + offset, 16)
                index = lax.broadcasted_iota(jnp.int32, (NARROW, width), 0) + here
                window = act_ref[pl.ds(here, NARROW), :]
                window = jnp.where((index >= begin) & (index < end), window, jnp.zeros_like(window))
                out_ref[seq, :, offset : offset + NARROW] = window.T

            put(0)
            pl.when(is_wide)(functools.partial(put, NARROW))

    return pl.pallas_call(
        kernel,
        out_shape=[
            shaped(SEQS, width, wide),
            shaped(2 * SEQS, dtype=jnp.int32),
            shaped(8, 128, dtype=F32),
        ],
        in_specs=[VMEM] * 6,
        out_specs=[VMEM, SMEM, VMEM],
        scratch_shapes=[pltpu.VMEM((rows, width), BF16)],
        compiler_params=pltpu.CompilerParams(vmem_limit_bytes=24 << 20),
    )(seq_ids.reshape(-1, 128), *blocks, token)


def correct(turned, places, blocks, known, crossed, outward):
    tokens, width = known.shape
    height, wide = turned.shape[1:]

    def kernel(place, turned, one, two, three, known, crossed, outward, out, grad, left, total, sems):
        col = lax.axis_index("col")
        inner = (col == 1) | (col == 2)

        def rows(block):
            index = jnp.where(col >= 2, 3 - block, block)
            return pl.ds(pl.multiple_of(index * tokens, tokens), tokens)

        lefts = [
            pltpu.make_async_copy(turned.at[seq], left.at[seq], sems.at[seq]) for seq in range(SEQS)
        ]
        copies = [
            pltpu.make_async_copy(ref, grad.at[rows(i + 1)], sems.at[SEQS + i])
            for i, ref in enumerate((one, two, three))
        ]
        for copy in copies + lefts:
            copy.start()
        came = jnp.where(inner, crossed[...], outward[...])
        grad[rows(0)] = (known[...] + came.astype(F32)).astype(BF16)
        for copy in copies:
            copy.wait()

        def put(columns):
            return pltpu.make_async_copy(total.at[:, columns], out.at[:, columns], sems.at[SEQS + 3])

        for seq in range(SEQS):
            lefts[seq].wait()
            start = pl.multiple_of(place[2 * seq], 16)
            is_wide = place[2 * seq + 1] == 1
            last = seq == SEQS - 1
            step = NARROW if last else width
            for begin in range(0, width, step):
                columns = slice(begin, begin + step)

                def add(depth):
                    part = dot(left[seq, :, :depth], grad[pl.ds(start, depth), columns])
                    part = part * part
                    if seq:
                        part = total[:, columns] + part
                    total[:, columns] = part / SEQS if last else part

                pl.when(is_wide)(functools.partial(add, wide))
                pl.when(jnp.logical_not(is_wide))(functools.partial(add, NARROW))
                if last:
                    put(columns).start()
        put(slice(0, width)).wait()

    return pl.pallas_call(
        kernel,
        out_shape=shaped(height, width, dtype=F32),
        in_specs=[SMEM] + [ANY] * 4 + [VMEM] * 3,
        out_specs=ANY,
        scratch_shapes=[
            pltpu.VMEM((4 * tokens, width), BF16),
            pltpu.VMEM(turned.shape, BF16),
            pltpu.VMEM((height, width), F32),
            pltpu.SemaphoreType.DMA((SEQS + 4,)),
        ],
        compiler_params=pltpu.CompilerParams(vmem_limit_bytes=24 << 20),
    )(places, turned, *blocks, known, crossed, outward)


def by_xor(values, axis, bits):
    return lax.ppermute(values, axis, [(i, i ^ bits) for i in range(4)])


def run(activations, gradients, input_basis, output_basis, seq_ids):
    depth, tokens = input_basis.shape[0], activations.shape[0]
    width = output_basis.shape[1]
    half = tokens // 2
    wide, short = shaped(tokens, width, dtype=F32), shaped(tokens, width)
    block = shaped(tokens, depth)
    parts, known, came, crossed, went = [], [None] * 4, [None] * 4, [None] * 4, [None] * 4

    def add_inward(j, token):
        def function(part, other):
            total = part[...] + other[...].astype(F32)
            return jnp.where(is_inner(), total, part[...]), total.astype(BF16)

        known[j], sent, token = step(function, [wide, short], [parts[j], came[j]], token)
        crossed[j] = lax.ppermute(sent, "col", [(1, 2), (2, 1)])
        return token

    def add_crossed(j, token):
        def function(part, other):
            return [(part[...] + other[...].astype(F32)).astype(BF16)]

        sent, token = step(function, [short], [parts[3 - j], crossed[j]], token)
        went[j] = lax.ppermute(sent, "col", [(1, 0), (2, 3)])
        return token

    def finish(j, token):
        def function(part, inner, outer):
            other = jnp.where(is_inner(), inner[...], outer[...])
            return [(part[...] + other.astype(F32)).astype(BF16)]

        return step(function, [short], [known[j], crossed[3 - j], went[3 - j]], token)

    def inward(sent):
        return lax.ppermute(sent, "col", [(0, 1), (3, 2)])

    def project_own(values, basis):
        total = dot(values[...], basis[...])
        return total, total.astype(BF16)

    def project_beside(here, there, own, basis):
        total = dot(both_halves(here[...], there[...]), basis[...])
        inner = is_inner()
        return jnp.where(inner, total, own[...]), jnp.where(inner, own[...], total), total.astype(BF16)

    def project_others(here, there, basis):
        across = both_halves(here[:half], there[:half])
        twice = both_halves(here[half:], there[half:])
        inner = is_inner()
        one = dot(jnp.where(inner, across, twice), basis[...])
        two = dot(jnp.where(inner, twice, across), basis[...])
        return one, two, one.astype(BF16), two.astype(BF16)

    def project_act(values, basis, other):
        total = dot(values[:, :depth], basis[...]) + dot(values[:, depth:], other[...])
        return total, total.astype(BF16)

    def add_there(total, other):
        return [(total[...] + other[...].astype(F32)).astype(BF16)]

    other_basis = by_xor(input_basis, "row", 1)
    beside, own, token = cut_first(gradients, depth)
    beside = by_xor(beside, "col", 1)
    own_part, sent, token = step(project_own, [wide, short], [own, output_basis], token)
    came[0] = inward(sent)
    far, mine, across, twice, token = cut_rest(activations, gradients, depth, token)
    across = by_xor(across, "col", 3)
    twice = by_xor(twice, "col", 2)
    far = by_xor(far, "row", 2)
    beside, token = step(
        lambda one: [one[...]], [shaped(half, depth)], [beside], token, after=[other_basis]
    )
    one, two, sent, token = step(
        project_beside,
        [wide, wide, short],
        [beside, by_xor(beside, "row", 1), own_part, output_basis],
        token,
    )
    parts += [one, two]
    came[1] = inward(sent)
    token = add_inward(0, token)
    pieces, token = step(
        lambda one, two: [jnp.concatenate([one[...], two[...]], 0)], [block], [across, twice], token
    )
    near_sum, sent, token = step(
        project_act, [wide, short], [mine, input_basis, other_basis], token, flops=10**11
    )
    near_there = by_xor(sent, "row", 2)
    one, two, one_sent, two_sent, token = step(
        project_others, [wide, wide, short, short], [pieces, by_xor(pieces, "row", 1), output_basis], token
    )
    parts += [one, two]
    came[2], came[3] = inward(one_sent), inward(two_sent)
    token = add_inward(1, token)
    token = add_crossed(0, token)
    far_sum, sent, token = step(project_act, [wide, short], [far, input_basis, other_basis], token)
    far_there = by_xor(sent, "row", 2)
    token = add_inward(2, token)
    token = add_crossed(1, token)
    far, token = step(add_there, [short], [far_sum, near_there], token)
    far_other = by_xor(far, "row", 1)
    token = add_inward(3, token)
    token = add_crossed(2, token)
    near, token = step(add_there, [short], [near_sum, far_there], token)
    near_other = by_xor(near, "row", 1)
    late = [None] * 4
    late[3], token = finish(3, token)
    late[2], token = finish(2, token)
    turned, places, token = turn([near, far, near_other, far_other], seq_ids, token)
    token = add_crossed(3, token)
    late[1], token = finish(1, token)
    return correct(turned, places, late[1:], known[0], crossed[3], went[3])


def on_device(rows, cols, activations, gradients, input_basis, output_basis, seq_ids):
    total = seq_ids.shape[0]
    if rows != 4 or cols != 4 or not total // 2 + 16 <= 2 * NARROW <= total:
        act_panel = project_any(activations, input_basis, "row")
        grad_panel = project_any(gradients, output_basis, "col")
        return correct_any(act_panel, grad_panel, seq_ids)
    return run(activations, gradients, input_basis, output_basis, seq_ids)


def solution(mesh):
    return jax.shard_map(
        functools.partial(on_device, mesh.shape["row"], mesh.shape["col"]),
        mesh=mesh,
        in_specs=(
            P(("grp", "row"), None),
            P(("grp", "col"), None),
            P(("grp", "row"), "col"),
            P(("grp", "col"), "row"),
            P("grp"),
        ),
        out_specs=P(("grp", "col"), "row"),
        check_vma=False,
    )
```

time: 404 us -> 104 us (0.26)
  waiting for transfers between devices: 359 us -> 38.8 us
  starting transfers between devices: 0.3 us -> 40.1 us
  matrix products: 28 us -> 0 us
  Pallas kernels: 0 us -> 20.8 us
  between operations: 15.7 us -> 0.57 us
    all_gather x4 -> x0, waiting for transfers between devices: 357 us -> none  [the longest x1 220 us: on_device(): lax.all_gather(output_basis, 'col', axis=0, tiled=True)]
    ppermute x0 -> x23, starting transfers between devices: none -> 40.1 us  [the longest x4 20 us: inward(): return lax.ppermute(sent, 'col', [(0, 1), (3, 2)])]
    ppermute x0 -> x23, waiting for transfers between devices: none -> 38.8 us  [the longest x4 24.1 us: add_crossed(): went[j] = lax.ppermute(sent, 'col', [(1, 0), (2, 3)])]
    dot_general x6 -> x0, matrix products: 28 us -> none  [the longest x2 15.6 us: add_piece(): return jnp.dot(values, piece, preferred_element_type=jnp.float32)]
    pallas_call x0 -> x24, Pallas kernels: none -> 20.8 us  [the longest x1 8.93 us: correct(): pl.pallas_call(kernel, out_shape=shaped(height, width, dtype=F32), in_spe...]
  transfers between devices with their start and end apart: 4 -> 23, of which waited for: 4 -> 8; matrix products, arithmetic and copies ran while one was open for 4% -> 0% of each run, Pallas kernels for 0% -> 11%
where the time goes in v2:
time: 104 us
  starting transfers between devices  40.1 us (39%)
  waiting for transfers between devices  38.8 us (37%)
  Pallas kernels  20.8 us (20%)
  local copies, waits for them, and re-layouts  3.63 us (3%)
    ppermute x4, waiting for transfers between devices, add_crossed(): went[j] = lax.ppermute(sent, 'col', [(1, 0), (2, 3)])  24.1 us
    ppermute x4, starting transfers between devices, inward(): return lax.ppermute(sent, 'col', [(0, 1), (3, 2)])  20 us
    ppermute x11, starting transfers between devices, by_xor(): return lax.ppermute(values, axis, [(i, i ^ bits) for i in range(4)])  12.2 us
    ppermute x11, waiting for transfers between devices, by_xor(): return lax.ppermute(values, axis, [(i, i ^ bits) for i in range(4)])  11.5 us
    pallas_call x1, Pallas kernels, correct(): pl.pallas_call(kernel, out_shape=shaped(height, width, dtype=F32), in_spe...  8.93 us
    pallas_call x20, Pallas kernels, step(): pl.pallas_call(kernel, out_shape=shapes, in_specs=[VMEM] * (count + 1) +...  7.31 us
    ppermute x4, starting transfers between devices, add_crossed(): went[j] = lax.ppermute(sent, 'col', [(1, 0), (2, 3)])  5.13 us
    unnamed x16, local copies, waits for them, and re-layouts  3.63 us
  transfers between devices with their start and end apart: 23, of which 8 were waited for; matrix products, arithmetic and copies ran while one was open for 0% of the time, Pallas kernels for 11%

profile of v2, /device:TPU:0, one launch (start us, length us, event | category | flops | bytes accessed | tf_op | source)
XLA Modules:
  0.0 103.9 jit_solution(11008918944263642728)
XLA Ops:
  0.5 2.0 %shard_map.55 = (bf16[80,1280]{1,0:T(8,128)(2,1)}, bf16[160,1280]{1,0:T(8,128)(2,1)}, f32[8,128]{1,0:T(8,128)}) custom-call(bf16[160,5120]{1,0:T(8,128)(2,1)} %grad.3), custom_call_target="tpu_custom_call" | custom-call | tf_op jit(solution)/shard_map/pallas_call | solution.py:86
  2.4 2.8 %collective-permute-start.3 = (bf16[80,1280]{1,0:T(8,128)(2,1)}, bf16[80,1280]{1,0:T(8,128)(2,1)S(1)}, u32[]{:S(2)}, u32[]{:S(2)}) collective-permute-start(bf16[80,1280]{1,0:T(8,128)(2,1)} %get-tuple-element.73), channel_id=1, source_target_pairs={{0,1},{1,0},{2,3},{3,2},{4,5},{5,4},{6,7},{7,6},{8,9},{9,8},{10,11... | collective-permute-start | bytes 614408 | tf_op jit(solution)/shard_map/ppermute | solution.py:274
  5.2 1.9 %copy-done = bf16[1280,1280]{1,0:T(8,128)(2,1)S(1)} copy-done((bf16[1280,1280]{1,0:T(8,128)(2,1)S(1)}, bf16[1280,1280]{1,0:T(8,128)(2,1)}, u32[]{:S(2)}) %copy-start) | copy-done | bytes 3276824
  7.1 1.0 copy-done.5
  8.8 0.7 shard_map.56
  9.5 1.9 %collective-permute-start.5 = (bf16[160,1280]{1,0:T(8,128)(2,1)S(1)}, bf16[160,1280]{1,0:T(8,128)(2,1)S(1)}, u32[]{:S(2)}, u32[]{:S(2)}) collective-permute-start(bf16[160,1280]{1,0:T(8,128)(2,1)S(1)} %get-tuple-element.79), channel_id=1, source_target_pairs={{0,1},{3,2},{4,5},{7,6},{8,9},{11,10},{12,13},{15,14},{16,17},{19,... | collective-permute-start | bytes 1228808 | tf_op jit(solution)/shard_map/ppermute | solution.py:310
  12.0 4.0 %collective-permute-start.1 = (bf16[80,1280]{1,0:T(8,128)(2,1)S(1)}, bf16[80,1280]{1,0:T(8,128)(2,1)S(1)}, u32[]{:S(2)}, u32[]{:S(2)}) collective-permute-start(bf16[80,1280]{1,0:T(8,128)(2,1)S(1)} %get-tuple-element.71), channel_id=1, source_target_pairs={{0,3},{1,2},{2,1},{3,0},{4,7},{5,6},{6,5},{7,4},{8,11},{9,10},{10,... | collective-permute-start | bytes 614408 | tf_op jit(solution)/shard_map/ppermute | solution.py:274
  16.1 1.5 %collective-permute-start.6 = (bf16[160,2560]{1,0:T(8,128)(2,1)S(1)}, bf16[160,2560]{1,0:T(8,128)(2,1)S(1)}, u32[]{:S(2)}, u32[]{:S(2)}) collective-permute-start(bf16[160,2560]{1,0:T(8,128)(2,1)S(1)} %get-tuple-element.84), channel_id=1, source_target_pairs={{0,8},{4,12},{8,0},{12,4},{1,9},{5,13},{9,1},{13,5},{2,10},{6,14},... | collective-permute-start | bytes 2457608 | tf_op jit(solution)/shard_map/ppermute | solution.py:274
  17.5 0.8 shard_map.59
  18.3 2.7 %collective-permute-start.9 = (bf16[160,1280]{1,0:T(8,128)(2,1)S(1)}, bf16[160,1280]{1,0:T(8,128)(2,1)S(1)}, u32[]{:S(2)}, u32[]{:S(2)}) collective-permute-start(bf16[160,1280]{1,0:T(8,128)(2,1)S(1)} %get-tuple-element.90), channel_id=1, source_target_pairs={{0,1},{3,2},{4,5},{7,6},{8,9},{11,10},{12,13},{15,14},{16,17},{19,... | collective-permute-start | bytes 1228808 | tf_op jit(solution)/shard_map/ppermute | solution.py:310
  21.4 8.8 %collective-permute-done.1.refs_0_ = bf16[80,1280]{1,0:T(8,128)(2,1)S(1)} collective-permute-done((bf16[80,1280]{1,0:T(8,128)(2,1)S(1)}, bf16[80,1280]{1,0:T(8,128)(2,1)S(1)}, u32[]{:S(2)}, u32[]{:S(2)}) %collective-permute-start.1) | collective-permute-done | bytes 204832 | tf_op jit(solution)/shard_map/ppermute | solution.py:274
  30.3 0.7 collective-permute-start.8
  31.0 1.2 %shard_map.62 = (f32[160,1280]{1,0:T(8,128)S(1)}, bf16[160,1280]{1,0:T(8,128)(2,1)S(1)}, f32[8,128]{1,0:T(8,128)S(1)}) custom-call(bf16[160,2560]{1,0:T(8,128)(2,1)S(1)} %get-tuple-element.70.refs_0_, bf16[1280,1280]{1,0:T(8,128)(2,1)S(1)} %copy-done.3, bf16[1280,1280]{1,0:T(8,128)(2,1)S(1)} %collective-permute-done.refs_2_, ...), custom_call_target="tpu_custom_call" | custom-call | flops 99999997952 | tf_op jit(solution)/shard_map/pallas_call | solution.py:140
  32.2 1.3 %shard_map.63 = (f32[160,1280]{1,0:T(8,128)S(1)}, f32[160,1280]{1,0:T(8,128)S(1)}, bf16[160,1280]{1,0:T(8,128)(2,1)S(1)}, bf16[160,1280]{1,0:T(8,128)(2,1)S(1)}, f32[8,128]{1,0:T(8,128)S(1)}) custom-call(bf16[160,1280]{1,0:T(8,128)(2,1)S(1)} %get-tuple-element.85.refs_0_, bf16[160,1280]{1,0:T(8,128)(2,1)S(1)} %collective-permute-done.7.refs_1_, ...), custom_call_target="tpu_custom_call" | custom-call | tf_op jit(solution)/shard_map/pallas_call | solution.py:140
  33.5 8.1 %collective-permute-start.11 = (bf16[160,1280]{1,0:T(8,128)(2,1)S(1)}, bf16[160,1280]{1,0:T(8,128)(2,1)S(1)}, u32[]{:S(2)}, u32[]{:S(2)}) collective-permute-start(bf16[160,1280]{1,0:T(8,128)(2,1)S(1)} %get-tuple-element.96), channel_id=1, source_target_pairs={{0,1},{3,2},{4,5},{7,6},{8,9},{11,10},{12,13},{15,14},{16,17},{19,... | collective-permute-start | bytes 1228808 | tf_op jit(solution)/shard_map/ppermute | solution.py:310
  41.8 0.7 collective-permute-start.15
  42.5 1.6 %collective-permute-start.14 = (bf16[160,1280]{1,0:T(8,128)(2,1)S(1)}, bf16[160,1280]{1,0:T(8,128)(2,1)S(1)}, u32[]{:S(2)}, u32[]{:S(2)}) collective-permute-start(bf16[160,1280]{1,0:T(8,128)(2,1)S(1)} %get-tuple-element.101), channel_id=1, source_target_pairs={{0,8},{4,12},{8,0},{12,4},{1,9},{5,13},{9,1},{13,5},{2,10},{6,14},... | collective-permute-start | bytes 1228808 | tf_op jit(solution)/shard_map/ppermute | solution.py:274
  44.1 7.2 %collective-permute-start.13 = (bf16[160,1280]{1,0:T(8,128)(2,1)S(1)}, bf16[160,1280]{1,0:T(8,128)(2,1)S(1)}, u32[]{:S(2)}, u32[]{:S(2)}) collective-permute-start(bf16[160,1280]{1,0:T(8,128)(2,1)S(1)} %get-tuple-element.99), channel_id=1, source_target_pairs={{0,1},{3,2},{4,5},{7,6},{8,9},{11,10},{12,13},{15,14},{16,17},{19,... | collective-permute-start | bytes 1228808 | tf_op jit(solution)/shard_map/ppermute | solution.py:310
  51.4 1.2 %shard_map.66 = (f32[160,1280]{1,0:T(8,128)S(1)}, bf16[160,1280]{1,0:T(8,128)(2,1)S(1)}, f32[8,128]{1,0:T(8,128)S(1)}) custom-call(bf16[160,2560]{1,0:T(8,128)(2,1)S(1)} %collective-permute-done.6.refs_0_, bf16[1280,1280]{1,0:T(8,128)(2,1)S(1)} %copy-done.3, bf16[1280,1280]{1,0:T(8,128)(2,1)S(1)} %collective-permute-done.refs_2_, ...), custom_call_target="tpu_custom_call" | custom-call | tf_op jit(solution)/shard_map/pallas_call | solution.py:140
  53.5 1.6 %collective-permute-start.10 = (bf16[160,1280]{1,0:T(8,128)(2,1)S(1)}, bf16[160,1280]{1,0:T(8,128)(2,1)S(1)}, u32[]{:S(2)}, u32[]{:S(2)}) collective-permute-start(bf16[160,1280]{1,0:T(8,128)(2,1)S(1)} %get-tuple-element.94), channel_id=1, source_target_pairs={{0,8},{4,12},{8,0},{12,4},{1,9},{5,13},{9,1},{13,5},{2,10},{6,14},... | collective-permute-start | bytes 1228808 | tf_op jit(solution)/shard_map/ppermute | solution.py:274
  55.1 1.3 %collective-permute-start.19 = (bf16[160,1280]{1,0:T(8,128)(2,1)S(1)}, bf16[160,1280]{1,0:T(8,128)(2,1)S(1)}, u32[]{:S(2)}, u32[]{:S(2)}) collective-permute-start(bf16[160,1280]{1,0:T(8,128)(2,1)S(1)} %get-tuple-element.113), channel_id=1, source_target_pairs={{1,0},{2,3},{5,4},{6,7},{9,8},{10,11},{13,12},{14,15},{17,16},{18,... | collective-permute-start | bytes 1228808 | tf_op jit(solution)/shard_map/ppermute | solution.py:299
  56.6 3.1 %collective-permute-done.13.refs_1_ = bf16[160,1280]{1,0:T(8,128)(2,1)S(1)} collective-permute-done((bf16[160,1280]{1,0:T(8,128)(2,1)S(1)}, bf16[160,1280]{1,0:T(8,128)(2,1)S(1)}, u32[]{:S(2)}, u32[]{:S(2)}) %collective-permute-start.13) | collective-permute-done | bytes 409632 | tf_op jit(solution)/shard_map/ppermute | solution.py:310
  59.7 1.3 %collective-permute-start.18 = (bf16[160,1280]{1,0:T(8,128)(2,1)S(1)}, bf16[160,1280]{1,0:T(8,128)(2,1)S(1)}, u32[]{:S(2)}, u32[]{:S(2)}) collective-permute-start(bf16[160,1280]{1,0:T(8,128)(2,1)S(1)} %get-tuple-element.111), channel_id=1, source_target_pairs={{1,0},{2,3},{5,4},{6,7},{9,8},{10,11},{13,12},{14,15},{17,16},{18,... | collective-permute-start | bytes 1228808 | tf_op jit(solution)/shard_map/ppermute | solution.py:299
  61.3 2.7 %collective-permute-done.10.refs_1_ = bf16[160,1280]{1,0:T(8,128)(2,1)S(1)} collective-permute-done((bf16[160,1280]{1,0:T(8,128)(2,1)S(1)}, bf16[160,1280]{1,0:T(8,128)(2,1)S(1)}, u32[]{:S(2)}, u32[]{:S(2)}) %collective-permute-start.10) | collective-permute-done | bytes 409632 | tf_op jit(solution)/shard_map/ppermute | solution.py:274
  64.8 6.3 %collective-permute-done.19.refs_2_ = bf16[160,1280]{1,0:T(8,128)(2,1)S(1)} collective-permute-done((bf16[160,1280]{1,0:T(8,128)(2,1)S(1)}, bf16[160,1280]{1,0:T(8,128)(2,1)S(1)}, u32[]{:S(2)}, u32[]{:S(2)}) %collective-permute-start.19) | collective-permute-done | bytes 409632 | tf_op jit(solution)/shard_map/ppermute | solution.py:299
  71.2 1.3 %collective-permute-start.20 = (bf16[160,1280]{1,0:T(8,128)(2,1)S(1)}, bf16[160,1280]{1,0:T(8,128)(2,1)S(1)}, u32[]{:S(2)}, u32[]{:S(2)}) collective-permute-start(bf16[160,1280]{1,0:T(8,128)(2,1)S(1)} %get-tuple-element.120), channel_id=1, source_target_pairs={{1,0},{2,3},{5,4},{6,7},{9,8},{10,11},{13,12},{14,15},{17,16},{18,... | collective-permute-start | bytes 1228808 | tf_op jit(solution)/shard_map/ppermute | solution.py:299
  72.6 7.3 %collective-permute-done.18.refs_2_ = bf16[160,1280]{1,0:T(8,128)(2,1)S(1)} collective-permute-done((bf16[160,1280]{1,0:T(8,128)(2,1)S(1)}, bf16[160,1280]{1,0:T(8,128)(2,1)S(1)}, u32[]{:S(2)}, u32[]{:S(2)}) %collective-permute-start.18) | collective-permute-done | bytes 409632 | tf_op jit(solution)/shard_map/ppermute | solution.py:299
  80.1 2.3 %shard_map.75 = (bf16[4,1280,512]{2,1,0:T(8,128)(2,1)S(1)}, s32[8]{0:T(128)S(1)}, f32[8,128]{1,0:T(8,128)S(1)}) custom-call(s32[5,128]{1,0:T(8,128)S(1)} %bitcast.1, bf16[160,1280]{1,0:T(8,128)(2,1)S(1)} %get-tuple-element.108.own, bf16[160,1280]{1,0:T(8,128)(2,1)S(1)} %get-tuple-element.109.other_chip, ...), custom_call_target="tpu_custom_call" | custom-call | tf_op jit(solution)/shard_map/pallas_call | solution.py:193
  82.5 1.3 %collective-permute-start.22 = (bf16[160,1280]{1,0:T(8,128)(2,1)S(1)}, bf16[160,1280]{1,0:T(8,128)(2,1)S(1)}, u32[]{:S(2)}, u32[]{:S(2)}) collective-permute-start(bf16[160,1280]{1,0:T(8,128)(2,1)S(1)} %get-tuple-element.128), channel_id=1, source_target_pairs={{1,0},{2,3},{5,4},{6,7},{9,8},{10,11},{13,12},{14,15},{17,16},{18,... | collective-permute-start | bytes 1228808 | tf_op jit(solution)/shard_map/ppermute | solution.py:299
  83.8 4.7 %collective-permute-done.20.refs_2_ = bf16[160,1280]{1,0:T(8,128)(2,1)S(1)} collective-permute-done((bf16[160,1280]{1,0:T(8,128)(2,1)S(1)}, bf16[160,1280]{1,0:T(8,128)(2,1)S(1)}, u32[]{:S(2)}, u32[]{:S(2)}) %collective-permute-start.20) | collective-permute-done | bytes 409632 | tf_op jit(solution)/shard_map/ppermute | solution.py:299
  89.1 5.7 %collective-permute-done.22.outward = bf16[160,1280]{1,0:T(8,128)(2,1)S(1)} collective-permute-done((bf16[160,1280]{1,0:T(8,128)(2,1)S(1)}, bf16[160,1280]{1,0:T(8,128)(2,1)S(1)}, u32[]{:S(2)}, u32[]{:S(2)}) %collective-permute-start.22) | collective-permute-done | bytes 409632 | tf_op jit(solution)/shard_map/ppermute | solution.py:299
  94.9 8.9 %shard_map.78 = f32[1280,1280]{1,0:T(8,128)} custom-call(s32[8]{0:T(128)S(1)} %get-tuple-element.117.place, bf16[4,1280,512]{2,1,0:T(8,128)(2,1)S(1)} %get-tuple-element.118.turned, bf16[160,1280]{1,0:T(8,128)(2,1)S(1)} %get-tuple-element.124.one, bf16[160,1280]{1,0:T(8,128)(2,1)S(1)} %get-tuple-element.125.two, ...), custom_call_target="tpu_custom_call" | custom-call | tf_op jit(solution)/shard_map/pallas_call | solution.py:258
  (54 shorter events, 5.5 us)
Async XLA Ops:
  0.0 11.5 %copy-start.2 = (bf16[160,5120]{1,0:T(8,128)(2,1)S(1)}, bf16[160,5120]{1,0:T(8,128)(2,1)}, u32[]{:S(2)}) copy-start(bf16[160,5120]{1,0:T(8,128)(2,1)} %grad.3) | copy-start | bytes 4915204
  0.0 11.8 %collective-permute-start = (bf16[1280,1280]{1,0:T(8,128)(2,1)}, bf16[1280,1280]{1,0:T(8,128)(2,1)S(1)}, u32[]{:S(2)}, u32[]{:S(2)}) collective-permute-start(bf16[1280,1280]{1,0:T(8,128)(2,1)} %refs_1_.5), channel_id=1, source_target_pairs={{0,4},{4,0},{8,12},{12,8},{1,5},{5,1},{9,13},{13,9},{2,6},{6,2},{1... | collective-permute-start | bytes 9830408 | tf_op jit(solution)/shard_map/ppermute | solution.py:274
  2.4 9.4 %collective-permute-start.3 = (bf16[80,1280]{1,0:T(8,128)(2,1)}, bf16[80,1280]{1,0:T(8,128)(2,1)S(1)}, u32[]{:S(2)}, u32[]{:S(2)}) collective-permute-start(bf16[80,1280]{1,0:T(8,128)(2,1)} %get-tuple-element.73), channel_id=1, source_target_pairs={{0,1},{1,0},{2,3},{3,2},{4,5},{5,4},{6,7},{7,6},{8,9},{9,8},{10,11... | collective-permute-start | bytes 614408 | tf_op jit(solution)/shard_map/ppermute | solution.py:274
  5.2 1.9 %copy-start = (bf16[1280,1280]{1,0:T(8,128)(2,1)S(1)}, bf16[1280,1280]{1,0:T(8,128)(2,1)}, u32[]{:S(2)}) copy-start(bf16[1280,1280]{1,0:T(8,128)(2,1)} %refs_2_.1) | copy-start | bytes 9830404
  7.1 1.0 copy-start.5
  8.1 0.7 copy-start.7
  8.8 2.7 %copy-start.4 = (bf16[160,5120]{1,0:T(8,128)(2,1)S(1)}, bf16[160,5120]{1,0:T(8,128)(2,1)}, u32[]{:S(2)}) copy-start(bf16[160,5120]{1,0:T(8,128)(2,1)} %act.1) | copy-start | bytes 4915204
  9.5 11.7 %collective-permute-start.5 = (bf16[160,1280]{1,0:T(8,128)(2,1)S(1)}, bf16[160,1280]{1,0:T(8,128)(2,1)S(1)}, u32[]{:S(2)}, u32[]{:S(2)}) collective-permute-start(bf16[160,1280]{1,0:T(8,128)(2,1)S(1)} %get-tuple-element.79), channel_id=1, source_target_pairs={{0,1},{3,2},{4,5},{7,6},{8,9},{11,10},{12,13},{15,14},{16,17},{19,... | collective-permute-start | bytes 1228808 | tf_op jit(solution)/shard_map/ppermute | solution.py:310
  11.5 6.1 %copy-start.1 = (bf16[1280,1280]{1,0:T(8,128)(2,1)S(1)}, bf16[1280,1280]{1,0:T(8,128)(2,1)}, u32[]{:S(2)}) copy-start(bf16[1280,1280]{1,0:T(8,128)(2,1)} %refs_2_.1) | copy-start | bytes 9830404
  11.9 19.1 %copy-start.3 = (bf16[1280,1280]{1,0:T(8,128)(2,1)S(1)}, bf16[1280,1280]{1,0:T(8,128)(2,1)}, u32[]{:S(2)}) copy-start(bf16[1280,1280]{1,0:T(8,128)(2,1)} %refs_1_.5) | copy-start | bytes 9830404
  11.9 5.7 %collective-permute-start.4 = (bf16[80,1280]{1,0:T(8,128)(2,1)S(1)}, bf16[80,1280]{1,0:T(8,128)(2,1)S(1)}, u32[]{:S(2)}, u32[]{:S(2)}) collective-permute-start(bf16[80,1280]{1,0:T(8,128)(2,1)S(1)} %get-tuple-element.75.refs_0_), channel_id=1, source_target_pairs={{0,4},{4,0},{8,12},{12,8},{1,5},{5,1},{9,13},{13,9},{2,6},{6,2},{1... | collective-permute-start | bytes 614408 | tf_op jit(solution)/shard_map/ppermute | solution.py:274
  12.0 18.1 %collective-permute-start.1 = (bf16[80,1280]{1,0:T(8,128)(2,1)S(1)}, bf16[80,1280]{1,0:T(8,128)(2,1)S(1)}, u32[]{:S(2)}, u32[]{:S(2)}) collective-permute-start(bf16[80,1280]{1,0:T(8,128)(2,1)S(1)} %get-tuple-element.71), channel_id=1, source_target_pairs={{0,3},{1,2},{2,1},{3,0},{4,7},{5,6},{6,5},{7,4},{8,11},{9,10},{10,... | collective-permute-start | bytes 614408 | tf_op jit(solution)/shard_map/ppermute | solution.py:274
  16.0 14.1 %collective-permute-start.2 = (bf16[80,1280]{1,0:T(8,128)(2,1)S(1)}, bf16[80,1280]{1,0:T(8,128)(2,1)S(1)}, u32[]{:S(2)}, u32[]{:S(2)}) collective-permute-start(bf16[80,1280]{1,0:T(8,128)(2,1)S(1)} %get-tuple-element.72), channel_id=1, source_target_pairs={{0,2},{1,3},{2,0},{3,1},{4,6},{5,7},{6,4},{7,5},{8,10},{9,11},{10,... | collective-permute-start | bytes 614408 | tf_op jit(solution)/shard_map/ppermute | solution.py:274
  16.1 35.4 %collective-permute-start.6 = (bf16[160,2560]{1,0:T(8,128)(2,1)S(1)}, bf16[160,2560]{1,0:T(8,128)(2,1)S(1)}, u32[]{:S(2)}, u32[]{:S(2)}) collective-permute-start(bf16[160,2560]{1,0:T(8,128)(2,1)S(1)} %get-tuple-element.84), channel_id=1, source_target_pairs={{0,8},{4,12},{8,0},{12,4},{1,9},{5,13},{9,1},{13,5},{2,10},{6,14},... | collective-permute-start | bytes 2457608 | tf_op jit(solution)/shard_map/ppermute | solution.py:274
  18.3 23.3 %collective-permute-start.9 = (bf16[160,1280]{1,0:T(8,128)(2,1)S(1)}, bf16[160,1280]{1,0:T(8,128)(2,1)S(1)}, u32[]{:S(2)}, u32[]{:S(2)}) collective-permute-start(bf16[160,1280]{1,0:T(8,128)(2,1)S(1)} %get-tuple-element.90), channel_id=1, source_target_pairs={{0,1},{3,2},{4,5},{7,6},{8,9},{11,10},{12,13},{15,14},{16,17},{19,... | collective-permute-start | bytes 1228808 | tf_op jit(solution)/shard_map/ppermute | solution.py:310
  30.2 2.0 %collective-permute-start.7 = (bf16[160,1280]{1,0:T(8,128)(2,1)S(1)}, bf16[160,1280]{1,0:T(8,128)(2,1)S(1)}, u32[]{:S(2)}, u32[]{:S(2)}) collective-permute-start(bf16[160,1280]{1,0:T(8,128)(2,1)S(1)} %get-tuple-element.85.refs_0_), channel_id=1, source_target_pairs={{0,4},{4,0},{8,12},{12,8},{1,5},{5,1},{9,13},{13,9},{2,6},{6,2},{1... | collective-permute-start | bytes 1228808 | tf_op jit(solution)/shard_map/ppermute | solution.py:274
  30.3 13.8 %collective-permute-start.8 = (bf16[160,1280]{1,0:T(8,128)(2,1)S(1)}, bf16[160,1280]{1,0:T(8,128)(2,1)S(1)}, u32[]{:S(2)}, u32[]{:S(2)}) collective-permute-start(bf16[160,1280]{1,0:T(8,128)(2,1)S(1)} %get-tuple-element.88), channel_id=1, source_target_pairs={{1,2},{2,1},{5,6},{6,5},{9,10},{10,9},{13,14},{14,13},{17,18},{18,... | collective-permute-start | bytes 1228808 | tf_op jit(solution)/shard_map/ppermute | solution.py:291
  33.5 19.1 %collective-permute-start.11 = (bf16[160,1280]{1,0:T(8,128)(2,1)S(1)}, bf16[160,1280]{1,0:T(8,128)(2,1)S(1)}, u32[]{:S(2)}, u32[]{:S(2)}) collective-permute-start(bf16[160,1280]{1,0:T(8,128)(2,1)S(1)} %get-tuple-element.96), channel_id=1, source_target_pairs={{0,1},{3,2},{4,5},{7,6},{8,9},{11,10},{12,13},{15,14},{16,17},{19,... | collective-permute-start | bytes 1228808 | tf_op jit(solution)/shard_map/ppermute | solution.py:310
  41.8 13.3 %collective-permute-start.15 = (bf16[160,1280]{1,0:T(8,128)(2,1)S(1)}, bf16[160,1280]{1,0:T(8,128)(2,1)S(1)}, u32[]{:S(2)}, u32[]{:S(2)}) collective-permute-start(bf16[160,1280]{1,0:T(8,128)(2,1)S(1)} %get-tuple-element.102), channel_id=1, source_target_pairs={{1,2},{2,1},{5,6},{6,5},{9,10},{10,9},{13,14},{14,13},{17,18},{18,... | collective-permute-start | bytes 1228808 | tf_op jit(solution)/shard_map/ppermute | solution.py:291
  42.5 14.0 %collective-permute-start.14 = (bf16[160,1280]{1,0:T(8,128)(2,1)S(1)}, bf16[160,1280]{1,0:T(8,128)(2,1)S(1)}, u32[]{:S(2)}, u32[]{:S(2)}) collective-permute-start(bf16[160,1280]{1,0:T(8,128)(2,1)S(1)} %get-tuple-element.101), channel_id=1, source_target_pairs={{0,8},{4,12},{8,0},{12,4},{1,9},{5,13},{9,1},{13,5},{2,10},{6,14},... | collective-permute-start | bytes 1228808 | tf_op jit(solution)/shard_map/ppermute | solution.py:274
  44.1 15.7 %collective-permute-start.13 = (bf16[160,1280]{1,0:T(8,128)(2,1)S(1)}, bf16[160,1280]{1,0:T(8,128)(2,1)S(1)}, u32[]{:S(2)}, u32[]{:S(2)}) collective-permute-start(bf16[160,1280]{1,0:T(8,128)(2,1)S(1)} %get-tuple-element.99), channel_id=1, source_target_pairs={{0,1},{3,2},{4,5},{7,6},{8,9},{11,10},{12,13},{15,14},{16,17},{19,... | collective-permute-start | bytes 1228808 | tf_op jit(solution)/shard_map/ppermute | solution.py:310
  52.8 8.4 %collective-permute-start.12 = (bf16[160,1280]{1,0:T(8,128)(2,1)S(1)}, bf16[160,1280]{1,0:T(8,128)(2,1)S(1)}, u32[]{:S(2)}, u32[]{:S(2)}) collective-permute-start(bf16[160,1280]{1,0:T(8,128)(2,1)S(1)} %get-tuple-element.98), channel_id=1, source_target_pairs={{1,2},{2,1},{5,6},{6,5},{9,10},{10,9},{13,14},{14,13},{17,18},{18,... | collective-permute-start | bytes 1228808 | tf_op jit(solution)/shard_map/ppermute | solution.py:291
  53.5 10.5 %collective-permute-start.10 = (bf16[160,1280]{1,0:T(8,128)(2,1)S(1)}, bf16[160,1280]{1,0:T(8,128)(2,1)S(1)}, u32[]{:S(2)}, u32[]{:S(2)}) collective-permute-start(bf16[160,1280]{1,0:T(8,128)(2,1)S(1)} %get-tuple-element.94), channel_id=1, source_target_pairs={{0,8},{4,12},{8,0},{12,4},{1,9},{5,13},{9,1},{13,5},{2,10},{6,14},... | collective-permute-start | bytes 1228808 | tf_op jit(solution)/shard_map/ppermute | solution.py:274
  55.1 16.1 %collective-permute-start.19 = (bf16[160,1280]{1,0:T(8,128)(2,1)S(1)}, bf16[160,1280]{1,0:T(8,128)(2,1)S(1)}, u32[]{:S(2)}, u32[]{:S(2)}) collective-permute-start(bf16[160,1280]{1,0:T(8,128)(2,1)S(1)} %get-tuple-element.113), channel_id=1, source_target_pairs={{1,0},{2,3},{5,4},{6,7},{9,8},{10,11},{13,12},{14,15},{17,16},{18,... | collective-permute-start | bytes 1228808 | tf_op jit(solution)/shard_map/ppermute | solution.py:299
  56.5 23.5 %collective-permute-start.17 = (bf16[160,1280]{1,0:T(8,128)(2,1)S(1)}, bf16[160,1280]{1,0:T(8,128)(2,1)S(1)}, u32[]{:S(2)}, u32[]{:S(2)}) collective-permute-start(bf16[160,1280]{1,0:T(8,128)(2,1)S(1)} %get-tuple-element.109.other_chip), channel_id=1, source_target_pairs={{0,4},{4,0},{8,12},{12,8},{1,5},{5,1},{9,13},{13,9},{2,6},{6,2},{1... | collective-permute-start | bytes 1228808 | tf_op jit(solution)/shard_map/ppermute | solution.py:274
  59.7 20.2 %collective-permute-start.18 = (bf16[160,1280]{1,0:T(8,128)(2,1)S(1)}, bf16[160,1280]{1,0:T(8,128)(2,1)S(1)}, u32[]{:S(2)}, u32[]{:S(2)}) collective-permute-start(bf16[160,1280]{1,0:T(8,128)(2,1)S(1)} %get-tuple-element.111), channel_id=1, source_target_pairs={{1,0},{2,3},{5,4},{6,7},{9,8},{10,11},{13,12},{14,15},{17,16},{18,... | collective-permute-start | bytes 1228808 | tf_op jit(solution)/shard_map/ppermute | solution.py:299
  61.0 19.1 %copy-start.6 = (s32[640]{0:T(1024)S(1)}, s32[640]{0:T(1024)}, u32[]{:S(2)}) copy-start(s32[640]{0:T(1024)} %param.9) | copy-start | bytes 7684
  64.1 16.0 %collective-permute-start.16 = (bf16[160,1280]{1,0:T(8,128)(2,1)S(1)}, bf16[160,1280]{1,0:T(8,128)(2,1)S(1)}, u32[]{:S(2)}, u32[]{:S(2)}) collective-permute-start(bf16[160,1280]{1,0:T(8,128)(2,1)S(1)} %get-tuple-element.108.own), channel_id=1, source_target_pairs={{0,4},{4,0},{8,12},{12,8},{1,5},{5,1},{9,13},{13,9},{2,6},{6,2},{1... | collective-permute-start | bytes 1228808 | tf_op jit(solution)/shard_map/ppermute | solution.py:274
  64.1 18.3 %collective-permute-start.21 = (bf16[160,1280]{1,0:T(8,128)(2,1)S(1)}, bf16[160,1280]{1,0:T(8,128)(2,1)S(1)}, u32[]{:S(2)}, u32[]{:S(2)}) collective-permute-start(bf16[160,1280]{1,0:T(8,128)(2,1)S(1)} %get-tuple-element.121), channel_id=1, source_target_pairs={{1,2},{2,1},{5,6},{6,5},{9,10},{10,9},{13,14},{14,13},{17,18},{18,... | collective-permute-start | bytes 1228808 | tf_op jit(solution)/shard_map/ppermute | solution.py:291
  71.2 17.3 %collective-permute-start.20 = (bf16[160,1280]{1,0:T(8,128)(2,1)S(1)}, bf16[160,1280]{1,0:T(8,128)(2,1)S(1)}, u32[]{:S(2)}, u32[]{:S(2)}) collective-permute-start(bf16[160,1280]{1,0:T(8,128)(2,1)S(1)} %get-tuple-element.120), channel_id=1, source_target_pairs={{1,0},{2,3},{5,4},{6,7},{9,8},{10,11},{13,12},{14,15},{17,16},{18,... | collective-permute-start | bytes 1228808 | tf_op jit(solution)/shard_map/ppermute | solution.py:299
  82.5 12.3 %collective-permute-start.22 = (bf16[160,1280]{1,0:T(8,128)(2,1)S(1)}, bf16[160,1280]{1,0:T(8,128)(2,1)S(1)}, u32[]{:S(2)}, u32[]{:S(2)}) collective-permute-start(bf16[160,1280]{1,0:T(8,128)(2,1)S(1)} %get-tuple-element.128), channel_id=1, source_target_pairs={{1,0},{2,3},{5,4},{6,7},{9,8},{10,11},{13,12},{14,15},{17,16},{18,... | collective-permute-start | bytes 1228808 | tf_op jit(solution)/shard_map/ppermute | solution.py:299

commit v3 on v2

--- a/solution.py
+++ b/solution.py
@@ -11,7 +11,8 @@
 BF16 = jnp.bfloat16
 F32 = jnp.float32
 NARROW = 256
-VMEM_GRANT = 56 << 20
+VMEM_GRANT = 24 << 20
+COST = pl.CostEstimate(flops=0, bytes_accessed=0, transcendentals=0)
 
 
 def dot(values, piece):
@@ -67,17 +68,23 @@
         copy.wait()
 
 
-def cut_first(gradients, depth):
+def cut_gradients(gradients, depth):
     tokens = gradients.shape[0]
     half = tokens // 2
 
-    def kernel(grad, beside, own, token, sems):
-        core, col = lax.axis_index("row") % 2, lax.axis_index("col")
-        part = pl.ds(pl.multiple_of(core * half, half), half)
+    def kernel(grad, beside, distant, own, token, sems):
+        row, col = lax.axis_index("row"), lax.axis_index("col")
+        core, chip = row % 2, row // 2
+        target = jnp.where(core == 0, 3 - col, col + 2 - 4 * (col // 2))
+
+        def part(index):
+            return pl.ds(pl.multiple_of(index * half, half), half)
+
         token[...] = jnp.zeros_like(token)
         copy_all(
             [
-                (columns_of(grad, part, col + 1 - 2 * (col % 2), depth), beside),
+                (columns_of(grad, part(core), col + 1 - 2 * (col % 2), depth), beside),
+                (columns_of(grad, part(chip), target, depth), distant),
                 (columns_of(grad, pl.ds(0, tokens), col, depth), own),
             ],
             sems,
@@ -85,29 +92,25 @@
 
     return pl.pallas_call(
         kernel,
-        out_shape=[shaped(half, depth), shaped(tokens, depth), shaped(8, 128, dtype=F32)],
+        out_shape=[shaped(half, depth)] * 2 + [shaped(tokens, depth), shaped(8, 128, dtype=F32)],
         in_specs=[ANY],
-        out_specs=[VMEM] * 3,
-        scratch_shapes=[pltpu.SemaphoreType.DMA((2,))],
+        out_specs=[VMEM] * 4,
+        scratch_shapes=[pltpu.SemaphoreType.DMA((3,))],
+        cost_estimate=COST,
         compiler_params=pltpu.CompilerParams(vmem_limit_bytes=VMEM_GRANT),
     )(gradients)
 
 
-def cut_rest(activations, gradients, depth, before):
+def cut_activations(activations, depth, token):
     tokens = activations.shape[0]
-    half = tokens // 2
-
-    def kernel(act, grad, before, far, mine, across, twice, token, sems):
+
+    def kernel(act, before, far, mine, token, sems):
+        row = lax.axis_index("row")
+        core, chip = row % 2, row // 2
+        whole, left, right = pl.ds(0, tokens), pl.ds(0, depth), pl.ds(depth, depth)
         token[...] = before[...]
-        row, col = lax.axis_index("row"), lax.axis_index("col")
-        core, chip = row % 2, row // 2
-        whole = pl.ds(0, tokens)
-        part = pl.ds(pl.multiple_of(core * half, half), half)
-        left, right = pl.ds(0, depth), pl.ds(depth, depth)
         copy_all(
             [
-                (columns_of(grad, part, 3 - col, depth), across),
-                (columns_of(grad, part, col + 2 - 4 * (col // 2), depth), twice),
                 (columns_of(act, whole, 2 - 2 * chip + core, depth), far.at[:, left]),
                 (columns_of(act, whole, 3 - 2 * chip - core, depth), far.at[:, right]),
                 (columns_of(act, whole, 2 * chip + core, depth), mine.at[:, left]),
@@ -118,17 +121,16 @@
 
     return pl.pallas_call(
         kernel,
-        out_shape=[shaped(tokens, 2 * depth)] * 2
-        + [shaped(half, depth)] * 2
-        + [shaped(8, 128, dtype=F32)],
-        in_specs=[ANY] * 2 + [VMEM],
-        out_specs=[VMEM] * 5,
-        scratch_shapes=[pltpu.SemaphoreType.DMA((6,))],
+        out_shape=[shaped(tokens, 2 * depth)] * 2 + [shaped(8, 128, dtype=F32)],
+        in_specs=[ANY, VMEM],
+        out_specs=[VMEM] * 3,
+        scratch_shapes=[pltpu.SemaphoreType.DMA((4,))],
+        cost_estimate=COST,
         compiler_params=pltpu.CompilerParams(vmem_limit_bytes=48 << 20),
-    )(activations, gradients, before)
-
-
-def step(function, shapes, values, token, after=(), grant=16 << 20, flops=0):
+    )(activations, token)
+
+
+def step(function, shapes, values, token, after=(), grant=16 << 20):
     count, shapes = len(values), list(shapes) + [shaped(8, 128, dtype=F32)]
 
     def kernel(*refs):
@@ -142,7 +144,7 @@
         out_shape=shapes,
         in_specs=[VMEM] * (count + 1) + [ANY] * len(after),
         out_specs=[VMEM] * len(shapes),
-        cost_estimate=pl.CostEstimate(flops=flops, bytes_accessed=0, transcendentals=0),
+        cost_estimate=COST,
         compiler_params=pltpu.CompilerParams(vmem_limit_bytes=grant),
     )(*values, token, *after)
 
@@ -152,8 +154,8 @@
     return (col == 1) | (col == 2)
 
 
-def both_halves(here, there):
-    first = lax.axis_index("row") % 2 == 0
+def both_halves(here, there, index):
+    first = index == 0
     return jnp.concatenate([jnp.where(first, here, there), jnp.where(first, there, here)], 0)
 
 
@@ -200,6 +202,7 @@
         in_specs=[VMEM] * 6,
         out_specs=[VMEM, SMEM, VMEM],
         scratch_shapes=[pltpu.VMEM((rows, width), BF16)],
+        cost_estimate=COST,
         compiler_params=pltpu.CompilerParams(vmem_limit_bytes=24 << 20),
     )(seq_ids.reshape(-1, 128), *blocks, token)
 
@@ -279,7 +282,7 @@
     width = output_basis.shape[1]
     half = tokens // 2
     wide, short = shaped(tokens, width, dtype=F32), shaped(tokens, width)
-    block = shaped(tokens, depth)
+    block, piece = shaped(tokens, depth), shaped(half, depth)
     parts, known, came, crossed, went = [], [None] * 4, [None] * 4, [None] * 4, [None] * 4
 
     def add_inward(j, token):
@@ -288,7 +291,7 @@
             return jnp.where(is_inner(), total, part[...]), total.astype(BF16)
 
         known[j], sent, token = step(function, [wide, short], [parts[j], came[j]], token)
-        crossed[j] = lax.ppermute(sent, "col", [(1, 2), (2, 1)])
+        crossed[j] = lax.ppermute(sent, ("row", "col"), [(4 * r + c, 4 * r + 3 - c if c in (1, 2) else 4 * (r ^ 1) + c) for r in range(4) for c in range(4)])
         return token
 
     def add_crossed(j, token):
@@ -314,16 +317,14 @@
         return total, total.astype(BF16)
 
     def project_beside(here, there, own, basis):
-        total = dot(both_halves(here[...], there[...]), basis[...])
+        total = dot(both_halves(here[...], there[...], lax.axis_index("row") % 2), basis[...])
         inner = is_inner()
         return jnp.where(inner, total, own[...]), jnp.where(inner, own[...], total), total.astype(BF16)
 
     def project_others(here, there, basis):
-        across = both_halves(here[:half], there[:half])
-        twice = both_halves(here[half:], there[half:])
-        inner = is_inner()
-        one = dot(jnp.where(inner, across, twice), basis[...])
-        two = dot(jnp.where(inner, twice, across), basis[...])
+        straight = is_inner() == (lax.axis_index("row") % 2 == 0)
+        one = dot(jnp.where(straight, here[...], there[...]), basis[...])
+        two = dot(jnp.where(straight, there[...], here[...]), basis[...])
         return one, two, one.astype(BF16), two.astype(BF16)
 
     def project_act(values, basis, other):
@@ -334,38 +335,52 @@
         return [(total[...] + other[...].astype(F32)).astype(BF16)]
 
     other_basis = by_xor(input_basis, "row", 1)
-    beside, own, token = cut_first(gradients, depth)
+    def same(value):
+        return [value[...]]
+
+    beside, distant, own, token = cut_gradients(gradients, depth)
     beside = by_xor(beside, "col", 1)
+    distant = lax.ppermute(
+        distant,
+        ("row", "col"),
+        [(4 * r + c, 4 * r + (c ^ 2 if r % 2 else 3 - c)) for r in range(4) for c in range(4)],
+    )
     own_part, sent, token = step(project_own, [wide, short], [own, output_basis], token)
     came[0] = inward(sent)
-    far, mine, across, twice, token = cut_rest(activations, gradients, depth, token)
-    across = by_xor(across, "col", 3)
-    twice = by_xor(twice, "col", 2)
+    far, mine, token = cut_activations(activations, depth, token)
     far = by_xor(far, "row", 2)
-    beside, token = step(
-        lambda one: [one[...]], [shaped(half, depth)], [beside], token, after=[other_basis]
-    )
+    beside, token = step(same, [piece], [beside], token)
+    distant, token = step(same, [piece], [distant], token)
+    distant_there = by_xor(distant, "row", 2)
     one, two, sent, token = step(
         project_beside,
         [wide, wide, short],
         [beside, by_xor(beside, "row", 1), own_part, output_basis],
         token,
+        after=[other_basis],
     )
     parts += [one, two]
     came[1] = inward(sent)
     token = add_inward(0, token)
-    pieces, token = step(
-        lambda one, two: [jnp.concatenate([one[...], two[...]], 0)], [block], [across, twice], token
-    )
-    near_sum, sent, token = step(
-        project_act, [wide, short], [mine, input_basis, other_basis], token, flops=10**11
-    )
-    near_there = by_xor(sent, "row", 2)
+    distant, token = step(
+        lambda here, there: [both_halves(here[...], there[...], lax.axis_index("row") // 2)],
+        [block],
+        [distant, distant_there],
+        token,
+    )
     one, two, one_sent, two_sent, token = step(
-        project_others, [wide, wide, short, short], [pieces, by_xor(pieces, "row", 1), output_basis], token
+        project_others,
+        [wide, wide, short, short],
+        [distant, by_xor(distant, "row", 1), output_basis],
+        token,
     )
     parts += [one, two]
     came[2], came[3] = inward(one_sent), inward(two_sent)
+    late = [None] * 4
+    near_sum, sent, token = step(
+        project_act, [wide, short], [mine, input_basis, other_basis], token
+    )
+    near_there = by_xor(sent, "row", 2)
     token = add_inward(1, token)
     token = add_crossed(0, token)
     far_sum, sent, token = step(project_act, [wide, short], [far, input_basis, other_basis], token)
@@ -375,14 +390,13 @@
     far, token = step(add_there, [short], [far_sum, near_there], token)
     far_other = by_xor(far, "row", 1)
     token = add_inward(3, token)
-    token = add_crossed(2, token)
+    late[3], token = finish(3, token)
     near, token = step(add_there, [short], [near_sum, far_there], token)
     near_other = by_xor(near, "row", 1)
-    late = [None] * 4
-    late[3], token = finish(3, token)
+    token = add_crossed(2, token)
     late[2], token = finish(2, token)
+    token = add_crossed(3, token)
     turned, places, token = turn([near, far, near_other, far_other], seq_ids, token)
-    token = add_crossed(3, token)
     late[1], token = finish(1, token)
     return correct(turned, places, late[1:], known[0], crossed[3], went[3])
 

time: 104 us -> 93.9 us (0.903)
  starting transfers between devices: 40.1 us -> 32.6 us
  Pallas kernels: 20.8 us -> 18.9 us
    ppermute x4, waiting for transfers between devices: 24.1 us -> 17.3 us  [add_crossed(): went[j] = lax.ppermute(sent, 'col', [(1, 0), (2, 3)])]
    ppermute x4, waiting for transfers between devices: 3.3 us -> 8.47 us  [inward(): return lax.ppermute(sent, 'col', [(0, 1), (3, 2)])]
    ppermute x4 -> x5, waiting for transfers between devices: 0.01 us -> 4.55 us  [the longest x1 4.54 us: run(): lax.ppermute(distant, ('row', 'col'), [(4 * r + c, 4 * r + (c ^ 2 if r %...]
    ppermute x4, starting transfers between devices: 20 us -> 15.7 us  [inward(): return lax.ppermute(sent, 'col', [(0, 1), (3, 2)])]
    ppermute x11 -> x10, waiting for transfers between devices: 11.5 us -> 7.83 us  [by_xor(): return lax.ppermute(values, axis, [(i, i ^ bits) for i in range(4)])]
    ppermute x11 -> x10, starting transfers between devices: 12.2 us -> 9.07 us  [by_xor(): return lax.ppermute(values, axis, [(i, i ^ bits) for i in range(4)])]
    pallas_call x2, Pallas kernels: 2.26 us -> 0.34 us  [the longest x1 0.2 us: cut_activations(): pl.pallas_call(kernel, out_shape=[shaped(tokens, 2 * depth)] * 2 + [shape...]
    unnamed x16 -> x12, local copies, waits for them, and re-layouts: 3.63 us -> 3.37 us
  transfers between devices with their start and end apart: 23 -> 23, of which waited for: 8 -> 11; matrix products, arithmetic and copies ran while one was open for 0% -> 0% of each run, Pallas kernels for 11% -> 11%
where the time goes in v3:
time: 93.9 us; the launch traced here: 93.6 us
  waiting for transfers between devices  38.2 us (41%)
  starting transfers between devices  32.6 us (35%)
  Pallas kernels  18.9 us (20%)
  local copies, waits for them, and re-layouts  3.37 us (4%)
    ppermute x4, waiting for transfers between devices, add_crossed(): went[j] = lax.ppermute(sent, 'col', [(1, 0), (2, 3)])  17.3 us
    ppermute x4, starting transfers between devices, inward(): return lax.ppermute(sent, 'col', [(0, 1), (3, 2)])  15.7 us
    ppermute x10, starting transfers between devices, by_xor(): return lax.ppermute(values, axis, [(i, i ^ bits) for i in range(4)])  9.07 us
    pallas_call x1, Pallas kernels, correct(): pl.pallas_call(kernel, out_shape=shaped(height, width, dtype=F32), in_spe...  8.94 us
    ppermute x4, waiting for transfers between devices, inward(): return lax.ppermute(sent, 'col', [(0, 1), (3, 2)])  8.47 us
    ppermute x10, waiting for transfers between devices, by_xor(): return lax.ppermute(values, axis, [(i, i ^ bits) for i in range(4)])  7.83 us
    pallas_call x21, Pallas kernels, step(): pl.pallas_call(kernel, out_shape=shapes, in_specs=[VMEM] * (count + 1) +...  7.33 us
    ppermute x4, starting transfers between devices, add_crossed(): went[j] = lax.ppermute(sent, 'col', [(1, 0), (2, 3)])  5.16 us
  transfers between devices with their start and end apart: 23, of which 11 were waited for; matrix products, arithmetic and copies ran while one was open for 0% of the time, Pallas kernels for 11%

profile of v3, /device:TPU:0, one launch (start us, length us, event | category | flops | bytes accessed | tf_op | source)
XLA Modules:
  0.0 93.6 jit_solution(16118726131581878409)
XLA Ops:
  0.5 1.4 %copy-done.3 = bf16[160,5120]{1,0:T(8,128)(2,1)S(1)} copy-done((bf16[160,5120]{1,0:T(8,128)(2,1)S(1)}, bf16[160,5120]{1,0:T(8,128)(2,1)}, u32[]{:S(2)}) %copy-start.3) | copy-done | bytes 1638424
  2.0 2.6 %collective-permute-start.2 = (bf16[80,1280]{1,0:T(8,128)(2,1)S(1)}, bf16[80,1280]{1,0:T(8,128)(2,1)S(1)}, u32[]{:S(2)}, u32[]{:S(2)}) collective-permute-start(bf16[80,1280]{1,0:T(8,128)(2,1)S(1)} %get-tuple-element.73), channel_id=1, source_target_pairs={{0,1},{1,0},{2,3},{3,2},{4,5},{5,4},{6,7},{7,6},{8,9},{9,8},{10,11... | collective-permute-start | bytes 614408 | tf_op jit(solution)/shard_map/ppermute | solution.py:277
  4.7 2.5 %collective-permute-start.1 = (bf16[80,1280]{1,0:T(8,128)(2,1)S(1)}, bf16[80,1280]{1,0:T(8,128)(2,1)S(1)}, u32[]{:S(2)}, u32[]{:S(2)}) collective-permute-start(bf16[80,1280]{1,0:T(8,128)(2,1)S(1)} %get-tuple-element.72), channel_id=1, source_target_pairs={{0,3},{1,2},{2,1},{3,0},{4,6},{5,7},{6,4},{7,5},{8,11},{9,10},{10,... | collective-permute-start | bytes 614408 | tf_op jit(solution)/shard_map/ppermute | solution.py:343
  7.1 1.9 %copy-done = bf16[1280,1280]{1,0:T(8,128)(2,1)S(1)} copy-done((bf16[1280,1280]{1,0:T(8,128)(2,1)S(1)}, bf16[1280,1280]{1,0:T(8,128)(2,1)}, u32[]{:S(2)}) %copy-start) | copy-done | bytes 3276824
  9.1 0.7 shard_map.56
  9.8 2.7 %collective-permute-start.5 = (bf16[160,1280]{1,0:T(8,128)(2,1)S(1)}, bf16[160,1280]{1,0:T(8,128)(2,1)S(1)}, u32[]{:S(2)}, u32[]{:S(2)}) collective-permute-start(bf16[160,1280]{1,0:T(8,128)(2,1)S(1)} %get-tuple-element.81), channel_id=1, source_target_pairs={{0,1},{3,2},{4,5},{7,6},{8,9},{11,10},{12,13},{15,14},{16,17},{19,... | collective-permute-start | bytes 1228808 | tf_op jit(solution)/shard_map/ppermute | solution.py:313
  12.9 4.5 %collective-permute-done.1.refs_0_ = bf16[80,1280]{1,0:T(8,128)(2,1)S(1)} collective-permute-done((bf16[80,1280]{1,0:T(8,128)(2,1)S(1)}, bf16[80,1280]{1,0:T(8,128)(2,1)S(1)}, u32[]{:S(2)}, u32[]{:S(2)}) %collective-permute-start.1) | collective-permute-done | bytes 204832 | tf_op jit(solution)/shard_map/ppermute | solution.py:343
  17.4 1.6 %collective-permute-start.3 = (bf16[80,1280]{1,0:T(8,128)(2,1)S(1)}, bf16[80,1280]{1,0:T(8,128)(2,1)S(1)}, u32[]{:S(2)}, u32[]{:S(2)}) collective-permute-start(bf16[80,1280]{1,0:T(8,128)(2,1)S(1)} %get-tuple-element.76.refs_0_), channel_id=1, source_target_pairs={{0,8},{4,12},{8,0},{12,4},{1,9},{5,13},{9,1},{13,5},{2,10},{6,14},... | collective-permute-start | bytes 614408 | tf_op jit(solution)/shard_map/ppermute | solution.py:277
  19.0 0.8 shard_map.60
  19.8 3.1 %collective-permute-done.5.refs_1_ = bf16[160,1280]{1,0:T(8,128)(2,1)S(1)} collective-permute-done((bf16[160,1280]{1,0:T(8,128)(2,1)S(1)}, bf16[160,1280]{1,0:T(8,128)(2,1)S(1)}, u32[]{:S(2)}, u32[]{:S(2)}) %collective-permute-start.5) | collective-permute-done | bytes 409632 | tf_op jit(solution)/shard_map/ppermute | solution.py:313
  23.4 1.6 %collective-permute-start.7 = (bf16[160,2560]{1,0:T(8,128)(2,1)S(1)}, bf16[160,2560]{1,0:T(8,128)(2,1)S(1)}, u32[]{:S(2)}, u32[]{:S(2)}) collective-permute-start(bf16[160,2560]{1,0:T(8,128)(2,1)S(1)} %get-tuple-element.88), channel_id=1, source_target_pairs={{0,8},{4,12},{8,0},{12,4},{1,9},{5,13},{9,1},{13,5},{2,10},{6,14},... | collective-permute-start | bytes 2457608 | tf_op jit(solution)/shard_map/ppermute | solution.py:277
  25.0 4.2 %collective-permute-start.9 = (bf16[160,1280]{1,0:T(8,128)(2,1)S(1)}, bf16[160,1280]{1,0:T(8,128)(2,1)S(1)}, u32[]{:S(2)}, u32[]{:S(2)}) collective-permute-start(bf16[160,1280]{1,0:T(8,128)(2,1)S(1)} %get-tuple-element.92), channel_id=1, source_target_pairs={{0,1},{3,2},{4,5},{7,6},{8,9},{11,10},{12,13},{15,14},{16,17},{19,... | collective-permute-start | bytes 1228808 | tf_op jit(solution)/shard_map/ppermute | solution.py:313
  29.2 1.3 %shard_map.63 = (f32[160,1280]{1,0:T(8,128)S(1)}, f32[160,1280]{1,0:T(8,128)S(1)}, bf16[160,1280]{1,0:T(8,128)(2,1)S(1)}, bf16[160,1280]{1,0:T(8,128)(2,1)S(1)}, f32[8,128]{1,0:T(8,128)S(1)}) custom-call(bf16[160,1280]{1,0:T(8,128)(2,1)S(1)} %get-tuple-element.84.refs_0_, bf16[160,1280]{1,0:T(8,128)(2,1)S(1)} %collective-permute-done.6.refs_1_, ...), custom_call_target="tpu_custom_call" | custom-call | tf_op jit(solution)/shard_map/pallas_call | solution.py:142
  30.5 2.8 %collective-permute-start.14 = (bf16[160,1280]{1,0:T(8,128)(2,1)S(1)}, bf16[160,1280]{1,0:T(8,128)(2,1)S(1)}, u32[]{:S(2)}, u32[]{:S(2)}) collective-permute-start(bf16[160,1280]{1,0:T(8,128)(2,1)S(1)} %get-tuple-element.102), channel_id=1, source_target_pairs={{0,1},{3,2},{4,5},{7,6},{8,9},{11,10},{12,13},{15,14},{16,17},{19,... | collective-permute-start | bytes 1228808 | tf_op jit(solution)/shard_map/ppermute | solution.py:313
  33.4 1.2 %shard_map.64 = (f32[160,1280]{1,0:T(8,128)S(1)}, bf16[160,1280]{1,0:T(8,128)(2,1)S(1)}, f32[8,128]{1,0:T(8,128)S(1)}) custom-call(bf16[160,2560]{1,0:T(8,128)(2,1)S(1)} %get-tuple-element.71.refs_0_, bf16[1280,1280]{1,0:T(8,128)(2,1)S(1)} %copy-done.2, bf16[1280,1280]{1,0:T(8,128)(2,1)S(1)} %collective-permute-done.refs_5_.refs_2_, ...), custom_call_target="tpu_custom_call" | custom-call | tf_op jit(solution)/shard_map/pallas_call | solution.py:142
  34.6 4.3 %collective-permute-done.9.refs_1_ = bf16[160,1280]{1,0:T(8,128)(2,1)S(1)} collective-permute-done((bf16[160,1280]{1,0:T(8,128)(2,1)S(1)}, bf16[160,1280]{1,0:T(8,128)(2,1)S(1)}, u32[]{:S(2)}, u32[]{:S(2)}) %collective-permute-start.9) | collective-permute-done | bytes 409632 | tf_op jit(solution)/shard_map/ppermute | solution.py:313
  39.8 5.9 %collective-permute-start.11 = (bf16[160,1280]{1,0:T(8,128)(2,1)S(1)}, bf16[160,1280]{1,0:T(8,128)(2,1)S(1)}, u32[]{:S(2)}, u32[]{:S(2)}) collective-permute-start(bf16[160,1280]{1,0:T(8,128)(2,1)S(1)} %get-tuple-element.97), channel_id=1, source_target_pairs={{0,1},{3,2},{4,5},{7,6},{8,9},{11,10},{12,13},{15,14},{16,17},{19,... | collective-permute-start | bytes 1228808 | tf_op jit(solution)/shard_map/ppermute | solution.py:313
  45.8 1.3 %collective-permute-start.15 = (bf16[160,1280]{1,0:T(8,128)(2,1)S(1)}, bf16[160,1280]{1,0:T(8,128)(2,1)S(1)}, u32[]{:S(2)}, u32[]{:S(2)}) collective-permute-start(bf16[160,1280]{1,0:T(8,128)(2,1)S(1)} %get-tuple-element.108), channel_id=1, source_target_pairs={{1,0},{2,3},{5,4},{6,7},{9,8},{10,11},{13,12},{14,15},{17,16},{18,... | collective-permute-start | bytes 1228808 | tf_op jit(solution)/shard_map/ppermute | solution.py:302
  47.1 1.2 %shard_map.67 = (f32[160,1280]{1,0:T(8,128)S(1)}, bf16[160,1280]{1,0:T(8,128)(2,1)S(1)}, f32[8,128]{1,0:T(8,128)S(1)}) custom-call(bf16[160,2560]{1,0:T(8,128)(2,1)S(1)} %collective-permute-done.7.refs_0_, bf16[1280,1280]{1,0:T(8,128)(2,1)S(1)} %copy-done.2, bf16[1280,1280]{1,0:T(8,128)(2,1)S(1)} %collective-permute-done.refs_5_.refs_2_, ...), custom_call_target="tpu_custom_call" | custom-call | tf_op jit(solution)/shard_map/pallas_call | solution.py:142
  48.3 1.6 %collective-permute-start.10 = (bf16[160,1280]{1,0:T(8,128)(2,1)S(1)}, bf16[160,1280]{1,0:T(8,128)(2,1)S(1)}, u32[]{:S(2)}, u32[]{:S(2)}) collective-permute-start(bf16[160,1280]{1,0:T(8,128)(2,1)S(1)} %get-tuple-element.96), channel_id=1, source_target_pairs={{0,8},{4,12},{8,0},{12,4},{1,9},{5,13},{9,1},{13,5},{2,10},{6,14},... | collective-permute-start | bytes 1228808 | tf_op jit(solution)/shard_map/ppermute | solution.py:277
  50.2 3.1 %collective-permute-done.12.refs_1_ = bf16[160,1280]{1,0:T(8,128)(2,1)S(1)} collective-permute-done((bf16[160,1280]{1,0:T(8,128)(2,1)S(1)}, bf16[160,1280]{1,0:T(8,128)(2,1)S(1)}, u32[]{:S(2)}, u32[]{:S(2)}) %collective-permute-start.12) | collective-permute-done | bytes 409632 | tf_op jit(solution)/shard_map/ppermute | solution.py:277
  53.3 1.3 %collective-permute-start.19 = (bf16[160,1280]{1,0:T(8,128)(2,1)S(1)}, bf16[160,1280]{1,0:T(8,128)(2,1)S(1)}, u32[]{:S(2)}, u32[]{:S(2)}) collective-permute-start(bf16[160,1280]{1,0:T(8,128)(2,1)S(1)} %get-tuple-element.115), channel_id=1, source_target_pairs={{1,0},{2,3},{5,4},{6,7},{9,8},{10,11},{13,12},{14,15},{17,16},{18,... | collective-permute-start | bytes 1228808 | tf_op jit(solution)/shard_map/ppermute | solution.py:302
  54.7 1.0 %collective-permute-done.11.refs_1_ = bf16[160,1280]{1,0:T(8,128)(2,1)S(1)} collective-permute-done((bf16[160,1280]{1,0:T(8,128)(2,1)S(1)}, bf16[160,1280]{1,0:T(8,128)(2,1)S(1)}, u32[]{:S(2)}, u32[]{:S(2)}) %collective-permute-start.11) | collective-permute-done | bytes 409632 | tf_op jit(solution)/shard_map/ppermute | solution.py:313
  55.9 1.0 %collective-permute-done.15.refs_2_ = bf16[160,1280]{1,0:T(8,128)(2,1)S(1)} collective-permute-done((bf16[160,1280]{1,0:T(8,128)(2,1)S(1)}, bf16[160,1280]{1,0:T(8,128)(2,1)S(1)}, u32[]{:S(2)}, u32[]{:S(2)}) %collective-permute-start.15) | collective-permute-done | bytes 409632 | tf_op jit(solution)/shard_map/ppermute | solution.py:302
  57.1 4.5 %collective-permute-done.10.refs_1_ = bf16[160,1280]{1,0:T(8,128)(2,1)S(1)} collective-permute-done((bf16[160,1280]{1,0:T(8,128)(2,1)S(1)}, bf16[160,1280]{1,0:T(8,128)(2,1)S(1)}, u32[]{:S(2)}, u32[]{:S(2)}) %collective-permute-start.10) | collective-permute-done | bytes 409632 | tf_op jit(solution)/shard_map/ppermute | solution.py:277
  62.4 1.3 %collective-permute-start.21 = (bf16[160,1280]{1,0:T(8,128)(2,1)S(1)}, bf16[160,1280]{1,0:T(8,128)(2,1)S(1)}, u32[]{:S(2)}, u32[]{:S(2)}) collective-permute-start(bf16[160,1280]{1,0:T(8,128)(2,1)S(1)} %get-tuple-element.124), channel_id=1, source_target_pairs={{1,0},{2,3},{5,4},{6,7},{9,8},{10,11},{13,12},{14,15},{17,16},{18,... | collective-permute-start | bytes 1228808 | tf_op jit(solution)/shard_map/ppermute | solution.py:302
  63.7 2.1 %collective-permute-done.19.refs_2_ = bf16[160,1280]{1,0:T(8,128)(2,1)S(1)} collective-permute-done((bf16[160,1280]{1,0:T(8,128)(2,1)S(1)}, bf16[160,1280]{1,0:T(8,128)(2,1)S(1)}, u32[]{:S(2)}, u32[]{:S(2)}) %collective-permute-start.19) | collective-permute-done | bytes 409632 | tf_op jit(solution)/shard_map/ppermute | solution.py:302
  66.0 1.3 %collective-permute-start.22 = (bf16[160,1280]{1,0:T(8,128)(2,1)S(1)}, bf16[160,1280]{1,0:T(8,128)(2,1)S(1)}, u32[]{:S(2)}, u32[]{:S(2)}) collective-permute-start(bf16[160,1280]{1,0:T(8,128)(2,1)S(1)} %get-tuple-element.130), channel_id=1, source_target_pairs={{1,0},{2,3},{5,4},{6,7},{9,8},{10,11},{13,12},{14,15},{17,16},{18,... | collective-permute-start | bytes 1228808 | tf_op jit(solution)/shard_map/ppermute | solution.py:302
  67.3 2.3 %shard_map.77 = (bf16[4,1280,512]{2,1,0:T(8,128)(2,1)S(1)}, s32[8]{0:T(128)S(1)}, f32[8,128]{1,0:T(8,128)S(1)}) custom-call(s32[5,128]{1,0:T(8,128)S(1)} %bitcast.1, bf16[160,1280]{1,0:T(8,128)(2,1)S(1)} %get-tuple-element.111.own, bf16[160,1280]{1,0:T(8,128)(2,1)S(1)} %get-tuple-element.112.other_chip, ...), custom_call_target="tpu_custom_call" | custom-call | tf_op jit(solution)/shard_map/pallas_call | solution.py:195
  69.6 7.0 %collective-permute-done.21.refs_2_ = bf16[160,1280]{1,0:T(8,128)(2,1)S(1)} collective-permute-done((bf16[160,1280]{1,0:T(8,128)(2,1)S(1)}, bf16[160,1280]{1,0:T(8,128)(2,1)S(1)}, u32[]{:S(2)}, u32[]{:S(2)}) %collective-permute-start.21) | collective-permute-done | bytes 409632 | tf_op jit(solution)/shard_map/ppermute | solution.py:302
  77.3 7.2 %collective-permute-done.22.outward = bf16[160,1280]{1,0:T(8,128)(2,1)S(1)} collective-permute-done((bf16[160,1280]{1,0:T(8,128)(2,1)S(1)}, bf16[160,1280]{1,0:T(8,128)(2,1)S(1)}, u32[]{:S(2)}, u32[]{:S(2)}) %collective-permute-start.22) | collective-permute-done | bytes 409632 | tf_op jit(solution)/shard_map/ppermute | solution.py:302
  84.5 8.9 %shard_map.79 = f32[1280,1280]{1,0:T(8,128)} custom-call(s32[8]{0:T(128)S(1)} %get-tuple-element.121.place, bf16[4,1280,512]{2,1,0:T(8,128)(2,1)S(1)} %get-tuple-element.122.turned, bf16[160,1280]{1,0:T(8,128)(2,1)S(1)} %get-tuple-element.126.one, bf16[160,1280]{1,0:T(8,128)(2,1)S(1)} %get-tuple-element.127.two, ...), custom_call_target="tpu_custom_call" | custom-call | tf_op jit(solution)/shard_map/pallas_call | solution.py:261
  (51 shorter events, 4.8 us)
Async XLA Ops:
  0.0 19.0 %collective-permute-start = (bf16[1280,1280]{1,0:T(8,128)(2,1)}, bf16[1280,1280]{1,0:T(8,128)(2,1)S(1)}, u32[]{:S(2)}, u32[]{:S(2)}) collective-permute-start(bf16[1280,1280]{1,0:T(8,128)(2,1)} %refs_1_.5), channel_id=1, source_target_pairs={{0,4},{4,0},{8,12},{12,8},{1,5},{5,1},{9,13},{13,9},{2,6},{6,2},{1... | collective-permute-start | bytes 9830408 | tf_op jit(solution)/shard_map/ppermute | solution.py:277
  0.5 1.4 %copy-start.3 = (bf16[160,5120]{1,0:T(8,128)(2,1)S(1)}, bf16[160,5120]{1,0:T(8,128)(2,1)}, u32[]{:S(2)}) copy-start(bf16[160,5120]{1,0:T(8,128)(2,1)} %grad.1) | copy-start | bytes 4915204
  1.9 10.7 %copy-start.4 = (bf16[160,5120]{1,0:T(8,128)(2,1)S(1)}, bf16[160,5120]{1,0:T(8,128)(2,1)}, u32[]{:S(2)}) copy-start(bf16[160,5120]{1,0:T(8,128)(2,1)} %act.1) | copy-start | bytes 4915204
  2.0 10.7 %collective-permute-start.2 = (bf16[80,1280]{1,0:T(8,128)(2,1)S(1)}, bf16[80,1280]{1,0:T(8,128)(2,1)S(1)}, u32[]{:S(2)}, u32[]{:S(2)}) collective-permute-start(bf16[80,1280]{1,0:T(8,128)(2,1)S(1)} %get-tuple-element.73), channel_id=1, source_target_pairs={{0,1},{1,0},{2,3},{3,2},{4,5},{5,4},{6,7},{7,6},{8,9},{9,8},{10,11... | collective-permute-start | bytes 614408 | tf_op jit(solution)/shard_map/ppermute | solution.py:277
  4.7 12.8 %collective-permute-start.1 = (bf16[80,1280]{1,0:T(8,128)(2,1)S(1)}, bf16[80,1280]{1,0:T(8,128)(2,1)S(1)}, u32[]{:S(2)}, u32[]{:S(2)}) collective-permute-start(bf16[80,1280]{1,0:T(8,128)(2,1)S(1)} %get-tuple-element.72), channel_id=1, source_target_pairs={{0,3},{1,2},{2,1},{3,0},{4,6},{5,7},{6,4},{7,5},{8,11},{9,10},{10,... | collective-permute-start | bytes 614408 | tf_op jit(solution)/shard_map/ppermute | solution.py:343
  7.1 1.9 %copy-start = (bf16[1280,1280]{1,0:T(8,128)(2,1)S(1)}, bf16[1280,1280]{1,0:T(8,128)(2,1)}, u32[]{:S(2)}) copy-start(bf16[1280,1280]{1,0:T(8,128)(2,1)} %refs_2_.1) | copy-start | bytes 9830404
  9.1 9.9 %copy-start.1 = (bf16[1280,1280]{1,0:T(8,128)(2,1)S(1)}, bf16[1280,1280]{1,0:T(8,128)(2,1)}, u32[]{:S(2)}) copy-start(bf16[1280,1280]{1,0:T(8,128)(2,1)} %refs_2_.1) | copy-start | bytes 9830404
  9.8 13.1 %collective-permute-start.5 = (bf16[160,1280]{1,0:T(8,128)(2,1)S(1)}, bf16[160,1280]{1,0:T(8,128)(2,1)S(1)}, u32[]{:S(2)}, u32[]{:S(2)}) collective-permute-start(bf16[160,1280]{1,0:T(8,128)(2,1)S(1)} %get-tuple-element.81), channel_id=1, source_target_pairs={{0,1},{3,2},{4,5},{7,6},{8,9},{11,10},{12,13},{15,14},{16,17},{19,... | collective-permute-start | bytes 1228808 | tf_op jit(solution)/shard_map/ppermute | solution.py:313
  12.8 6.2 %collective-permute-start.4 = (bf16[80,1280]{1,0:T(8,128)(2,1)S(1)}, bf16[80,1280]{1,0:T(8,128)(2,1)S(1)}, u32[]{:S(2)}, u32[]{:S(2)}) collective-permute-start(bf16[80,1280]{1,0:T(8,128)(2,1)S(1)} %get-tuple-element.77.refs_0_), channel_id=1, source_target_pairs={{0,4},{4,0},{8,12},{12,8},{1,5},{5,1},{9,13},{13,9},{2,6},{6,2},{1... | collective-permute-start | bytes 614408 | tf_op jit(solution)/shard_map/ppermute | solution.py:277
  17.4 5.8 %collective-permute-start.3 = (bf16[80,1280]{1,0:T(8,128)(2,1)S(1)}, bf16[80,1280]{1,0:T(8,128)(2,1)S(1)}, u32[]{:S(2)}, u32[]{:S(2)}) collective-permute-start(bf16[80,1280]{1,0:T(8,128)(2,1)S(1)} %get-tuple-element.76.refs_0_), channel_id=1, source_target_pairs={{0,8},{4,12},{8,0},{12,4},{1,9},{5,13},{9,1},{13,5},{2,10},{6,14},... | collective-permute-start | bytes 614408 | tf_op jit(solution)/shard_map/ppermute | solution.py:277
  19.8 13.6 %copy-start.2 = (bf16[1280,1280]{1,0:T(8,128)(2,1)S(1)}, bf16[1280,1280]{1,0:T(8,128)(2,1)}, u32[]{:S(2)}) copy-start(bf16[1280,1280]{1,0:T(8,128)(2,1)} %refs_1_.5) | copy-start | bytes 9830404
  23.3 5.9 %collective-permute-start.6 = (bf16[160,1280]{1,0:T(8,128)(2,1)S(1)}, bf16[160,1280]{1,0:T(8,128)(2,1)S(1)}, u32[]{:S(2)}, u32[]{:S(2)}) collective-permute-start(bf16[160,1280]{1,0:T(8,128)(2,1)S(1)} %get-tuple-element.84.refs_0_), channel_id=1, source_target_pairs={{0,4},{4,0},{8,12},{12,8},{1,5},{5,1},{9,13},{13,9},{2,6},{6,2},{1... | collective-permute-start | bytes 1228808 | tf_op jit(solution)/shard_map/ppermute | solution.py:277
  23.4 22.4 %collective-permute-start.7 = (bf16[160,2560]{1,0:T(8,128)(2,1)S(1)}, bf16[160,2560]{1,0:T(8,128)(2,1)S(1)}, u32[]{:S(2)}, u32[]{:S(2)}) collective-permute-start(bf16[160,2560]{1,0:T(8,128)(2,1)S(1)} %get-tuple-element.88), channel_id=1, source_target_pairs={{0,8},{4,12},{8,0},{12,4},{1,9},{5,13},{9,1},{13,5},{2,10},{6,14},... | collective-permute-start | bytes 2457608 | tf_op jit(solution)/shard_map/ppermute | solution.py:277
  25.0 14.0 %collective-permute-start.9 = (bf16[160,1280]{1,0:T(8,128)(2,1)S(1)}, bf16[160,1280]{1,0:T(8,128)(2,1)S(1)}, u32[]{:S(2)}, u32[]{:S(2)}) collective-permute-start(bf16[160,1280]{1,0:T(8,128)(2,1)S(1)} %get-tuple-element.92), channel_id=1, source_target_pairs={{0,1},{3,2},{4,5},{7,6},{8,9},{11,10},{12,13},{15,14},{16,17},{19,... | collective-permute-start | bytes 1228808 | tf_op jit(solution)/shard_map/ppermute | solution.py:313
  29.1 10.6 %collective-permute-start.8 = (bf16[160,1280]{1,0:T(8,128)(2,1)S(1)}, bf16[160,1280]{1,0:T(8,128)(2,1)S(1)}, u32[]{:S(2)}, u32[]{:S(2)}) collective-permute-start(bf16[160,1280]{1,0:T(8,128)(2,1)S(1)} %get-tuple-element.90), channel_id=1, source_target_pairs={{0,4},{1,2},{2,1},{3,7},{4,0},{5,6},{6,5},{7,3},{8,12},{9,10},{10,... | collective-permute-start | bytes 1228808 | tf_op jit(solution)/shard_map/ppermute | solution.py:294
  30.5 17.8 %collective-permute-start.14 = (bf16[160,1280]{1,0:T(8,128)(2,1)S(1)}, bf16[160,1280]{1,0:T(8,128)(2,1)S(1)}, u32[]{:S(2)}, u32[]{:S(2)}) collective-permute-start(bf16[160,1280]{1,0:T(8,128)(2,1)S(1)} %get-tuple-element.102), channel_id=1, source_target_pairs={{0,1},{3,2},{4,5},{7,6},{8,9},{11,10},{12,13},{15,14},{16,17},{19,... | collective-permute-start | bytes 1228808 | tf_op jit(solution)/shard_map/ppermute | solution.py:313
  39.1 11.0 %collective-permute-start.13 = (bf16[160,1280]{1,0:T(8,128)(2,1)S(1)}, bf16[160,1280]{1,0:T(8,128)(2,1)S(1)}, u32[]{:S(2)}, u32[]{:S(2)}) collective-permute-start(bf16[160,1280]{1,0:T(8,128)(2,1)S(1)} %get-tuple-element.101), channel_id=1, source_target_pairs={{0,4},{1,2},{2,1},{3,7},{4,0},{5,6},{6,5},{7,3},{8,12},{9,10},{10,... | collective-permute-start | bytes 1228808 | tf_op jit(solution)/shard_map/ppermute | solution.py:294
  39.2 14.1 %collective-permute-start.12 = (bf16[160,1280]{1,0:T(8,128)(2,1)S(1)}, bf16[160,1280]{1,0:T(8,128)(2,1)S(1)}, u32[]{:S(2)}, u32[]{:S(2)}) collective-permute-start(bf16[160,1280]{1,0:T(8,128)(2,1)S(1)} %get-tuple-element.99), channel_id=1, source_target_pairs={{0,8},{4,12},{8,0},{12,4},{1,9},{5,13},{9,1},{13,5},{2,10},{6,14},... | collective-permute-start | bytes 1228808 | tf_op jit(solution)/shard_map/ppermute | solution.py:277
  39.8 16.0 %collective-permute-start.11 = (bf16[160,1280]{1,0:T(8,128)(2,1)S(1)}, bf16[160,1280]{1,0:T(8,128)(2,1)S(1)}, u32[]{:S(2)}, u32[]{:S(2)}) collective-permute-start(bf16[160,1280]{1,0:T(8,128)(2,1)S(1)} %get-tuple-element.97), channel_id=1, source_target_pairs={{0,1},{3,2},{4,5},{7,6},{8,9},{11,10},{12,13},{15,14},{16,17},{19,... | collective-permute-start | bytes 1228808 | tf_op jit(solution)/shard_map/ppermute | solution.py:313
  45.8 11.2 %collective-permute-start.15 = (bf16[160,1280]{1,0:T(8,128)(2,1)S(1)}, bf16[160,1280]{1,0:T(8,128)(2,1)S(1)}, u32[]{:S(2)}, u32[]{:S(2)}) collective-permute-start(bf16[160,1280]{1,0:T(8,128)(2,1)S(1)} %get-tuple-element.108), channel_id=1, source_target_pairs={{1,0},{2,3},{5,4},{6,7},{9,8},{10,11},{13,12},{14,15},{17,16},{18,... | collective-permute-start | bytes 1228808 | tf_op jit(solution)/shard_map/ppermute | solution.py:302
  48.3 13.3 %collective-permute-start.10 = (bf16[160,1280]{1,0:T(8,128)(2,1)S(1)}, bf16[160,1280]{1,0:T(8,128)(2,1)S(1)}, u32[]{:S(2)}, u32[]{:S(2)}) collective-permute-start(bf16[160,1280]{1,0:T(8,128)(2,1)S(1)} %get-tuple-element.96), channel_id=1, source_target_pairs={{0,8},{4,12},{8,0},{12,4},{1,9},{5,13},{9,1},{13,5},{2,10},{6,14},... | collective-permute-start | bytes 1228808 | tf_op jit(solution)/shard_map/ppermute | solution.py:277
  50.1 12.2 %collective-permute-start.20 = (bf16[160,1280]{1,0:T(8,128)(2,1)S(1)}, bf16[160,1280]{1,0:T(8,128)(2,1)S(1)}, u32[]{:S(2)}, u32[]{:S(2)}) collective-permute-start(bf16[160,1280]{1,0:T(8,128)(2,1)S(1)} %get-tuple-element.116), channel_id=1, source_target_pairs={{0,4},{1,2},{2,1},{3,7},{4,0},{5,6},{6,5},{7,3},{8,12},{9,10},{10,... | collective-permute-start | bytes 1228808 | tf_op jit(solution)/shard_map/ppermute | solution.py:294
  53.3 12.5 %collective-permute-start.19 = (bf16[160,1280]{1,0:T(8,128)(2,1)S(1)}, bf16[160,1280]{1,0:T(8,128)(2,1)S(1)}, u32[]{:S(2)}, u32[]{:S(2)}) collective-permute-start(bf16[160,1280]{1,0:T(8,128)(2,1)S(1)} %get-tuple-element.115), channel_id=1, source_target_pairs={{1,0},{2,3},{5,4},{6,7},{9,8},{10,11},{13,12},{14,15},{17,16},{18,... | collective-permute-start | bytes 1228808 | tf_op jit(solution)/shard_map/ppermute | solution.py:302
  55.9 10.0 %collective-permute-start.18 = (bf16[160,1280]{1,0:T(8,128)(2,1)S(1)}, bf16[160,1280]{1,0:T(8,128)(2,1)S(1)}, u32[]{:S(2)}, u32[]{:S(2)}) collective-permute-start(bf16[160,1280]{1,0:T(8,128)(2,1)S(1)} %get-tuple-element.113), channel_id=1, source_target_pairs={{0,4},{1,2},{2,1},{3,7},{4,0},{5,6},{6,5},{7,3},{8,12},{9,10},{10,... | collective-permute-start | bytes 1228808 | tf_op jit(solution)/shard_map/ppermute | solution.py:294
  57.0 10.3 %copy-start.5 = (s32[640]{0:T(1024)S(1)}, s32[640]{0:T(1024)}, u32[]{:S(2)}) copy-start(s32[640]{0:T(1024)} %param.9) | copy-start | bytes 7684
  61.7 5.6 %collective-permute-start.16 = (bf16[160,1280]{1,0:T(8,128)(2,1)S(1)}, bf16[160,1280]{1,0:T(8,128)(2,1)S(1)}, u32[]{:S(2)}, u32[]{:S(2)}) collective-permute-start(bf16[160,1280]{1,0:T(8,128)(2,1)S(1)} %get-tuple-element.111.own), channel_id=1, source_target_pairs={{0,4},{4,0},{8,12},{12,8},{1,5},{5,1},{9,13},{13,9},{2,6},{6,2},{1... | collective-permute-start | bytes 1228808 | tf_op jit(solution)/shard_map/ppermute | solution.py:277
  61.8 5.5 %collective-permute-start.17 = (bf16[160,1280]{1,0:T(8,128)(2,1)S(1)}, bf16[160,1280]{1,0:T(8,128)(2,1)S(1)}, u32[]{:S(2)}, u32[]{:S(2)}) collective-permute-start(bf16[160,1280]{1,0:T(8,128)(2,1)S(1)} %get-tuple-element.112.other_chip), channel_id=1, source_target_pairs={{0,4},{4,0},{8,12},{12,8},{1,5},{5,1},{9,13},{13,9},{2,6},{6,2},{1... | collective-permute-start | bytes 1228808 | tf_op jit(solution)/shard_map/ppermute | solution.py:277
  62.4 14.2 %collective-permute-start.21 = (bf16[160,1280]{1,0:T(8,128)(2,1)S(1)}, bf16[160,1280]{1,0:T(8,128)(2,1)S(1)}, u32[]{:S(2)}, u32[]{:S(2)}) collective-permute-start(bf16[160,1280]{1,0:T(8,128)(2,1)S(1)} %get-tuple-element.124), channel_id=1, source_target_pairs={{1,0},{2,3},{5,4},{6,7},{9,8},{10,11},{13,12},{14,15},{17,16},{18,... | collective-permute-start | bytes 1228808 | tf_op jit(solution)/shard_map/ppermute | solution.py:302
  66.0 18.5 %collective-permute-start.22 = (bf16[160,1280]{1,0:T(8,128)(2,1)S(1)}, bf16[160,1280]{1,0:T(8,128)(2,1)S(1)}, u32[]{:S(2)}, u32[]{:S(2)}) collective-permute-start(bf16[160,1280]{1,0:T(8,128)(2,1)S(1)} %get-tuple-element.130), channel_id=1, source_target_pairs={{1,0},{2,3},{5,4},{6,7},{9,8},{10,11},{13,12},{14,15},{17,16},{18,... | collective-permute-start | bytes 1228808 | tf_op jit(solution)/shard_map/ppermute | solution.py:302

commit v4 on v3

--- a/solution.py
+++ b/solution.py
@@ -211,7 +211,7 @@
     tokens, width = known.shape
     height, wide = turned.shape[1:]
 
-    def kernel(place, turned, one, two, three, known, crossed, outward, out, grad, left, total, sems):
+    def kernel(place, turned, one, two, three, known, crossed, outward, out, grad, total, sems):
         col = lax.axis_index("col")
         inner = (col == 1) | (col == 2)
 
@@ -219,14 +219,11 @@
             index = jnp.where(col >= 2, 3 - block, block)
             return pl.ds(pl.multiple_of(index * tokens, tokens), tokens)
 
-        lefts = [
-            pltpu.make_async_copy(turned.at[seq], left.at[seq], sems.at[seq]) for seq in range(SEQS)
-        ]
         copies = [
-            pltpu.make_async_copy(ref, grad.at[rows(i + 1)], sems.at[SEQS + i])
+            pltpu.make_async_copy(ref, grad.at[rows(i + 1)], sems.at[i])
             for i, ref in enumerate((one, two, three))
         ]
-        for copy in copies + lefts:
+        for copy in copies:
             copy.start()
         came = jnp.where(inner, crossed[...], outward[...])
         grad[rows(0)] = (known[...] + came.astype(F32)).astype(BF16)
@@ -234,10 +231,9 @@
             copy.wait()
 
         def put(columns):
-            return pltpu.make_async_copy(total.at[:, columns], out.at[:, columns], sems.at[SEQS + 3])
+            return pltpu.make_async_copy(total.at[:, columns], out.at[:, columns], sems.at[3])
 
         for seq in range(SEQS):
-            lefts[seq].wait()
             start = pl.multiple_of(place[2 * seq], 16)
             is_wide = place[2 * seq + 1] == 1
             last = seq == SEQS - 1
@@ -246,7 +242,7 @@
                 columns = slice(begin, begin + step)
 
                 def add(depth):
-                    part = dot(left[seq, :, :depth], grad[pl.ds(start, depth), columns])
+                    part = dot(turned[seq, :, :depth], grad[pl.ds(start, depth), columns])
                     part = part * part
                     if seq:
                         part = total[:, columns] + part
@@ -261,13 +257,12 @@
     return pl.pallas_call(
         kernel,
         out_shape=shaped(height, width, dtype=F32),
-        in_specs=[SMEM] + [ANY] * 4 + [VMEM] * 3,
+        in_specs=[SMEM, VMEM] + [ANY] * 3 + [VMEM] * 3,
         out_specs=ANY,
         scratch_shapes=[
             pltpu.VMEM((4 * tokens, width), BF16),
-            pltpu.VMEM(turned.shape, BF16),
             pltpu.VMEM((height, width), F32),
-            pltpu.SemaphoreType.DMA((SEQS + 4,)),
+            pltpu.SemaphoreType.DMA((4,)),
         ],
         compiler_params=pltpu.CompilerParams(vmem_limit_bytes=24 << 20),
     )(places, turned, *blocks, known, crossed, outward)
@@ -391,9 +386,9 @@
     far_other = by_xor(far, "row", 1)
     token = add_inward(3, token)
     late[3], token = finish(3, token)
+    token = add_crossed(2, token)
     near, token = step(add_there, [short], [near_sum, far_there], token)
     near_other = by_xor(near, "row", 1)
-    token = add_crossed(2, token)
     late[2], token = finish(2, token)
     token = add_crossed(3, token)
     turned, places, token = turn([near, far, near_other, far_other], seq_ids, token)

time: 93.9 us -> 93.4 us (level)
  no operation moved by 1% of the time
where the time goes in v4:
time: 93.4 us; the launch traced here: 93.1 us
  waiting for transfers between devices  38.4 us (41%)
  starting transfers between devices  32.2 us (34%)
  Pallas kernels  18.6 us (20%)
  local copies, waits for them, and re-layouts  3.37 us (4%)
    ppermute x4, waiting for transfers between devices, add_crossed(): went[j] = lax.ppermute(sent, 'col', [(1, 0), (2, 3)])  17.7 us
    ppermute x4, starting transfers between devices, inward(): return lax.ppermute(sent, 'col', [(0, 1), (3, 2)])  15.7 us
    pallas_call x1, Pallas kernels, correct(): pl.pallas_call(kernel, out_shape=shaped(height, width, dtype=F32), in_spe...  8.63 us
    ppermute x10, starting transfers between devices, by_xor(): return lax.ppermute(values, axis, [(i, i ^ bits) for i in range(4)])  8.58 us
    ppermute x4, waiting for transfers between devices, inward(): return lax.ppermute(sent, 'col', [(0, 1), (3, 2)])  8.47 us
    ppermute x10, waiting for transfers between devices, by_xor(): return lax.ppermute(values, axis, [(i, i ^ bits) for i in range(4)])  7.73 us
    pallas_call x21, Pallas kernels, step(): pl.pallas_call(kernel, out_shape=shapes, in_specs=[VMEM] * (count + 1) +...  7.36 us
    ppermute x4, starting transfers between devices, add_crossed(): went[j] = lax.ppermute(sent, 'col', [(1, 0), (2, 3)])  5.16 us
  transfers between devices with their start and end apart: 23, of which 11 were waited for; matrix products, arithmetic and copies ran while one was open for 0% of the time, Pallas kernels for 11%

profile of v4, /device:TPU:0, one launch (start us, length us, event | category | flops | bytes accessed | tf_op | source)
XLA Modules:
  0.0 93.1 jit_solution(11615017988756726802)
XLA Ops:
  0.5 1.4 %copy-done.3 = bf16[160,5120]{1,0:T(8,128)(2,1)S(1)} copy-done((bf16[160,5120]{1,0:T(8,128)(2,1)S(1)}, bf16[160,5120]{1,0:T(8,128)(2,1)}, u32[]{:S(2)}) %copy-start.3) | copy-done | bytes 1638424
  2.0 2.6 %collective-permute-start.2 = (bf16[80,1280]{1,0:T(8,128)(2,1)S(1)}, bf16[80,1280]{1,0:T(8,128)(2,1)S(1)}, u32[]{:S(2)}, u32[]{:S(2)}) collective-permute-start(bf16[80,1280]{1,0:T(8,128)(2,1)S(1)} %get-tuple-element.73), channel_id=1, source_target_pairs={{0,1},{1,0},{2,3},{3,2},{4,5},{5,4},{6,7},{7,6},{8,9},{9,8},{10,11... | collective-permute-start | bytes 614408 | tf_op jit(solution)/shard_map/ppermute | solution.py:272
  4.7 2.5 %collective-permute-start.1 = (bf16[80,1280]{1,0:T(8,128)(2,1)S(1)}, bf16[80,1280]{1,0:T(8,128)(2,1)S(1)}, u32[]{:S(2)}, u32[]{:S(2)}) collective-permute-start(bf16[80,1280]{1,0:T(8,128)(2,1)S(1)} %get-tuple-element.72), channel_id=1, source_target_pairs={{0,3},{1,2},{2,1},{3,0},{4,6},{5,7},{6,4},{7,5},{8,11},{9,10},{10,... | collective-permute-start | bytes 614408 | tf_op jit(solution)/shard_map/ppermute | solution.py:338
  7.1 1.9 %copy-done = bf16[1280,1280]{1,0:T(8,128)(2,1)S(1)} copy-done((bf16[1280,1280]{1,0:T(8,128)(2,1)S(1)}, bf16[1280,1280]{1,0:T(8,128)(2,1)}, u32[]{:S(2)}) %copy-start) | copy-done | bytes 3276824
  9.1 0.7 shard_map.56
  9.8 2.7 %collective-permute-start.5 = (bf16[160,1280]{1,0:T(8,128)(2,1)S(1)}, bf16[160,1280]{1,0:T(8,128)(2,1)S(1)}, u32[]{:S(2)}, u32[]{:S(2)}) collective-permute-start(bf16[160,1280]{1,0:T(8,128)(2,1)S(1)} %get-tuple-element.81), channel_id=1, source_target_pairs={{0,1},{3,2},{4,5},{7,6},{8,9},{11,10},{12,13},{15,14},{16,17},{19,... | collective-permute-start | bytes 1228808 | tf_op jit(solution)/shard_map/ppermute | solution.py:308
  12.9 4.5 %collective-permute-done.1.refs_0_ = bf16[80,1280]{1,0:T(8,128)(2,1)S(1)} collective-permute-done((bf16[80,1280]{1,0:T(8,128)(2,1)S(1)}, bf16[80,1280]{1,0:T(8,128)(2,1)S(1)}, u32[]{:S(2)}, u32[]{:S(2)}) %collective-permute-start.1) | collective-permute-done | bytes 204832 | tf_op jit(solution)/shard_map/ppermute | solution.py:338
  17.4 1.6 %collective-permute-start.3 = (bf16[80,1280]{1,0:T(8,128)(2,1)S(1)}, bf16[80,1280]{1,0:T(8,128)(2,1)S(1)}, u32[]{:S(2)}, u32[]{:S(2)}) collective-permute-start(bf16[80,1280]{1,0:T(8,128)(2,1)S(1)} %get-tuple-element.76.refs_0_), channel_id=1, source_target_pairs={{0,8},{4,12},{8,0},{12,4},{1,9},{5,13},{9,1},{13,5},{2,10},{6,14},... | collective-permute-start | bytes 614408 | tf_op jit(solution)/shard_map/ppermute | solution.py:272
  19.0 0.8 shard_map.60
  19.8 3.1 %collective-permute-done.5.refs_1_ = bf16[160,1280]{1,0:T(8,128)(2,1)S(1)} collective-permute-done((bf16[160,1280]{1,0:T(8,128)(2,1)S(1)}, bf16[160,1280]{1,0:T(8,128)(2,1)S(1)}, u32[]{:S(2)}, u32[]{:S(2)}) %collective-permute-start.5) | collective-permute-done | bytes 409632 | tf_op jit(solution)/shard_map/ppermute | solution.py:308
  23.4 1.6 %collective-permute-start.7 = (bf16[160,2560]{1,0:T(8,128)(2,1)S(1)}, bf16[160,2560]{1,0:T(8,128)(2,1)S(1)}, u32[]{:S(2)}, u32[]{:S(2)}) collective-permute-start(bf16[160,2560]{1,0:T(8,128)(2,1)S(1)} %get-tuple-element.88), channel_id=1, source_target_pairs={{0,8},{4,12},{8,0},{12,4},{1,9},{5,13},{9,1},{13,5},{2,10},{6,14},... | collective-permute-start | bytes 2457608 | tf_op jit(solution)/shard_map/ppermute | solution.py:272
  25.0 4.2 %collective-permute-start.9 = (bf16[160,1280]{1,0:T(8,128)(2,1)S(1)}, bf16[160,1280]{1,0:T(8,128)(2,1)S(1)}, u32[]{:S(2)}, u32[]{:S(2)}) collective-permute-start(bf16[160,1280]{1,0:T(8,128)(2,1)S(1)} %get-tuple-element.92), channel_id=1, source_target_pairs={{0,1},{3,2},{4,5},{7,6},{8,9},{11,10},{12,13},{15,14},{16,17},{19,... | collective-permute-start | bytes 1228808 | tf_op jit(solution)/shard_map/ppermute | solution.py:308
  29.2 1.3 %shard_map.63 = (f32[160,1280]{1,0:T(8,128)S(1)}, f32[160,1280]{1,0:T(8,128)S(1)}, bf16[160,1280]{1,0:T(8,128)(2,1)S(1)}, bf16[160,1280]{1,0:T(8,128)(2,1)S(1)}, f32[8,128]{1,0:T(8,128)S(1)}) custom-call(bf16[160,1280]{1,0:T(8,128)(2,1)S(1)} %get-tuple-element.84.refs_0_, bf16[160,1280]{1,0:T(8,128)(2,1)S(1)} %collective-permute-done.6.refs_1_, ...), custom_call_target="tpu_custom_call" | custom-call | tf_op jit(solution)/shard_map/pallas_call | solution.py:142
  30.5 2.8 %collective-permute-start.11 = (bf16[160,1280]{1,0:T(8,128)(2,1)S(1)}, bf16[160,1280]{1,0:T(8,128)(2,1)S(1)}, u32[]{:S(2)}, u32[]{:S(2)}) collective-permute-start(bf16[160,1280]{1,0:T(8,128)(2,1)S(1)} %get-tuple-element.98), channel_id=1, source_target_pairs={{0,1},{3,2},{4,5},{7,6},{8,9},{11,10},{12,13},{15,14},{16,17},{19,... | collective-permute-start | bytes 1228808 | tf_op jit(solution)/shard_map/ppermute | solution.py:308
  33.4 1.2 %shard_map.64 = (f32[160,1280]{1,0:T(8,128)S(1)}, bf16[160,1280]{1,0:T(8,128)(2,1)S(1)}, f32[8,128]{1,0:T(8,128)S(1)}) custom-call(bf16[160,2560]{1,0:T(8,128)(2,1)S(1)} %get-tuple-element.71.refs_0_, bf16[1280,1280]{1,0:T(8,128)(2,1)S(1)} %copy-done.2, bf16[1280,1280]{1,0:T(8,128)(2,1)S(1)} %collective-permute-done.refs_5_.refs_2_, ...), custom_call_target="tpu_custom_call" | custom-call | tf_op jit(solution)/shard_map/pallas_call | solution.py:142
  34.6 4.3 %collective-permute-done.9.refs_1_ = bf16[160,1280]{1,0:T(8,128)(2,1)S(1)} collective-permute-done((bf16[160,1280]{1,0:T(8,128)(2,1)S(1)}, bf16[160,1280]{1,0:T(8,128)(2,1)S(1)}, u32[]{:S(2)}, u32[]{:S(2)}) %collective-permute-start.9) | collective-permute-done | bytes 409632 | tf_op jit(solution)/shard_map/ppermute | solution.py:308
  39.8 5.9 %collective-permute-start.13 = (bf16[160,1280]{1,0:T(8,128)(2,1)S(1)}, bf16[160,1280]{1,0:T(8,128)(2,1)S(1)}, u32[]{:S(2)}, u32[]{:S(2)}) collective-permute-start(bf16[160,1280]{1,0:T(8,128)(2,1)S(1)} %get-tuple-element.101), channel_id=1, source_target_pairs={{0,1},{3,2},{4,5},{7,6},{8,9},{11,10},{12,13},{15,14},{16,17},{19,... | collective-permute-start | bytes 1228808 | tf_op jit(solution)/shard_map/ppermute | solution.py:308
  45.8 1.3 %collective-permute-start.16 = (bf16[160,1280]{1,0:T(8,128)(2,1)S(1)}, bf16[160,1280]{1,0:T(8,128)(2,1)S(1)}, u32[]{:S(2)}, u32[]{:S(2)}) collective-permute-start(bf16[160,1280]{1,0:T(8,128)(2,1)S(1)} %get-tuple-element.109), channel_id=1, source_target_pairs={{1,0},{2,3},{5,4},{6,7},{9,8},{10,11},{13,12},{14,15},{17,16},{18,... | collective-permute-start | bytes 1228808 | tf_op jit(solution)/shard_map/ppermute | solution.py:297
  47.1 1.2 %shard_map.67 = (f32[160,1280]{1,0:T(8,128)S(1)}, bf16[160,1280]{1,0:T(8,128)(2,1)S(1)}, f32[8,128]{1,0:T(8,128)S(1)}) custom-call(bf16[160,2560]{1,0:T(8,128)(2,1)S(1)} %collective-permute-done.7.refs_0_, bf16[1280,1280]{1,0:T(8,128)(2,1)S(1)} %copy-done.2, bf16[1280,1280]{1,0:T(8,128)(2,1)S(1)} %collective-permute-done.refs_5_.refs_2_, ...), custom_call_target="tpu_custom_call" | custom-call | tf_op jit(solution)/shard_map/pallas_call | solution.py:142
  48.6 1.6 %collective-permute-start.10 = (bf16[160,1280]{1,0:T(8,128)(2,1)S(1)}, bf16[160,1280]{1,0:T(8,128)(2,1)S(1)}, u32[]{:S(2)}, u32[]{:S(2)}) collective-permute-start(bf16[160,1280]{1,0:T(8,128)(2,1)S(1)} %get-tuple-element.96), channel_id=1, source_target_pairs={{0,8},{4,12},{8,0},{12,4},{1,9},{5,13},{9,1},{13,5},{2,10},{6,14},... | collective-permute-start | bytes 1228808 | tf_op jit(solution)/shard_map/ppermute | solution.py:272
  50.2 3.1 %collective-permute-done.14.refs_1_ = bf16[160,1280]{1,0:T(8,128)(2,1)S(1)} collective-permute-done((bf16[160,1280]{1,0:T(8,128)(2,1)S(1)}, bf16[160,1280]{1,0:T(8,128)(2,1)S(1)}, u32[]{:S(2)}, u32[]{:S(2)}) %collective-permute-start.14) | collective-permute-done | bytes 409632 | tf_op jit(solution)/shard_map/ppermute | solution.py:272
  53.3 1.3 %collective-permute-start.20 = (bf16[160,1280]{1,0:T(8,128)(2,1)S(1)}, bf16[160,1280]{1,0:T(8,128)(2,1)S(1)}, u32[]{:S(2)}, u32[]{:S(2)}) collective-permute-start(bf16[160,1280]{1,0:T(8,128)(2,1)S(1)} %get-tuple-element.117), channel_id=1, source_target_pairs={{1,0},{2,3},{5,4},{6,7},{9,8},{10,11},{13,12},{14,15},{17,16},{18,... | collective-permute-start | bytes 1228808 | tf_op jit(solution)/shard_map/ppermute | solution.py:297
  54.7 1.0 %collective-permute-done.13.refs_1_ = bf16[160,1280]{1,0:T(8,128)(2,1)S(1)} collective-permute-done((bf16[160,1280]{1,0:T(8,128)(2,1)S(1)}, bf16[160,1280]{1,0:T(8,128)(2,1)S(1)}, u32[]{:S(2)}, u32[]{:S(2)}) %collective-permute-start.13) | collective-permute-done | bytes 409632 | tf_op jit(solution)/shard_map/ppermute | solution.py:308
  55.9 1.0 %collective-permute-done.16.refs_2_ = bf16[160,1280]{1,0:T(8,128)(2,1)S(1)} collective-permute-done((bf16[160,1280]{1,0:T(8,128)(2,1)S(1)}, bf16[160,1280]{1,0:T(8,128)(2,1)S(1)}, u32[]{:S(2)}, u32[]{:S(2)}) %collective-permute-start.16) | collective-permute-done | bytes 409632 | tf_op jit(solution)/shard_map/ppermute | solution.py:297
  57.2 4.4 %collective-permute-done.10.refs_1_ = bf16[160,1280]{1,0:T(8,128)(2,1)S(1)} collective-permute-done((bf16[160,1280]{1,0:T(8,128)(2,1)S(1)}, bf16[160,1280]{1,0:T(8,128)(2,1)S(1)}, u32[]{:S(2)}, u32[]{:S(2)}) %collective-permute-start.10) | collective-permute-done | bytes 409632 | tf_op jit(solution)/shard_map/ppermute | solution.py:272
  61.8 1.3 %collective-permute-start.21 = (bf16[160,1280]{1,0:T(8,128)(2,1)S(1)}, bf16[160,1280]{1,0:T(8,128)(2,1)S(1)}, u32[]{:S(2)}, u32[]{:S(2)}) collective-permute-start(bf16[160,1280]{1,0:T(8,128)(2,1)S(1)} %get-tuple-element.124), channel_id=1, source_target_pairs={{1,0},{2,3},{5,4},{6,7},{9,8},{10,11},{13,12},{14,15},{17,16},{18,... | collective-permute-start | bytes 1228808 | tf_op jit(solution)/shard_map/ppermute | solution.py:297
  63.1 2.7 %collective-permute-done.20.refs_2_ = bf16[160,1280]{1,0:T(8,128)(2,1)S(1)} collective-permute-done((bf16[160,1280]{1,0:T(8,128)(2,1)S(1)}, bf16[160,1280]{1,0:T(8,128)(2,1)S(1)}, u32[]{:S(2)}, u32[]{:S(2)}) %collective-permute-start.20) | collective-permute-done | bytes 409632 | tf_op jit(solution)/shard_map/ppermute | solution.py:297
  66.0 1.3 %collective-permute-start.22 = (bf16[160,1280]{1,0:T(8,128)(2,1)S(1)}, bf16[160,1280]{1,0:T(8,128)(2,1)S(1)}, u32[]{:S(2)}, u32[]{:S(2)}) collective-permute-start(bf16[160,1280]{1,0:T(8,128)(2,1)S(1)} %get-tuple-element.130), channel_id=1, source_target_pairs={{1,0},{2,3},{5,4},{6,7},{9,8},{10,11},{13,12},{14,15},{17,16},{18,... | collective-permute-start | bytes 1228808 | tf_op jit(solution)/shard_map/ppermute | solution.py:297
  67.3 2.3 %shard_map.77 = (bf16[4,1280,512]{2,1,0:T(8,128)(2,1)S(1)}, s32[8]{0:T(128)S(1)}, f32[8,128]{1,0:T(8,128)S(1)}) custom-call(s32[5,128]{1,0:T(8,128)S(1)} %bitcast.1, bf16[160,1280]{1,0:T(8,128)(2,1)S(1)} %get-tuple-element.113.own, bf16[160,1280]{1,0:T(8,128)(2,1)S(1)} %get-tuple-element.114.other_chip, ...), custom_call_target="tpu_custom_call" | custom-call | tf_op jit(solution)/shard_map/pallas_call | solution.py:195
  69.6 6.3 %collective-permute-done.21.refs_2_ = bf16[160,1280]{1,0:T(8,128)(2,1)S(1)} collective-permute-done((bf16[160,1280]{1,0:T(8,128)(2,1)S(1)}, bf16[160,1280]{1,0:T(8,128)(2,1)S(1)}, u32[]{:S(2)}, u32[]{:S(2)}) %collective-permute-start.21) | collective-permute-done | bytes 409632 | tf_op jit(solution)/shard_map/ppermute | solution.py:297
  76.6 7.7 %collective-permute-done.22.outward = bf16[160,1280]{1,0:T(8,128)(2,1)S(1)} collective-permute-done((bf16[160,1280]{1,0:T(8,128)(2,1)S(1)}, bf16[160,1280]{1,0:T(8,128)(2,1)S(1)}, u32[]{:S(2)}, u32[]{:S(2)}) %collective-permute-start.22) | collective-permute-done | bytes 409632 | tf_op jit(solution)/shard_map/ppermute | solution.py:297
  84.3 8.6 %shard_map.79 = f32[1280,1280]{1,0:T(8,128)} custom-call(s32[8]{0:T(128)S(1)} %get-tuple-element.121.place, bf16[4,1280,512]{2,1,0:T(8,128)(2,1)S(1)} %get-tuple-element.122.turned, bf16[160,1280]{1,0:T(8,128)(2,1)S(1)} %get-tuple-element.126.one, bf16[160,1280]{1,0:T(8,128)(2,1)S(1)} %get-tuple-element.127.two, ...), custom_call_target="tpu_custom_call" | custom-call | tf_op jit(solution)/shard_map/pallas_call | solution.py:257
  (51 shorter events, 4.3 us)
Async XLA Ops:
  0.0 19.0 %collective-permute-start = (bf16[1280,1280]{1,0:T(8,128)(2,1)}, bf16[1280,1280]{1,0:T(8,128)(2,1)S(1)}, u32[]{:S(2)}, u32[]{:S(2)}) collective-permute-start(bf16[1280,1280]{1,0:T(8,128)(2,1)} %refs_1_.5), channel_id=1, source_target_pairs={{0,4},{4,0},{8,12},{12,8},{1,5},{5,1},{9,13},{13,9},{2,6},{6,2},{1... | collective-permute-start | bytes 9830408 | tf_op jit(solution)/shard_map/ppermute | solution.py:272
  0.5 1.4 %copy-start.3 = (bf16[160,5120]{1,0:T(8,128)(2,1)S(1)}, bf16[160,5120]{1,0:T(8,128)(2,1)}, u32[]{:S(2)}) copy-start(bf16[160,5120]{1,0:T(8,128)(2,1)} %grad.1) | copy-start | bytes 4915204
  1.9 10.7 %copy-start.4 = (bf16[160,5120]{1,0:T(8,128)(2,1)S(1)}, bf16[160,5120]{1,0:T(8,128)(2,1)}, u32[]{:S(2)}) copy-start(bf16[160,5120]{1,0:T(8,128)(2,1)} %act.1) | copy-start | bytes 4915204
  2.0 10.7 %collective-permute-start.2 = (bf16[80,1280]{1,0:T(8,128)(2,1)S(1)}, bf16[80,1280]{1,0:T(8,128)(2,1)S(1)}, u32[]{:S(2)}, u32[]{:S(2)}) collective-permute-start(bf16[80,1280]{1,0:T(8,128)(2,1)S(1)} %get-tuple-element.73), channel_id=1, source_target_pairs={{0,1},{1,0},{2,3},{3,2},{4,5},{5,4},{6,7},{7,6},{8,9},{9,8},{10,11... | collective-permute-start | bytes 614408 | tf_op jit(solution)/shard_map/ppermute | solution.py:272
  4.7 12.8 %collective-permute-start.1 = (bf16[80,1280]{1,0:T(8,128)(2,1)S(1)}, bf16[80,1280]{1,0:T(8,128)(2,1)S(1)}, u32[]{:S(2)}, u32[]{:S(2)}) collective-permute-start(bf16[80,1280]{1,0:T(8,128)(2,1)S(1)} %get-tuple-element.72), channel_id=1, source_target_pairs={{0,3},{1,2},{2,1},{3,0},{4,6},{5,7},{6,4},{7,5},{8,11},{9,10},{10,... | collective-permute-start | bytes 614408 | tf_op jit(solution)/shard_map/ppermute | solution.py:338
  7.1 1.9 %copy-start = (bf16[1280,1280]{1,0:T(8,128)(2,1)S(1)}, bf16[1280,1280]{1,0:T(8,128)(2,1)}, u32[]{:S(2)}) copy-start(bf16[1280,1280]{1,0:T(8,128)(2,1)} %refs_2_.1) | copy-start | bytes 9830404
  9.1 9.9 %copy-start.1 = (bf16[1280,1280]{1,0:T(8,128)(2,1)S(1)}, bf16[1280,1280]{1,0:T(8,128)(2,1)}, u32[]{:S(2)}) copy-start(bf16[1280,1280]{1,0:T(8,128)(2,1)} %refs_2_.1) | copy-start | bytes 9830404
  9.8 13.1 %collective-permute-start.5 = (bf16[160,1280]{1,0:T(8,128)(2,1)S(1)}, bf16[160,1280]{1,0:T(8,128)(2,1)S(1)}, u32[]{:S(2)}, u32[]{:S(2)}) collective-permute-start(bf16[160,1280]{1,0:T(8,128)(2,1)S(1)} %get-tuple-element.81), channel_id=1, source_target_pairs={{0,1},{3,2},{4,5},{7,6},{8,9},{11,10},{12,13},{15,14},{16,17},{19,... | collective-permute-start | bytes 1228808 | tf_op jit(solution)/shard_map/ppermute | solution.py:308
  12.8 6.2 %collective-permute-start.4 = (bf16[80,1280]{1,0:T(8,128)(2,1)S(1)}, bf16[80,1280]{1,0:T(8,128)(2,1)S(1)}, u32[]{:S(2)}, u32[]{:S(2)}) collective-permute-start(bf16[80,1280]{1,0:T(8,128)(2,1)S(1)} %get-tuple-element.77.refs_0_), channel_id=1, source_target_pairs={{0,4},{4,0},{8,12},{12,8},{1,5},{5,1},{9,13},{13,9},{2,6},{6,2},{1... | collective-permute-start | bytes 614408 | tf_op jit(solution)/shard_map/ppermute | solution.py:272
  17.4 5.8 %collective-permute-start.3 = (bf16[80,1280]{1,0:T(8,128)(2,1)S(1)}, bf16[80,1280]{1,0:T(8,128)(2,1)S(1)}, u32[]{:S(2)}, u32[]{:S(2)}) collective-permute-start(bf16[80,1280]{1,0:T(8,128)(2,1)S(1)} %get-tuple-element.76.refs_0_), channel_id=1, source_target_pairs={{0,8},{4,12},{8,0},{12,4},{1,9},{5,13},{9,1},{13,5},{2,10},{6,14},... | collective-permute-start | bytes 614408 | tf_op jit(solution)/shard_map/ppermute | solution.py:272
  19.8 13.6 %copy-start.2 = (bf16[1280,1280]{1,0:T(8,128)(2,1)S(1)}, bf16[1280,1280]{1,0:T(8,128)(2,1)}, u32[]{:S(2)}) copy-start(bf16[1280,1280]{1,0:T(8,128)(2,1)} %refs_1_.5) | copy-start | bytes 9830404
  23.3 5.9 %collective-permute-start.6 = (bf16[160,1280]{1,0:T(8,128)(2,1)S(1)}, bf16[160,1280]{1,0:T(8,128)(2,1)S(1)}, u32[]{:S(2)}, u32[]{:S(2)}) collective-permute-start(bf16[160,1280]{1,0:T(8,128)(2,1)S(1)} %get-tuple-element.84.refs_0_), channel_id=1, source_target_pairs={{0,4},{4,0},{8,12},{12,8},{1,5},{5,1},{9,13},{13,9},{2,6},{6,2},{1... | collective-permute-start | bytes 1228808 | tf_op jit(solution)/shard_map/ppermute | solution.py:272
  23.4 22.4 %collective-permute-start.7 = (bf16[160,2560]{1,0:T(8,128)(2,1)S(1)}, bf16[160,2560]{1,0:T(8,128)(2,1)S(1)}, u32[]{:S(2)}, u32[]{:S(2)}) collective-permute-start(bf16[160,2560]{1,0:T(8,128)(2,1)S(1)} %get-tuple-element.88), channel_id=1, source_target_pairs={{0,8},{4,12},{8,0},{12,4},{1,9},{5,13},{9,1},{13,5},{2,10},{6,14},... | collective-permute-start | bytes 2457608 | tf_op jit(solution)/shard_map/ppermute | solution.py:272
  25.0 14.0 %collective-permute-start.9 = (bf16[160,1280]{1,0:T(8,128)(2,1)S(1)}, bf16[160,1280]{1,0:T(8,128)(2,1)S(1)}, u32[]{:S(2)}, u32[]{:S(2)}) collective-permute-start(bf16[160,1280]{1,0:T(8,128)(2,1)S(1)} %get-tuple-element.92), channel_id=1, source_target_pairs={{0,1},{3,2},{4,5},{7,6},{8,9},{11,10},{12,13},{15,14},{16,17},{19,... | collective-permute-start | bytes 1228808 | tf_op jit(solution)/shard_map/ppermute | solution.py:308
  29.1 10.6 %collective-permute-start.8 = (bf16[160,1280]{1,0:T(8,128)(2,1)S(1)}, bf16[160,1280]{1,0:T(8,128)(2,1)S(1)}, u32[]{:S(2)}, u32[]{:S(2)}) collective-permute-start(bf16[160,1280]{1,0:T(8,128)(2,1)S(1)} %get-tuple-element.90), channel_id=1, source_target_pairs={{0,4},{1,2},{2,1},{3,7},{4,0},{5,6},{6,5},{7,3},{8,12},{9,10},{10,... | collective-permute-start | bytes 1228808 | tf_op jit(solution)/shard_map/ppermute | solution.py:289
  30.5 17.8 %collective-permute-start.11 = (bf16[160,1280]{1,0:T(8,128)(2,1)S(1)}, bf16[160,1280]{1,0:T(8,128)(2,1)S(1)}, u32[]{:S(2)}, u32[]{:S(2)}) collective-permute-start(bf16[160,1280]{1,0:T(8,128)(2,1)S(1)} %get-tuple-element.98), channel_id=1, source_target_pairs={{0,1},{3,2},{4,5},{7,6},{8,9},{11,10},{12,13},{15,14},{16,17},{19,... | collective-permute-start | bytes 1228808 | tf_op jit(solution)/shard_map/ppermute | solution.py:308
  39.1 9.5 %collective-permute-start.15 = (bf16[160,1280]{1,0:T(8,128)(2,1)S(1)}, bf16[160,1280]{1,0:T(8,128)(2,1)S(1)}, u32[]{:S(2)}, u32[]{:S(2)}) collective-permute-start(bf16[160,1280]{1,0:T(8,128)(2,1)S(1)} %get-tuple-element.104), channel_id=1, source_target_pairs={{0,4},{1,2},{2,1},{3,7},{4,0},{5,6},{6,5},{7,3},{8,12},{9,10},{10,... | collective-permute-start | bytes 1228808 | tf_op jit(solution)/shard_map/ppermute | solution.py:289
  39.2 14.1 %collective-permute-start.14 = (bf16[160,1280]{1,0:T(8,128)(2,1)S(1)}, bf16[160,1280]{1,0:T(8,128)(2,1)S(1)}, u32[]{:S(2)}, u32[]{:S(2)}) collective-permute-start(bf16[160,1280]{1,0:T(8,128)(2,1)S(1)} %get-tuple-element.103), channel_id=1, source_target_pairs={{0,8},{4,12},{8,0},{12,4},{1,9},{5,13},{9,1},{13,5},{2,10},{6,14},... | collective-permute-start | bytes 1228808 | tf_op jit(solution)/shard_map/ppermute | solution.py:272
  39.8 16.0 %collective-permute-start.13 = (bf16[160,1280]{1,0:T(8,128)(2,1)S(1)}, bf16[160,1280]{1,0:T(8,128)(2,1)S(1)}, u32[]{:S(2)}, u32[]{:S(2)}) collective-permute-start(bf16[160,1280]{1,0:T(8,128)(2,1)S(1)} %get-tuple-element.101), channel_id=1, source_target_pairs={{0,1},{3,2},{4,5},{7,6},{8,9},{11,10},{12,13},{15,14},{16,17},{19,... | collective-permute-start | bytes 1228808 | tf_op jit(solution)/shard_map/ppermute | solution.py:308
  45.8 11.2 %collective-permute-start.16 = (bf16[160,1280]{1,0:T(8,128)(2,1)S(1)}, bf16[160,1280]{1,0:T(8,128)(2,1)S(1)}, u32[]{:S(2)}, u32[]{:S(2)}) collective-permute-start(bf16[160,1280]{1,0:T(8,128)(2,1)S(1)} %get-tuple-element.109), channel_id=1, source_target_pairs={{1,0},{2,3},{5,4},{6,7},{9,8},{10,11},{13,12},{14,15},{17,16},{18,... | collective-permute-start | bytes 1228808 | tf_op jit(solution)/shard_map/ppermute | solution.py:297
  48.5 8.6 %collective-permute-start.12 = (bf16[160,1280]{1,0:T(8,128)(2,1)S(1)}, bf16[160,1280]{1,0:T(8,128)(2,1)S(1)}, u32[]{:S(2)}, u32[]{:S(2)}) collective-permute-start(bf16[160,1280]{1,0:T(8,128)(2,1)S(1)} %get-tuple-element.100), channel_id=1, source_target_pairs={{0,4},{1,2},{2,1},{3,7},{4,0},{5,6},{6,5},{7,3},{8,12},{9,10},{10,... | collective-permute-start | bytes 1228808 | tf_op jit(solution)/shard_map/ppermute | solution.py:289
  48.6 13.0 %collective-permute-start.10 = (bf16[160,1280]{1,0:T(8,128)(2,1)S(1)}, bf16[160,1280]{1,0:T(8,128)(2,1)S(1)}, u32[]{:S(2)}, u32[]{:S(2)}) collective-permute-start(bf16[160,1280]{1,0:T(8,128)(2,1)S(1)} %get-tuple-element.96), channel_id=1, source_target_pairs={{0,8},{4,12},{8,0},{12,4},{1,9},{5,13},{9,1},{13,5},{2,10},{6,14},... | collective-permute-start | bytes 1228808 | tf_op jit(solution)/shard_map/ppermute | solution.py:272
  53.3 12.5 %collective-permute-start.20 = (bf16[160,1280]{1,0:T(8,128)(2,1)S(1)}, bf16[160,1280]{1,0:T(8,128)(2,1)S(1)}, u32[]{:S(2)}, u32[]{:S(2)}) collective-permute-start(bf16[160,1280]{1,0:T(8,128)(2,1)S(1)} %get-tuple-element.117), channel_id=1, source_target_pairs={{1,0},{2,3},{5,4},{6,7},{9,8},{10,11},{13,12},{14,15},{17,16},{18,... | collective-permute-start | bytes 1228808 | tf_op jit(solution)/shard_map/ppermute | solution.py:297
  55.9 10.0 %collective-permute-start.19 = (bf16[160,1280]{1,0:T(8,128)(2,1)S(1)}, bf16[160,1280]{1,0:T(8,128)(2,1)S(1)}, u32[]{:S(2)}, u32[]{:S(2)}) collective-permute-start(bf16[160,1280]{1,0:T(8,128)(2,1)S(1)} %get-tuple-element.115), channel_id=1, source_target_pairs={{0,4},{1,2},{2,1},{3,7},{4,0},{5,6},{6,5},{7,3},{8,12},{9,10},{10,... | collective-permute-start | bytes 1228808 | tf_op jit(solution)/shard_map/ppermute | solution.py:289
  57.0 10.3 %collective-permute-start.18 = (bf16[160,1280]{1,0:T(8,128)(2,1)S(1)}, bf16[160,1280]{1,0:T(8,128)(2,1)S(1)}, u32[]{:S(2)}, u32[]{:S(2)}) collective-permute-start(bf16[160,1280]{1,0:T(8,128)(2,1)S(1)} %get-tuple-element.114.other_chip), channel_id=1, source_target_pairs={{0,4},{4,0},{8,12},{12,8},{1,5},{5,1},{9,13},{13,9},{2,6},{6,2},{1... | collective-permute-start | bytes 1228808 | tf_op jit(solution)/shard_map/ppermute | solution.py:272
  57.0 10.3 %copy-start.5 = (s32[640]{0:T(1024)S(1)}, s32[640]{0:T(1024)}, u32[]{:S(2)}) copy-start(s32[640]{0:T(1024)} %param.9) | copy-start | bytes 7684
  61.7 5.6 %collective-permute-start.17 = (bf16[160,1280]{1,0:T(8,128)(2,1)S(1)}, bf16[160,1280]{1,0:T(8,128)(2,1)S(1)}, u32[]{:S(2)}, u32[]{:S(2)}) collective-permute-start(bf16[160,1280]{1,0:T(8,128)(2,1)S(1)} %get-tuple-element.113.own), channel_id=1, source_target_pairs={{0,4},{4,0},{8,12},{12,8},{1,5},{5,1},{9,13},{13,9},{2,6},{6,2},{1... | collective-permute-start | bytes 1228808 | tf_op jit(solution)/shard_map/ppermute | solution.py:272
  61.8 14.2 %collective-permute-start.21 = (bf16[160,1280]{1,0:T(8,128)(2,1)S(1)}, bf16[160,1280]{1,0:T(8,128)(2,1)S(1)}, u32[]{:S(2)}, u32[]{:S(2)}) collective-permute-start(bf16[160,1280]{1,0:T(8,128)(2,1)S(1)} %get-tuple-element.124), channel_id=1, source_target_pairs={{1,0},{2,3},{5,4},{6,7},{9,8},{10,11},{13,12},{14,15},{17,16},{18,... | collective-permute-start | bytes 1228808 | tf_op jit(solution)/shard_map/ppermute | solution.py:297
  66.0 18.3 %collective-permute-start.22 = (bf16[160,1280]{1,0:T(8,128)(2,1)S(1)}, bf16[160,1280]{1,0:T(8,128)(2,1)S(1)}, u32[]{:S(2)}, u32[]{:S(2)}) collective-permute-start(bf16[160,1280]{1,0:T(8,128)(2,1)S(1)} %get-tuple-element.130), channel_id=1, source_target_pairs={{1,0},{2,3},{5,4},{6,7},{9,8},{10,11},{13,12},{14,15},{17,16},{18,... | collective-permute-start | bytes 1228808 | tf_op jit(solution)/shard_map/ppermute | solution.py:297

commit v5 on v4

--- a/solution.py
+++ b/solution.py
@@ -386,13 +386,13 @@
     far_other = by_xor(far, "row", 1)
     token = add_inward(3, token)
     late[3], token = finish(3, token)
-    token = add_crossed(2, token)
     near, token = step(add_there, [short], [near_sum, far_there], token)
     near_other = by_xor(near, "row", 1)
+    token = add_crossed(2, token)
     late[2], token = finish(2, token)
     token = add_crossed(3, token)
+    late[1], token = finish(1, token)
     turned, places, token = turn([near, far, near_other, far_other], seq_ids, token)
-    late[1], token = finish(1, token)
     return correct(turned, places, late[1:], known[0], crossed[3], went[3])
 
 

time: 93.4 us -> 93.5 us (level)
  transfers between devices with their start and end apart: 23 -> 23, of which waited for: 11 -> 11; matrix products, arithmetic and copies ran while one was open for 0% -> 0% of each run, Pallas kernels for 11% -> 10%
where the time goes in v5:
time: 93.5 us; the launch traced here: 93.2 us
  waiting for transfers between devices  38.6 us (41%)
  starting transfers between devices  32.7 us (35%)
  Pallas kernels  18 us (19%)
  local copies, waits for them, and re-layouts  3.37 us (4%)
    ppermute x4, waiting for transfers between devices, add_crossed(): went[j] = lax.ppermute(sent, 'col', [(1, 0), (2, 3)])  17.7 us
    ppermute x4, starting transfers between devices, inward(): return lax.ppermute(sent, 'col', [(0, 1), (3, 2)])  15.7 us
    ppermute x10, starting transfers between devices, by_xor(): return lax.ppermute(values, axis, [(i, i ^ bits) for i in range(4)])  9.12 us
    pallas_call x1, Pallas kernels, correct(): pl.pallas_call(kernel, out_shape=shaped(height, width, dtype=F32), in_spe...  8.64 us
    ppermute x4, waiting for transfers between devices, inward(): return lax.ppermute(sent, 'col', [(0, 1), (3, 2)])  8.48 us
    ppermute x10, waiting for transfers between devices, by_xor(): return lax.ppermute(values, axis, [(i, i ^ bits) for i in range(4)])  7.82 us
    pallas_call x21, Pallas kernels, step(): pl.pallas_call(kernel, out_shape=shapes, in_specs=[VMEM] * (count + 1) +...  6.73 us
    ppermute x4, starting transfers between devices, add_crossed(): went[j] = lax.ppermute(sent, 'col', [(1, 0), (2, 3)])  5.16 us
  transfers between devices with their start and end apart: 23, of which 11 were waited for; matrix products, arithmetic and copies ran while one was open for 0% of the time, Pallas kernels for 10%

profile of v5, /device:TPU:0, one launch (start us, length us, event | category | flops | bytes accessed | tf_op | source)
XLA Modules:
  0.0 93.2 jit_solution(16409141546406916873)
XLA Ops:
  0.5 1.4 %copy-done.3 = bf16[160,5120]{1,0:T(8,128)(2,1)S(1)} copy-done((bf16[160,5120]{1,0:T(8,128)(2,1)S(1)}, bf16[160,5120]{1,0:T(8,128)(2,1)}, u32[]{:S(2)}) %copy-start.3) | copy-done | bytes 1638424
  2.0 2.6 %collective-permute-start.2 = (bf16[80,1280]{1,0:T(8,128)(2,1)S(1)}, bf16[80,1280]{1,0:T(8,128)(2,1)S(1)}, u32[]{:S(2)}, u32[]{:S(2)}) collective-permute-start(bf16[80,1280]{1,0:T(8,128)(2,1)S(1)} %get-tuple-element.73), channel_id=1, source_target_pairs={{0,1},{1,0},{2,3},{3,2},{4,5},{5,4},{6,7},{7,6},{8,9},{9,8},{10,11... | collective-permute-start | bytes 614408 | tf_op jit(solution)/shard_map/ppermute | solution.py:272
  4.7 2.5 %collective-permute-start.1 = (bf16[80,1280]{1,0:T(8,128)(2,1)S(1)}, bf16[80,1280]{1,0:T(8,128)(2,1)S(1)}, u32[]{:S(2)}, u32[]{:S(2)}) collective-permute-start(bf16[80,1280]{1,0:T(8,128)(2,1)S(1)} %get-tuple-element.72), channel_id=1, source_target_pairs={{0,3},{1,2},{2,1},{3,0},{4,6},{5,7},{6,4},{7,5},{8,11},{9,10},{10,... | collective-permute-start | bytes 614408 | tf_op jit(solution)/shard_map/ppermute | solution.py:338
  7.1 1.9 %copy-done = bf16[1280,1280]{1,0:T(8,128)(2,1)S(1)} copy-done((bf16[1280,1280]{1,0:T(8,128)(2,1)S(1)}, bf16[1280,1280]{1,0:T(8,128)(2,1)}, u32[]{:S(2)}) %copy-start) | copy-done | bytes 3276824
  9.1 0.7 shard_map.56
  9.8 2.7 %collective-permute-start.5 = (bf16[160,1280]{1,0:T(8,128)(2,1)S(1)}, bf16[160,1280]{1,0:T(8,128)(2,1)S(1)}, u32[]{:S(2)}, u32[]{:S(2)}) collective-permute-start(bf16[160,1280]{1,0:T(8,128)(2,1)S(1)} %get-tuple-element.81), channel_id=1, source_target_pairs={{0,1},{3,2},{4,5},{7,6},{8,9},{11,10},{12,13},{15,14},{16,17},{19,... | collective-permute-start | bytes 1228808 | tf_op jit(solution)/shard_map/ppermute | solution.py:308
  12.9 4.5 %collective-permute-done.1.refs_0_ = bf16[80,1280]{1,0:T(8,128)(2,1)S(1)} collective-permute-done((bf16[80,1280]{1,0:T(8,128)(2,1)S(1)}, bf16[80,1280]{1,0:T(8,128)(2,1)S(1)}, u32[]{:S(2)}, u32[]{:S(2)}) %collective-permute-start.1) | collective-permute-done | bytes 204832 | tf_op jit(solution)/shard_map/ppermute | solution.py:338
  17.4 1.6 %collective-permute-start.3 = (bf16[80,1280]{1,0:T(8,128)(2,1)S(1)}, bf16[80,1280]{1,0:T(8,128)(2,1)S(1)}, u32[]{:S(2)}, u32[]{:S(2)}) collective-permute-start(bf16[80,1280]{1,0:T(8,128)(2,1)S(1)} %get-tuple-element.76.refs_0_), channel_id=1, source_target_pairs={{0,8},{4,12},{8,0},{12,4},{1,9},{5,13},{9,1},{13,5},{2,10},{6,14},... | collective-permute-start | bytes 614408 | tf_op jit(solution)/shard_map/ppermute | solution.py:272
  19.0 0.8 shard_map.60
  19.8 3.1 %collective-permute-done.5.refs_1_ = bf16[160,1280]{1,0:T(8,128)(2,1)S(1)} collective-permute-done((bf16[160,1280]{1,0:T(8,128)(2,1)S(1)}, bf16[160,1280]{1,0:T(8,128)(2,1)S(1)}, u32[]{:S(2)}, u32[]{:S(2)}) %collective-permute-start.5) | collective-permute-done | bytes 409632 | tf_op jit(solution)/shard_map/ppermute | solution.py:308
  23.4 1.6 %collective-permute-start.7 = (bf16[160,2560]{1,0:T(8,128)(2,1)S(1)}, bf16[160,2560]{1,0:T(8,128)(2,1)S(1)}, u32[]{:S(2)}, u32[]{:S(2)}) collective-permute-start(bf16[160,2560]{1,0:T(8,128)(2,1)S(1)} %get-tuple-element.88), channel_id=1, source_target_pairs={{0,8},{4,12},{8,0},{12,4},{1,9},{5,13},{9,1},{13,5},{2,10},{6,14},... | collective-permute-start | bytes 2457608 | tf_op jit(solution)/shard_map/ppermute | solution.py:272
  25.0 4.2 %collective-permute-start.9 = (bf16[160,1280]{1,0:T(8,128)(2,1)S(1)}, bf16[160,1280]{1,0:T(8,128)(2,1)S(1)}, u32[]{:S(2)}, u32[]{:S(2)}) collective-permute-start(bf16[160,1280]{1,0:T(8,128)(2,1)S(1)} %get-tuple-element.92), channel_id=1, source_target_pairs={{0,1},{3,2},{4,5},{7,6},{8,9},{11,10},{12,13},{15,14},{16,17},{19,... | collective-permute-start | bytes 1228808 | tf_op jit(solution)/shard_map/ppermute | solution.py:308
  29.2 1.3 %shard_map.63 = (f32[160,1280]{1,0:T(8,128)S(1)}, f32[160,1280]{1,0:T(8,128)S(1)}, bf16[160,1280]{1,0:T(8,128)(2,1)S(1)}, bf16[160,1280]{1,0:T(8,128)(2,1)S(1)}, f32[8,128]{1,0:T(8,128)S(1)}) custom-call(bf16[160,1280]{1,0:T(8,128)(2,1)S(1)} %get-tuple-element.84.refs_0_, bf16[160,1280]{1,0:T(8,128)(2,1)S(1)} %collective-permute-done.6.refs_1_, ...), custom_call_target="tpu_custom_call" | custom-call | tf_op jit(solution)/shard_map/pallas_call | solution.py:142
  30.5 2.8 %collective-permute-start.14 = (bf16[160,1280]{1,0:T(8,128)(2,1)S(1)}, bf16[160,1280]{1,0:T(8,128)(2,1)S(1)}, u32[]{:S(2)}, u32[]{:S(2)}) collective-permute-start(bf16[160,1280]{1,0:T(8,128)(2,1)S(1)} %get-tuple-element.102), channel_id=1, source_target_pairs={{0,1},{3,2},{4,5},{7,6},{8,9},{11,10},{12,13},{15,14},{16,17},{19,... | collective-permute-start | bytes 1228808 | tf_op jit(solution)/shard_map/ppermute | solution.py:308
  33.4 1.2 %shard_map.64 = (f32[160,1280]{1,0:T(8,128)S(1)}, bf16[160,1280]{1,0:T(8,128)(2,1)S(1)}, f32[8,128]{1,0:T(8,128)S(1)}) custom-call(bf16[160,2560]{1,0:T(8,128)(2,1)S(1)} %get-tuple-element.71.refs_0_, bf16[1280,1280]{1,0:T(8,128)(2,1)S(1)} %copy-done.2, bf16[1280,1280]{1,0:T(8,128)(2,1)S(1)} %collective-permute-done.refs_5_.refs_2_, ...), custom_call_target="tpu_custom_call" | custom-call | tf_op jit(solution)/shard_map/pallas_call | solution.py:142
  34.6 4.3 %collective-permute-done.9.refs_1_ = bf16[160,1280]{1,0:T(8,128)(2,1)S(1)} collective-permute-done((bf16[160,1280]{1,0:T(8,128)(2,1)S(1)}, bf16[160,1280]{1,0:T(8,128)(2,1)S(1)}, u32[]{:S(2)}, u32[]{:S(2)}) %collective-permute-start.9) | collective-permute-done | bytes 409632 | tf_op jit(solution)/shard_map/ppermute | solution.py:308
  39.8 5.9 %collective-permute-start.11 = (bf16[160,1280]{1,0:T(8,128)(2,1)S(1)}, bf16[160,1280]{1,0:T(8,128)(2,1)S(1)}, u32[]{:S(2)}, u32[]{:S(2)}) collective-permute-start(bf16[160,1280]{1,0:T(8,128)(2,1)S(1)} %get-tuple-element.97), channel_id=1, source_target_pairs={{0,1},{3,2},{4,5},{7,6},{8,9},{11,10},{12,13},{15,14},{16,17},{19,... | collective-permute-start | bytes 1228808 | tf_op jit(solution)/shard_map/ppermute | solution.py:308
  45.8 1.3 %collective-permute-start.15 = (bf16[160,1280]{1,0:T(8,128)(2,1)S(1)}, bf16[160,1280]{1,0:T(8,128)(2,1)S(1)}, u32[]{:S(2)}, u32[]{:S(2)}) collective-permute-start(bf16[160,1280]{1,0:T(8,128)(2,1)S(1)} %get-tuple-element.108), channel_id=1, source_target_pairs={{1,0},{2,3},{5,4},{6,7},{9,8},{10,11},{13,12},{14,15},{17,16},{18,... | collective-permute-start | bytes 1228808 | tf_op jit(solution)/shard_map/ppermute | solution.py:297
  47.1 1.2 %shard_map.67 = (f32[160,1280]{1,0:T(8,128)S(1)}, bf16[160,1280]{1,0:T(8,128)(2,1)S(1)}, f32[8,128]{1,0:T(8,128)S(1)}) custom-call(bf16[160,2560]{1,0:T(8,128)(2,1)S(1)} %collective-permute-done.7.refs_0_, bf16[1280,1280]{1,0:T(8,128)(2,1)S(1)} %copy-done.2, bf16[1280,1280]{1,0:T(8,128)(2,1)S(1)} %collective-permute-done.refs_5_.refs_2_, ...), custom_call_target="tpu_custom_call" | custom-call | tf_op jit(solution)/shard_map/pallas_call | solution.py:142
  48.3 1.6 %collective-permute-start.10 = (bf16[160,1280]{1,0:T(8,128)(2,1)S(1)}, bf16[160,1280]{1,0:T(8,128)(2,1)S(1)}, u32[]{:S(2)}, u32[]{:S(2)}) collective-permute-start(bf16[160,1280]{1,0:T(8,128)(2,1)S(1)} %get-tuple-element.96), channel_id=1, source_target_pairs={{0,8},{4,12},{8,0},{12,4},{1,9},{5,13},{9,1},{13,5},{2,10},{6,14},... | collective-permute-start | bytes 1228808 | tf_op jit(solution)/shard_map/ppermute | solution.py:272
  50.2 3.1 %collective-permute-done.12.refs_1_ = bf16[160,1280]{1,0:T(8,128)(2,1)S(1)} collective-permute-done((bf16[160,1280]{1,0:T(8,128)(2,1)S(1)}, bf16[160,1280]{1,0:T(8,128)(2,1)S(1)}, u32[]{:S(2)}, u32[]{:S(2)}) %collective-permute-start.12) | collective-permute-done | bytes 409632 | tf_op jit(solution)/shard_map/ppermute | solution.py:272
  53.3 1.3 %collective-permute-start.21 = (bf16[160,1280]{1,0:T(8,128)(2,1)S(1)}, bf16[160,1280]{1,0:T(8,128)(2,1)S(1)}, u32[]{:S(2)}, u32[]{:S(2)}) collective-permute-start(bf16[160,1280]{1,0:T(8,128)(2,1)S(1)} %get-tuple-element.119), channel_id=1, source_target_pairs={{1,0},{2,3},{5,4},{6,7},{9,8},{10,11},{13,12},{14,15},{17,16},{18,... | collective-permute-start | bytes 1228808 | tf_op jit(solution)/shard_map/ppermute | solution.py:297
  54.7 1.1 %collective-permute-done.11.refs_1_ = bf16[160,1280]{1,0:T(8,128)(2,1)S(1)} collective-permute-done((bf16[160,1280]{1,0:T(8,128)(2,1)S(1)}, bf16[160,1280]{1,0:T(8,128)(2,1)S(1)}, u32[]{:S(2)}, u32[]{:S(2)}) %collective-permute-start.11) | collective-permute-done | bytes 409632 | tf_op jit(solution)/shard_map/ppermute | solution.py:308
  55.9 1.0 %collective-permute-done.15.refs_2_ = bf16[160,1280]{1,0:T(8,128)(2,1)S(1)} collective-permute-done((bf16[160,1280]{1,0:T(8,128)(2,1)S(1)}, bf16[160,1280]{1,0:T(8,128)(2,1)S(1)}, u32[]{:S(2)}, u32[]{:S(2)}) %collective-permute-start.15) | collective-permute-done | bytes 409632 | tf_op jit(solution)/shard_map/ppermute | solution.py:297
  57.1 4.5 %collective-permute-done.10.refs_1_ = bf16[160,1280]{1,0:T(8,128)(2,1)S(1)} collective-permute-done((bf16[160,1280]{1,0:T(8,128)(2,1)S(1)}, bf16[160,1280]{1,0:T(8,128)(2,1)S(1)}, u32[]{:S(2)}, u32[]{:S(2)}) %collective-permute-start.10) | collective-permute-done | bytes 409632 | tf_op jit(solution)/shard_map/ppermute | solution.py:272
  61.9 1.3 %collective-permute-start.19 = (bf16[160,1280]{1,0:T(8,128)(2,1)S(1)}, bf16[160,1280]{1,0:T(8,128)(2,1)S(1)}, u32[]{:S(2)}, u32[]{:S(2)}) collective-permute-start(bf16[160,1280]{1,0:T(8,128)(2,1)S(1)} %get-tuple-element.116), channel_id=1, source_target_pairs={{1,0},{2,3},{5,4},{6,7},{9,8},{10,11},{13,12},{14,15},{17,16},{18,... | collective-permute-start | bytes 1228808 | tf_op jit(solution)/shard_map/ppermute | solution.py:297
  63.7 2.0 %collective-permute-done.21.refs_2_ = bf16[160,1280]{1,0:T(8,128)(2,1)S(1)} collective-permute-done((bf16[160,1280]{1,0:T(8,128)(2,1)S(1)}, bf16[160,1280]{1,0:T(8,128)(2,1)S(1)}, u32[]{:S(2)}, u32[]{:S(2)}) %collective-permute-start.21) | collective-permute-done | bytes 409632 | tf_op jit(solution)/shard_map/ppermute | solution.py:297
  65.9 1.3 %collective-permute-start.22 = (bf16[160,1280]{1,0:T(8,128)(2,1)S(1)}, bf16[160,1280]{1,0:T(8,128)(2,1)S(1)}, u32[]{:S(2)}, u32[]{:S(2)}) collective-permute-start(bf16[160,1280]{1,0:T(8,128)(2,1)S(1)} %get-tuple-element.130), channel_id=1, source_target_pairs={{1,0},{2,3},{5,4},{6,7},{9,8},{10,11},{13,12},{14,15},{17,16},{18,... | collective-permute-start | bytes 1228808 | tf_op jit(solution)/shard_map/ppermute | solution.py:297
  67.2 8.8 %collective-permute-done.19.refs_2_ = bf16[160,1280]{1,0:T(8,128)(2,1)S(1)} collective-permute-done((bf16[160,1280]{1,0:T(8,128)(2,1)S(1)}, bf16[160,1280]{1,0:T(8,128)(2,1)S(1)}, u32[]{:S(2)}, u32[]{:S(2)}) %collective-permute-start.19) | collective-permute-done | bytes 409632 | tf_op jit(solution)/shard_map/ppermute | solution.py:297
  76.2 2.3 %shard_map.78 = (bf16[4,1280,512]{2,1,0:T(8,128)(2,1)S(1)}, s32[8]{0:T(128)S(1)}, f32[8,128]{1,0:T(8,128)}) custom-call(s32[5,128]{1,0:T(8,128)S(1)} %bitcast.1, bf16[160,1280]{1,0:T(8,128)(2,1)S(1)} %get-tuple-element.111.own, bf16[160,1280]{1,0:T(8,128)(2,1)S(1)} %get-tuple-element.112.other_chip, ...), custom_call_target="tpu_custom_call" | custom-call | tf_op jit(solution)/shard_map/pallas_call | solution.py:195
  78.5 5.9 %collective-permute-done.22.outward = bf16[160,1280]{1,0:T(8,128)(2,1)S(1)} collective-permute-done((bf16[160,1280]{1,0:T(8,128)(2,1)S(1)}, bf16[160,1280]{1,0:T(8,128)(2,1)S(1)}, u32[]{:S(2)}, u32[]{:S(2)}) %collective-permute-start.22) | collective-permute-done | bytes 409632 | tf_op jit(solution)/shard_map/ppermute | solution.py:297
  84.4 8.6 %shard_map.79 = f32[1280,1280]{1,0:T(8,128)} custom-call(s32[8]{0:T(128)S(1)} %get-tuple-element.124.place, bf16[4,1280,512]{2,1,0:T(8,128)(2,1)S(1)} %get-tuple-element.125.turned, bf16[160,1280]{1,0:T(8,128)(2,1)S(1)} %get-tuple-element.126.one, bf16[160,1280]{1,0:T(8,128)(2,1)S(1)} %get-tuple-element.127.two, ...), custom_call_target="tpu_custom_call" | custom-call | tf_op jit(solution)/shard_map/pallas_call | solution.py:257
  (51 shorter events, 4.2 us)
Async XLA Ops:
  0.0 19.0 %collective-permute-start = (bf16[1280,1280]{1,0:T(8,128)(2,1)}, bf16[1280,1280]{1,0:T(8,128)(2,1)S(1)}, u32[]{:S(2)}, u32[]{:S(2)}) collective-permute-start(bf16[1280,1280]{1,0:T(8,128)(2,1)} %refs_1_.5), channel_id=1, source_target_pairs={{0,4},{4,0},{8,12},{12,8},{1,5},{5,1},{9,13},{13,9},{2,6},{6,2},{1... | collective-permute-start | bytes 9830408 | tf_op jit(solution)/shard_map/ppermute | solution.py:272
  0.5 1.4 %copy-start.3 = (bf16[160,5120]{1,0:T(8,128)(2,1)S(1)}, bf16[160,5120]{1,0:T(8,128)(2,1)}, u32[]{:S(2)}) copy-start(bf16[160,5120]{1,0:T(8,128)(2,1)} %grad.1) | copy-start | bytes 4915204
  1.9 10.7 %copy-start.4 = (bf16[160,5120]{1,0:T(8,128)(2,1)S(1)}, bf16[160,5120]{1,0:T(8,128)(2,1)}, u32[]{:S(2)}) copy-start(bf16[160,5120]{1,0:T(8,128)(2,1)} %act.1) | copy-start | bytes 4915204
  2.0 10.7 %collective-permute-start.2 = (bf16[80,1280]{1,0:T(8,128)(2,1)S(1)}, bf16[80,1280]{1,0:T(8,128)(2,1)S(1)}, u32[]{:S(2)}, u32[]{:S(2)}) collective-permute-start(bf16[80,1280]{1,0:T(8,128)(2,1)S(1)} %get-tuple-element.73), channel_id=1, source_target_pairs={{0,1},{1,0},{2,3},{3,2},{4,5},{5,4},{6,7},{7,6},{8,9},{9,8},{10,11... | collective-permute-start | bytes 614408 | tf_op jit(solution)/shard_map/ppermute | solution.py:272
  4.7 12.8 %collective-permute-start.1 = (bf16[80,1280]{1,0:T(8,128)(2,1)S(1)}, bf16[80,1280]{1,0:T(8,128)(2,1)S(1)}, u32[]{:S(2)}, u32[]{:S(2)}) collective-permute-start(bf16[80,1280]{1,0:T(8,128)(2,1)S(1)} %get-tuple-element.72), channel_id=1, source_target_pairs={{0,3},{1,2},{2,1},{3,0},{4,6},{5,7},{6,4},{7,5},{8,11},{9,10},{10,... | collective-permute-start | bytes 614408 | tf_op jit(solution)/shard_map/ppermute | solution.py:338
  7.1 1.9 %copy-start = (bf16[1280,1280]{1,0:T(8,128)(2,1)S(1)}, bf16[1280,1280]{1,0:T(8,128)(2,1)}, u32[]{:S(2)}) copy-start(bf16[1280,1280]{1,0:T(8,128)(2,1)} %refs_2_.1) | copy-start | bytes 9830404
  9.1 9.9 %copy-start.1 = (bf16[1280,1280]{1,0:T(8,128)(2,1)S(1)}, bf16[1280,1280]{1,0:T(8,128)(2,1)}, u32[]{:S(2)}) copy-start(bf16[1280,1280]{1,0:T(8,128)(2,1)} %refs_2_.1) | copy-start | bytes 9830404
  9.8 13.1 %collective-permute-start.5 = (bf16[160,1280]{1,0:T(8,128)(2,1)S(1)}, bf16[160,1280]{1,0:T(8,128)(2,1)S(1)}, u32[]{:S(2)}, u32[]{:S(2)}) collective-permute-start(bf16[160,1280]{1,0:T(8,128)(2,1)S(1)} %get-tuple-element.81), channel_id=1, source_target_pairs={{0,1},{3,2},{4,5},{7,6},{8,9},{11,10},{12,13},{15,14},{16,17},{19,... | collective-permute-start | bytes 1228808 | tf_op jit(solution)/shard_map/ppermute | solution.py:308
  12.8 6.2 %collective-permute-start.4 = (bf16[80,1280]{1,0:T(8,128)(2,1)S(1)}, bf16[80,1280]{1,0:T(8,128)(2,1)S(1)}, u32[]{:S(2)}, u32[]{:S(2)}) collective-permute-start(bf16[80,1280]{1,0:T(8,128)(2,1)S(1)} %get-tuple-element.77.refs_0_), channel_id=1, source_target_pairs={{0,4},{4,0},{8,12},{12,8},{1,5},{5,1},{9,13},{13,9},{2,6},{6,2},{1... | collective-permute-start | bytes 614408 | tf_op jit(solution)/shard_map/ppermute | solution.py:272
  17.4 5.8 %collective-permute-start.3 = (bf16[80,1280]{1,0:T(8,128)(2,1)S(1)}, bf16[80,1280]{1,0:T(8,128)(2,1)S(1)}, u32[]{:S(2)}, u32[]{:S(2)}) collective-permute-start(bf16[80,1280]{1,0:T(8,128)(2,1)S(1)} %get-tuple-element.76.refs_0_), channel_id=1, source_target_pairs={{0,8},{4,12},{8,0},{12,4},{1,9},{5,13},{9,1},{13,5},{2,10},{6,14},... | collective-permute-start | bytes 614408 | tf_op jit(solution)/shard_map/ppermute | solution.py:272
  19.8 13.6 %copy-start.2 = (bf16[1280,1280]{1,0:T(8,128)(2,1)S(1)}, bf16[1280,1280]{1,0:T(8,128)(2,1)}, u32[]{:S(2)}) copy-start(bf16[1280,1280]{1,0:T(8,128)(2,1)} %refs_1_.5) | copy-start | bytes 9830404
  23.3 5.9 %collective-permute-start.6 = (bf16[160,1280]{1,0:T(8,128)(2,1)S(1)}, bf16[160,1280]{1,0:T(8,128)(2,1)S(1)}, u32[]{:S(2)}, u32[]{:S(2)}) collective-permute-start(bf16[160,1280]{1,0:T(8,128)(2,1)S(1)} %get-tuple-element.84.refs_0_), channel_id=1, source_target_pairs={{0,4},{4,0},{8,12},{12,8},{1,5},{5,1},{9,13},{13,9},{2,6},{6,2},{1... | collective-permute-start | bytes 1228808 | tf_op jit(solution)/shard_map/ppermute | solution.py:272
  23.4 22.4 %collective-permute-start.7 = (bf16[160,2560]{1,0:T(8,128)(2,1)S(1)}, bf16[160,2560]{1,0:T(8,128)(2,1)S(1)}, u32[]{:S(2)}, u32[]{:S(2)}) collective-permute-start(bf16[160,2560]{1,0:T(8,128)(2,1)S(1)} %get-tuple-element.88), channel_id=1, source_target_pairs={{0,8},{4,12},{8,0},{12,4},{1,9},{5,13},{9,1},{13,5},{2,10},{6,14},... | collective-permute-start | bytes 2457608 | tf_op jit(solution)/shard_map/ppermute | solution.py:272
  25.0 14.0 %collective-permute-start.9 = (bf16[160,1280]{1,0:T(8,128)(2,1)S(1)}, bf16[160,1280]{1,0:T(8,128)(2,1)S(1)}, u32[]{:S(2)}, u32[]{:S(2)}) collective-permute-start(bf16[160,1280]{1,0:T(8,128)(2,1)S(1)} %get-tuple-element.92), channel_id=1, source_target_pairs={{0,1},{3,2},{4,5},{7,6},{8,9},{11,10},{12,13},{15,14},{16,17},{19,... | collective-permute-start | bytes 1228808 | tf_op jit(solution)/shard_map/ppermute | solution.py:308
  29.1 10.6 %collective-permute-start.8 = (bf16[160,1280]{1,0:T(8,128)(2,1)S(1)}, bf16[160,1280]{1,0:T(8,128)(2,1)S(1)}, u32[]{:S(2)}, u32[]{:S(2)}) collective-permute-start(bf16[160,1280]{1,0:T(8,128)(2,1)S(1)} %get-tuple-element.90), channel_id=1, source_target_pairs={{0,4},{1,2},{2,1},{3,7},{4,0},{5,6},{6,5},{7,3},{8,12},{9,10},{10,... | collective-permute-start | bytes 1228808 | tf_op jit(solution)/shard_map/ppermute | solution.py:289
  30.5 17.8 %collective-permute-start.14 = (bf16[160,1280]{1,0:T(8,128)(2,1)S(1)}, bf16[160,1280]{1,0:T(8,128)(2,1)S(1)}, u32[]{:S(2)}, u32[]{:S(2)}) collective-permute-start(bf16[160,1280]{1,0:T(8,128)(2,1)S(1)} %get-tuple-element.102), channel_id=1, source_target_pairs={{0,1},{3,2},{4,5},{7,6},{8,9},{11,10},{12,13},{15,14},{16,17},{19,... | collective-permute-start | bytes 1228808 | tf_op jit(solution)/shard_map/ppermute | solution.py:308
  39.1 11.0 %collective-permute-start.13 = (bf16[160,1280]{1,0:T(8,128)(2,1)S(1)}, bf16[160,1280]{1,0:T(8,128)(2,1)S(1)}, u32[]{:S(2)}, u32[]{:S(2)}) collective-permute-start(bf16[160,1280]{1,0:T(8,128)(2,1)S(1)} %get-tuple-element.101), channel_id=1, source_target_pairs={{0,4},{1,2},{2,1},{3,7},{4,0},{5,6},{6,5},{7,3},{8,12},{9,10},{10,... | collective-permute-start | bytes 1228808 | tf_op jit(solution)/shard_map/ppermute | solution.py:289
  39.2 14.1 %collective-permute-start.12 = (bf16[160,1280]{1,0:T(8,128)(2,1)S(1)}, bf16[160,1280]{1,0:T(8,128)(2,1)S(1)}, u32[]{:S(2)}, u32[]{:S(2)}) collective-permute-start(bf16[160,1280]{1,0:T(8,128)(2,1)S(1)} %get-tuple-element.99), channel_id=1, source_target_pairs={{0,8},{4,12},{8,0},{12,4},{1,9},{5,13},{9,1},{13,5},{2,10},{6,14},... | collective-permute-start | bytes 1228808 | tf_op jit(solution)/shard_map/ppermute | solution.py:272
  39.8 16.0 %collective-permute-start.11 = (bf16[160,1280]{1,0:T(8,128)(2,1)S(1)}, bf16[160,1280]{1,0:T(8,128)(2,1)S(1)}, u32[]{:S(2)}, u32[]{:S(2)}) collective-permute-start(bf16[160,1280]{1,0:T(8,128)(2,1)S(1)} %get-tuple-element.97), channel_id=1, source_target_pairs={{0,1},{3,2},{4,5},{7,6},{8,9},{11,10},{12,13},{15,14},{16,17},{19,... | collective-permute-start | bytes 1228808 | tf_op jit(solution)/shard_map/ppermute | solution.py:308
  45.8 11.2 %collective-permute-start.15 = (bf16[160,1280]{1,0:T(8,128)(2,1)S(1)}, bf16[160,1280]{1,0:T(8,128)(2,1)S(1)}, u32[]{:S(2)}, u32[]{:S(2)}) collective-permute-start(bf16[160,1280]{1,0:T(8,128)(2,1)S(1)} %get-tuple-element.108), channel_id=1, source_target_pairs={{1,0},{2,3},{5,4},{6,7},{9,8},{10,11},{13,12},{14,15},{17,16},{18,... | collective-permute-start | bytes 1228808 | tf_op jit(solution)/shard_map/ppermute | solution.py:297
  48.3 13.3 %collective-permute-start.10 = (bf16[160,1280]{1,0:T(8,128)(2,1)S(1)}, bf16[160,1280]{1,0:T(8,128)(2,1)S(1)}, u32[]{:S(2)}, u32[]{:S(2)}) collective-permute-start(bf16[160,1280]{1,0:T(8,128)(2,1)S(1)} %get-tuple-element.96), channel_id=1, source_target_pairs={{0,8},{4,12},{8,0},{12,4},{1,9},{5,13},{9,1},{13,5},{2,10},{6,14},... | collective-permute-start | bytes 1228808 | tf_op jit(solution)/shard_map/ppermute | solution.py:272
  50.1 11.7 %collective-permute-start.18 = (bf16[160,1280]{1,0:T(8,128)(2,1)S(1)}, bf16[160,1280]{1,0:T(8,128)(2,1)S(1)}, u32[]{:S(2)}, u32[]{:S(2)}) collective-permute-start(bf16[160,1280]{1,0:T(8,128)(2,1)S(1)} %get-tuple-element.114), channel_id=1, source_target_pairs={{0,4},{1,2},{2,1},{3,7},{4,0},{5,6},{6,5},{7,3},{8,12},{9,10},{10,... | collective-permute-start | bytes 1228808 | tf_op jit(solution)/shard_map/ppermute | solution.py:289
  53.3 12.5 %collective-permute-start.21 = (bf16[160,1280]{1,0:T(8,128)(2,1)S(1)}, bf16[160,1280]{1,0:T(8,128)(2,1)S(1)}, u32[]{:S(2)}, u32[]{:S(2)}) collective-permute-start(bf16[160,1280]{1,0:T(8,128)(2,1)S(1)} %get-tuple-element.119), channel_id=1, source_target_pairs={{1,0},{2,3},{5,4},{6,7},{9,8},{10,11},{13,12},{14,15},{17,16},{18,... | collective-permute-start | bytes 1228808 | tf_op jit(solution)/shard_map/ppermute | solution.py:297
  55.9 10.0 %collective-permute-start.20 = (bf16[160,1280]{1,0:T(8,128)(2,1)S(1)}, bf16[160,1280]{1,0:T(8,128)(2,1)S(1)}, u32[]{:S(2)}, u32[]{:S(2)}) collective-permute-start(bf16[160,1280]{1,0:T(8,128)(2,1)S(1)} %get-tuple-element.117), channel_id=1, source_target_pairs={{0,4},{1,2},{2,1},{3,7},{4,0},{5,6},{6,5},{7,3},{8,12},{9,10},{10,... | collective-permute-start | bytes 1228808 | tf_op jit(solution)/shard_map/ppermute | solution.py:289
  61.6 14.6 %copy-start.5 = (s32[640]{0:T(1024)S(1)}, s32[640]{0:T(1024)}, u32[]{:S(2)}) copy-start(s32[640]{0:T(1024)} %param.9) | copy-start | bytes 7684
  61.7 14.4 %collective-permute-start.16 = (bf16[160,1280]{1,0:T(8,128)(2,1)S(1)}, bf16[160,1280]{1,0:T(8,128)(2,1)S(1)}, u32[]{:S(2)}, u32[]{:S(2)}) collective-permute-start(bf16[160,1280]{1,0:T(8,128)(2,1)S(1)} %get-tuple-element.111.own), channel_id=1, source_target_pairs={{0,4},{4,0},{8,12},{12,8},{1,5},{5,1},{9,13},{13,9},{2,6},{6,2},{1... | collective-permute-start | bytes 1228808 | tf_op jit(solution)/shard_map/ppermute | solution.py:272
  61.9 14.2 %collective-permute-start.19 = (bf16[160,1280]{1,0:T(8,128)(2,1)S(1)}, bf16[160,1280]{1,0:T(8,128)(2,1)S(1)}, u32[]{:S(2)}, u32[]{:S(2)}) collective-permute-start(bf16[160,1280]{1,0:T(8,128)(2,1)S(1)} %get-tuple-element.116), channel_id=1, source_target_pairs={{1,0},{2,3},{5,4},{6,7},{9,8},{10,11},{13,12},{14,15},{17,16},{18,... | collective-permute-start | bytes 1228808 | tf_op jit(solution)/shard_map/ppermute | solution.py:297
  63.2 13.0 %collective-permute-start.17 = (bf16[160,1280]{1,0:T(8,128)(2,1)S(1)}, bf16[160,1280]{1,0:T(8,128)(2,1)S(1)}, u32[]{:S(2)}, u32[]{:S(2)}) collective-permute-start(bf16[160,1280]{1,0:T(8,128)(2,1)S(1)} %get-tuple-element.112.other_chip), channel_id=1, source_target_pairs={{0,4},{4,0},{8,12},{12,8},{1,5},{5,1},{9,13},{13,9},{2,6},{6,2},{1... | collective-permute-start | bytes 1228808 | tf_op jit(solution)/shard_map/ppermute | solution.py:272
  65.9 18.5 %collective-permute-start.22 = (bf16[160,1280]{1,0:T(8,128)(2,1)S(1)}, bf16[160,1280]{1,0:T(8,128)(2,1)S(1)}, u32[]{:S(2)}, u32[]{:S(2)}) collective-permute-start(bf16[160,1280]{1,0:T(8,128)(2,1)S(1)} %get-tuple-element.130), channel_id=1, source_target_pairs={{1,0},{2,3},{5,4},{6,7},{9,8},{10,11},{13,12},{14,15},{17,16},{18,... | collective-permute-start | bytes 1228808 | tf_op jit(solution)/shard_map/ppermute | solution.py:297

commit v6 on v5

--- a/solution.py
+++ b/solution.py
@@ -233,25 +233,27 @@
         def put(columns):
             return pltpu.make_async_copy(total.at[:, columns], out.at[:, columns], sems.at[3])
 
-        for seq in range(SEQS):
+        def add_sequence(seq, columns):
             start = pl.multiple_of(place[2 * seq], 16)
             is_wide = place[2 * seq + 1] == 1
-            last = seq == SEQS - 1
-            step = NARROW if last else width
-            for begin in range(0, width, step):
-                columns = slice(begin, begin + step)
-
-                def add(depth):
-                    part = dot(turned[seq, :, :depth], grad[pl.ds(start, depth), columns])
-                    part = part * part
-                    if seq:
-                        part = total[:, columns] + part
-                    total[:, columns] = part / SEQS if last else part
-
-                pl.when(is_wide)(functools.partial(add, wide))
-                pl.when(jnp.logical_not(is_wide))(functools.partial(add, NARROW))
-                if last:
-                    put(columns).start()
+
+            def add(depth):
+                part = dot(turned[seq, :, :depth], grad[pl.ds(start, depth), columns])
+                part = part * part
+                if seq:
+                    part = total[:, columns] + part
+                total[:, columns] = part / SEQS if seq == SEQS - 1 else part
+
+            pl.when(is_wide)(functools.partial(add, wide))
+            pl.when(jnp.logical_not(is_wide))(functools.partial(add, NARROW))
+
+        for seq in range(SEQS - 2):
+            add_sequence(seq, slice(0, width))
+        for begin in range(0, width, NARROW):
+            columns = slice(begin, begin + NARROW)
+            for seq in (SEQS - 2, SEQS - 1):
+                add_sequence(seq, columns)
+            put(columns).start()
         put(slice(0, width)).wait()
 
     return pl.pallas_call(

time: 93.5 us -> 93.9 us (level)
  no operation moved by 1% of the time
where the time goes in v6:
time: 93.9 us; the launch traced here: 93.5 us
  waiting for transfers between devices  38.6 us (41%)
  starting transfers between devices  32.7 us (35%)
  Pallas kernels  18.3 us (19%)
  local copies, waits for them, and re-layouts  3.37 us (4%)
    ppermute x4, waiting for transfers between devices, add_crossed(): went[j] = lax.ppermute(sent, 'col', [(1, 0), (2, 3)])  17.7 us
    ppermute x4, starting transfers between devices, inward(): return lax.ppermute(sent, 'col', [(0, 1), (3, 2)])  15.7 us
    ppermute x10, starting transfers between devices, by_xor(): return lax.ppermute(values, axis, [(i, i ^ bits) for i in range(4)])  9.12 us
    pallas_call x1, Pallas kernels, correct(): pl.pallas_call(kernel, out_shape=shaped(height, width, dtype=F32), in_spe...  8.94 us
    ppermute x4, waiting for transfers between devices, inward(): return lax.ppermute(sent, 'col', [(0, 1), (3, 2)])  8.48 us
    ppermute x10, waiting for transfers between devices, by_xor(): return lax.ppermute(values, axis, [(i, i ^ bits) for i in range(4)])  7.82 us
    pallas_call x21, Pallas kernels, step(): pl.pallas_call(kernel, out_shape=shapes, in_specs=[VMEM] * (count + 1) +...  6.73 us
    ppermute x4, starting transfers between devices, add_crossed(): went[j] = lax.ppermute(sent, 'col', [(1, 0), (2, 3)])  5.16 us
  transfers between devices with their start and end apart: 23, of which 11 were waited for; matrix products, arithmetic and copies ran while one was open for 0% of the time, Pallas kernels for 10%

profile of v6, /device:TPU:0, one launch (start us, length us, event | category | flops | bytes accessed | tf_op | source)
XLA Modules:
  0.0 93.5 jit_solution(5849153203804376096)
XLA Ops:
  0.5 1.4 %copy-done.3 = bf16[160,5120]{1,0:T(8,128)(2,1)S(1)} copy-done((bf16[160,5120]{1,0:T(8,128)(2,1)S(1)}, bf16[160,5120]{1,0:T(8,128)(2,1)}, u32[]{:S(2)}) %copy-start.3) | copy-done | bytes 1638424
  2.0 2.6 %collective-permute-start.2 = (bf16[80,1280]{1,0:T(8,128)(2,1)S(1)}, bf16[80,1280]{1,0:T(8,128)(2,1)S(1)}, u32[]{:S(2)}, u32[]{:S(2)}) collective-permute-start(bf16[80,1280]{1,0:T(8,128)(2,1)S(1)} %get-tuple-element.73), channel_id=1, source_target_pairs={{0,1},{1,0},{2,3},{3,2},{4,5},{5,4},{6,7},{7,6},{8,9},{9,8},{10,11... | collective-permute-start | bytes 614408 | tf_op jit(solution)/shard_map/ppermute | solution.py:274
  4.7 2.5 %collective-permute-start.1 = (bf16[80,1280]{1,0:T(8,128)(2,1)S(1)}, bf16[80,1280]{1,0:T(8,128)(2,1)S(1)}, u32[]{:S(2)}, u32[]{:S(2)}) collective-permute-start(bf16[80,1280]{1,0:T(8,128)(2,1)S(1)} %get-tuple-element.72), channel_id=1, source_target_pairs={{0,3},{1,2},{2,1},{3,0},{4,6},{5,7},{6,4},{7,5},{8,11},{9,10},{10,... | collective-permute-start | bytes 614408 | tf_op jit(solution)/shard_map/ppermute | solution.py:340
  7.1 1.9 %copy-done = bf16[1280,1280]{1,0:T(8,128)(2,1)S(1)} copy-done((bf16[1280,1280]{1,0:T(8,128)(2,1)S(1)}, bf16[1280,1280]{1,0:T(8,128)(2,1)}, u32[]{:S(2)}) %copy-start) | copy-done | bytes 3276824
  9.1 0.7 shard_map.56
  9.8 2.7 %collective-permute-start.5 = (bf16[160,1280]{1,0:T(8,128)(2,1)S(1)}, bf16[160,1280]{1,0:T(8,128)(2,1)S(1)}, u32[]{:S(2)}, u32[]{:S(2)}) collective-permute-start(bf16[160,1280]{1,0:T(8,128)(2,1)S(1)} %get-tuple-element.81), channel_id=1, source_target_pairs={{0,1},{3,2},{4,5},{7,6},{8,9},{11,10},{12,13},{15,14},{16,17},{19,... | collective-permute-start | bytes 1228808 | tf_op jit(solution)/shard_map/ppermute | solution.py:310
  12.9 4.5 %collective-permute-done.1.refs_0_ = bf16[80,1280]{1,0:T(8,128)(2,1)S(1)} collective-permute-done((bf16[80,1280]{1,0:T(8,128)(2,1)S(1)}, bf16[80,1280]{1,0:T(8,128)(2,1)S(1)}, u32[]{:S(2)}, u32[]{:S(2)}) %collective-permute-start.1) | collective-permute-done | bytes 204832 | tf_op jit(solution)/shard_map/ppermute | solution.py:340
  17.4 1.6 %collective-permute-start.3 = (bf16[80,1280]{1,0:T(8,128)(2,1)S(1)}, bf16[80,1280]{1,0:T(8,128)(2,1)S(1)}, u32[]{:S(2)}, u32[]{:S(2)}) collective-permute-start(bf16[80,1280]{1,0:T(8,128)(2,1)S(1)} %get-tuple-element.76.refs_0_), channel_id=1, source_target_pairs={{0,8},{4,12},{8,0},{12,4},{1,9},{5,13},{9,1},{13,5},{2,10},{6,14},... | collective-permute-start | bytes 614408 | tf_op jit(solution)/shard_map/ppermute | solution.py:274
  19.0 0.8 shard_map.60
  19.8 3.1 %collective-permute-done.5.refs_1_ = bf16[160,1280]{1,0:T(8,128)(2,1)S(1)} collective-permute-done((bf16[160,1280]{1,0:T(8,128)(2,1)S(1)}, bf16[160,1280]{1,0:T(8,128)(2,1)S(1)}, u32[]{:S(2)}, u32[]{:S(2)}) %collective-permute-start.5) | collective-permute-done | bytes 409632 | tf_op jit(solution)/shard_map/ppermute | solution.py:310
  23.4 1.6 %collective-permute-start.7 = (bf16[160,2560]{1,0:T(8,128)(2,1)S(1)}, bf16[160,2560]{1,0:T(8,128)(2,1)S(1)}, u32[]{:S(2)}, u32[]{:S(2)}) collective-permute-start(bf16[160,2560]{1,0:T(8,128)(2,1)S(1)} %get-tuple-element.88), channel_id=1, source_target_pairs={{0,8},{4,12},{8,0},{12,4},{1,9},{5,13},{9,1},{13,5},{2,10},{6,14},... | collective-permute-start | bytes 2457608 | tf_op jit(solution)/shard_map/ppermute | solution.py:274
  25.0 4.2 %collective-permute-start.9 = (bf16[160,1280]{1,0:T(8,128)(2,1)S(1)}, bf16[160,1280]{1,0:T(8,128)(2,1)S(1)}, u32[]{:S(2)}, u32[]{:S(2)}) collective-permute-start(bf16[160,1280]{1,0:T(8,128)(2,1)S(1)} %get-tuple-element.92), channel_id=1, source_target_pairs={{0,1},{3,2},{4,5},{7,6},{8,9},{11,10},{12,13},{15,14},{16,17},{19,... | collective-permute-start | bytes 1228808 | tf_op jit(solution)/shard_map/ppermute | solution.py:310
  29.2 1.3 %shard_map.63 = (f32[160,1280]{1,0:T(8,128)S(1)}, f32[160,1280]{1,0:T(8,128)S(1)}, bf16[160,1280]{1,0:T(8,128)(2,1)S(1)}, bf16[160,1280]{1,0:T(8,128)(2,1)S(1)}, f32[8,128]{1,0:T(8,128)S(1)}) custom-call(bf16[160,1280]{1,0:T(8,128)(2,1)S(1)} %get-tuple-element.84.refs_0_, bf16[160,1280]{1,0:T(8,128)(2,1)S(1)} %collective-permute-done.6.refs_1_, ...), custom_call_target="tpu_custom_call" | custom-call | tf_op jit(solution)/shard_map/pallas_call | solution.py:142
  30.5 2.8 %collective-permute-start.14 = (bf16[160,1280]{1,0:T(8,128)(2,1)S(1)}, bf16[160,1280]{1,0:T(8,128)(2,1)S(1)}, u32[]{:S(2)}, u32[]{:S(2)}) collective-permute-start(bf16[160,1280]{1,0:T(8,128)(2,1)S(1)} %get-tuple-element.102), channel_id=1, source_target_pairs={{0,1},{3,2},{4,5},{7,6},{8,9},{11,10},{12,13},{15,14},{16,17},{19,... | collective-permute-start | bytes 1228808 | tf_op jit(solution)/shard_map/ppermute | solution.py:310
  33.4 1.2 %shard_map.64 = (f32[160,1280]{1,0:T(8,128)S(1)}, bf16[160,1280]{1,0:T(8,128)(2,1)S(1)}, f32[8,128]{1,0:T(8,128)S(1)}) custom-call(bf16[160,2560]{1,0:T(8,128)(2,1)S(1)} %get-tuple-element.71.refs_0_, bf16[1280,1280]{1,0:T(8,128)(2,1)S(1)} %copy-done.2, bf16[1280,1280]{1,0:T(8,128)(2,1)S(1)} %collective-permute-done.refs_5_.refs_2_, ...), custom_call_target="tpu_custom_call" | custom-call | tf_op jit(solution)/shard_map/pallas_call | solution.py:142
  34.6 4.3 %collective-permute-done.9.refs_1_ = bf16[160,1280]{1,0:T(8,128)(2,1)S(1)} collective-permute-done((bf16[160,1280]{1,0:T(8,128)(2,1)S(1)}, bf16[160,1280]{1,0:T(8,128)(2,1)S(1)}, u32[]{:S(2)}, u32[]{:S(2)}) %collective-permute-start.9) | collective-permute-done | bytes 409632 | tf_op jit(solution)/shard_map/ppermute | solution.py:310
  39.8 5.9 %collective-permute-start.11 = (bf16[160,1280]{1,0:T(8,128)(2,1)S(1)}, bf16[160,1280]{1,0:T(8,128)(2,1)S(1)}, u32[]{:S(2)}, u32[]{:S(2)}) collective-permute-start(bf16[160,1280]{1,0:T(8,128)(2,1)S(1)} %get-tuple-element.97), channel_id=1, source_target_pairs={{0,1},{3,2},{4,5},{7,6},{8,9},{11,10},{12,13},{15,14},{16,17},{19,... | collective-permute-start | bytes 1228808 | tf_op jit(solution)/shard_map/ppermute | solution.py:310
  45.8 1.3 %collective-permute-start.15 = (bf16[160,1280]{1,0:T(8,128)(2,1)S(1)}, bf16[160,1280]{1,0:T(8,128)(2,1)S(1)}, u32[]{:S(2)}, u32[]{:S(2)}) collective-permute-start(bf16[160,1280]{1,0:T(8,128)(2,1)S(1)} %get-tuple-element.108), channel_id=1, source_target_pairs={{1,0},{2,3},{5,4},{6,7},{9,8},{10,11},{13,12},{14,15},{17,16},{18,... | collective-permute-start | bytes 1228808 | tf_op jit(solution)/shard_map/ppermute | solution.py:299
  47.1 1.2 %shard_map.67 = (f32[160,1280]{1,0:T(8,128)S(1)}, bf16[160,1280]{1,0:T(8,128)(2,1)S(1)}, f32[8,128]{1,0:T(8,128)S(1)}) custom-call(bf16[160,2560]{1,0:T(8,128)(2,1)S(1)} %collective-permute-done.7.refs_0_, bf16[1280,1280]{1,0:T(8,128)(2,1)S(1)} %copy-done.2, bf16[1280,1280]{1,0:T(8,128)(2,1)S(1)} %collective-permute-done.refs_5_.refs_2_, ...), custom_call_target="tpu_custom_call" | custom-call | tf_op jit(solution)/shard_map/pallas_call | solution.py:142
  48.3 1.6 %collective-permute-start.10 = (bf16[160,1280]{1,0:T(8,128)(2,1)S(1)}, bf16[160,1280]{1,0:T(8,128)(2,1)S(1)}, u32[]{:S(2)}, u32[]{:S(2)}) collective-permute-start(bf16[160,1280]{1,0:T(8,128)(2,1)S(1)} %get-tuple-element.96), channel_id=1, source_target_pairs={{0,8},{4,12},{8,0},{12,4},{1,9},{5,13},{9,1},{13,5},{2,10},{6,14},... | collective-permute-start | bytes 1228808 | tf_op jit(solution)/shard_map/ppermute | solution.py:274
  50.2 3.1 %collective-permute-done.12.refs_1_ = bf16[160,1280]{1,0:T(8,128)(2,1)S(1)} collective-permute-done((bf16[160,1280]{1,0:T(8,128)(2,1)S(1)}, bf16[160,1280]{1,0:T(8,128)(2,1)S(1)}, u32[]{:S(2)}, u32[]{:S(2)}) %collective-permute-start.12) | collective-permute-done | bytes 409632 | tf_op jit(solution)/shard_map/ppermute | solution.py:274
  53.3 1.3 %collective-permute-start.21 = (bf16[160,1280]{1,0:T(8,128)(2,1)S(1)}, bf16[160,1280]{1,0:T(8,128)(2,1)S(1)}, u32[]{:S(2)}, u32[]{:S(2)}) collective-permute-start(bf16[160,1280]{1,0:T(8,128)(2,1)S(1)} %get-tuple-element.119), channel_id=1, source_target_pairs={{1,0},{2,3},{5,4},{6,7},{9,8},{10,11},{13,12},{14,15},{17,16},{18,... | collective-permute-start | bytes 1228808 | tf_op jit(solution)/shard_map/ppermute | solution.py:299
  54.7 1.1 %collective-permute-done.11.refs_1_ = bf16[160,1280]{1,0:T(8,128)(2,1)S(1)} collective-permute-done((bf16[160,1280]{1,0:T(8,128)(2,1)S(1)}, bf16[160,1280]{1,0:T(8,128)(2,1)S(1)}, u32[]{:S(2)}, u32[]{:S(2)}) %collective-permute-start.11) | collective-permute-done | bytes 409632 | tf_op jit(solution)/shard_map/ppermute | solution.py:310
  55.9 1.0 %collective-permute-done.15.refs_2_ = bf16[160,1280]{1,0:T(8,128)(2,1)S(1)} collective-permute-done((bf16[160,1280]{1,0:T(8,128)(2,1)S(1)}, bf16[160,1280]{1,0:T(8,128)(2,1)S(1)}, u32[]{:S(2)}, u32[]{:S(2)}) %collective-permute-start.15) | collective-permute-done | bytes 409632 | tf_op jit(solution)/shard_map/ppermute | solution.py:299
  57.1 4.5 %collective-permute-done.10.refs_1_ = bf16[160,1280]{1,0:T(8,128)(2,1)S(1)} collective-permute-done((bf16[160,1280]{1,0:T(8,128)(2,1)S(1)}, bf16[160,1280]{1,0:T(8,128)(2,1)S(1)}, u32[]{:S(2)}, u32[]{:S(2)}) %collective-permute-start.10) | collective-permute-done | bytes 409632 | tf_op jit(solution)/shard_map/ppermute | solution.py:274
  61.9 1.3 %collective-permute-start.19 = (bf16[160,1280]{1,0:T(8,128)(2,1)S(1)}, bf16[160,1280]{1,0:T(8,128)(2,1)S(1)}, u32[]{:S(2)}, u32[]{:S(2)}) collective-permute-start(bf16[160,1280]{1,0:T(8,128)(2,1)S(1)} %get-tuple-element.116), channel_id=1, source_target_pairs={{1,0},{2,3},{5,4},{6,7},{9,8},{10,11},{13,12},{14,15},{17,16},{18,... | collective-permute-start | bytes 1228808 | tf_op jit(solution)/shard_map/ppermute | solution.py:299
  63.7 2.0 %collective-permute-done.21.refs_2_ = bf16[160,1280]{1,0:T(8,128)(2,1)S(1)} collective-permute-done((bf16[160,1280]{1,0:T(8,128)(2,1)S(1)}, bf16[160,1280]{1,0:T(8,128)(2,1)S(1)}, u32[]{:S(2)}, u32[]{:S(2)}) %collective-permute-start.21) | collective-permute-done | bytes 409632 | tf_op jit(solution)/shard_map/ppermute | solution.py:299
  65.9 1.3 %collective-permute-start.22 = (bf16[160,1280]{1,0:T(8,128)(2,1)S(1)}, bf16[160,1280]{1,0:T(8,128)(2,1)S(1)}, u32[]{:S(2)}, u32[]{:S(2)}) collective-permute-start(bf16[160,1280]{1,0:T(8,128)(2,1)S(1)} %get-tuple-element.130), channel_id=1, source_target_pairs={{1,0},{2,3},{5,4},{6,7},{9,8},{10,11},{13,12},{14,15},{17,16},{18,... | collective-permute-start | bytes 1228808 | tf_op jit(solution)/shard_map/ppermute | solution.py:299
  67.2 8.8 %collective-permute-done.19.refs_2_ = bf16[160,1280]{1,0:T(8,128)(2,1)S(1)} collective-permute-done((bf16[160,1280]{1,0:T(8,128)(2,1)S(1)}, bf16[160,1280]{1,0:T(8,128)(2,1)S(1)}, u32[]{:S(2)}, u32[]{:S(2)}) %collective-permute-start.19) | collective-permute-done | bytes 409632 | tf_op jit(solution)/shard_map/ppermute | solution.py:299
  76.2 2.3 %shard_map.78 = (bf16[4,1280,512]{2,1,0:T(8,128)(2,1)S(1)}, s32[8]{0:T(128)S(1)}, f32[8,128]{1,0:T(8,128)}) custom-call(s32[5,128]{1,0:T(8,128)S(1)} %bitcast.1, bf16[160,1280]{1,0:T(8,128)(2,1)S(1)} %get-tuple-element.111.own, bf16[160,1280]{1,0:T(8,128)(2,1)S(1)} %get-tuple-element.112.other_chip, ...), custom_call_target="tpu_custom_call" | custom-call | tf_op jit(solution)/shard_map/pallas_call | solution.py:195
  78.5 5.9 %collective-permute-done.22.outward = bf16[160,1280]{1,0:T(8,128)(2,1)S(1)} collective-permute-done((bf16[160,1280]{1,0:T(8,128)(2,1)S(1)}, bf16[160,1280]{1,0:T(8,128)(2,1)S(1)}, u32[]{:S(2)}, u32[]{:S(2)}) %collective-permute-start.22) | collective-permute-done | bytes 409632 | tf_op jit(solution)/shard_map/ppermute | solution.py:299
  84.4 8.9 %shard_map.79 = f32[1280,1280]{1,0:T(8,128)} custom-call(s32[8]{0:T(128)S(1)} %get-tuple-element.124.place, bf16[4,1280,512]{2,1,0:T(8,128)(2,1)S(1)} %get-tuple-element.125.turned, bf16[160,1280]{1,0:T(8,128)(2,1)S(1)} %get-tuple-element.126.one, bf16[160,1280]{1,0:T(8,128)(2,1)S(1)} %get-tuple-element.127.two, ...), custom_call_target="tpu_custom_call" | custom-call | tf_op jit(solution)/shard_map/pallas_call | solution.py:259
  (51 shorter events, 4.2 us)
Async XLA Ops:
  0.0 19.0 %collective-permute-start = (bf16[1280,1280]{1,0:T(8,128)(2,1)}, bf16[1280,1280]{1,0:T(8,128)(2,1)S(1)}, u32[]{:S(2)}, u32[]{:S(2)}) collective-permute-start(bf16[1280,1280]{1,0:T(8,128)(2,1)} %refs_1_.5), channel_id=1, source_target_pairs={{0,4},{4,0},{8,12},{12,8},{1,5},{5,1},{9,13},{13,9},{2,6},{6,2},{1... | collective-permute-start | bytes 9830408 | tf_op jit(solution)/shard_map/ppermute | solution.py:274
  0.5 1.4 %copy-start.3 = (bf16[160,5120]{1,0:T(8,128)(2,1)S(1)}, bf16[160,5120]{1,0:T(8,128)(2,1)}, u32[]{:S(2)}) copy-start(bf16[160,5120]{1,0:T(8,128)(2,1)} %grad.1) | copy-start | bytes 4915204
  1.9 10.7 %copy-start.4 = (bf16[160,5120]{1,0:T(8,128)(2,1)S(1)}, bf16[160,5120]{1,0:T(8,128)(2,1)}, u32[]{:S(2)}) copy-start(bf16[160,5120]{1,0:T(8,128)(2,1)} %act.1) | copy-start | bytes 4915204
  2.0 10.7 %collective-permute-start.2 = (bf16[80,1280]{1,0:T(8,128)(2,1)S(1)}, bf16[80,1280]{1,0:T(8,128)(2,1)S(1)}, u32[]{:S(2)}, u32[]{:S(2)}) collective-permute-start(bf16[80,1280]{1,0:T(8,128)(2,1)S(1)} %get-tuple-element.73), channel_id=1, source_target_pairs={{0,1},{1,0},{2,3},{3,2},{4,5},{5,4},{6,7},{7,6},{8,9},{9,8},{10,11... | collective-permute-start | bytes 614408 | tf_op jit(solution)/shard_map/ppermute | solution.py:274
  4.7 12.8 %collective-permute-start.1 = (bf16[80,1280]{1,0:T(8,128)(2,1)S(1)}, bf16[80,1280]{1,0:T(8,128)(2,1)S(1)}, u32[]{:S(2)}, u32[]{:S(2)}) collective-permute-start(bf16[80,1280]{1,0:T(8,128)(2,1)S(1)} %get-tuple-element.72), channel_id=1, source_target_pairs={{0,3},{1,2},{2,1},{3,0},{4,6},{5,7},{6,4},{7,5},{8,11},{9,10},{10,... | collective-permute-start | bytes 614408 | tf_op jit(solution)/shard_map/ppermute | solution.py:340
  7.1 1.9 %copy-start = (bf16[1280,1280]{1,0:T(8,128)(2,1)S(1)}, bf16[1280,1280]{1,0:T(8,128)(2,1)}, u32[]{:S(2)}) copy-start(bf16[1280,1280]{1,0:T(8,128)(2,1)} %refs_2_.1) | copy-start | bytes 9830404
  9.1 9.9 %copy-start.1 = (bf16[1280,1280]{1,0:T(8,128)(2,1)S(1)}, bf16[1280,1280]{1,0:T(8,128)(2,1)}, u32[]{:S(2)}) copy-start(bf16[1280,1280]{1,0:T(8,128)(2,1)} %refs_2_.1) | copy-start | bytes 9830404
  9.8 13.1 %collective-permute-start.5 = (bf16[160,1280]{1,0:T(8,128)(2,1)S(1)}, bf16[160,1280]{1,0:T(8,128)(2,1)S(1)}, u32[]{:S(2)}, u32[]{:S(2)}) collective-permute-start(bf16[160,1280]{1,0:T(8,128)(2,1)S(1)} %get-tuple-element.81), channel_id=1, source_target_pairs={{0,1},{3,2},{4,5},{7,6},{8,9},{11,10},{12,13},{15,14},{16,17},{19,... | collective-permute-start | bytes 1228808 | tf_op jit(solution)/shard_map/ppermute | solution.py:310
  12.8 6.2 %collective-permute-start.4 = (bf16[80,1280]{1,0:T(8,128)(2,1)S(1)}, bf16[80,1280]{1,0:T(8,128)(2,1)S(1)}, u32[]{:S(2)}, u32[]{:S(2)}) collective-permute-start(bf16[80,1280]{1,0:T(8,128)(2,1)S(1)} %get-tuple-element.77.refs_0_), channel_id=1, source_target_pairs={{0,4},{4,0},{8,12},{12,8},{1,5},{5,1},{9,13},{13,9},{2,6},{6,2},{1... | collective-permute-start | bytes 614408 | tf_op jit(solution)/shard_map/ppermute | solution.py:274
  17.4 5.8 %collective-permute-start.3 = (bf16[80,1280]{1,0:T(8,128)(2,1)S(1)}, bf16[80,1280]{1,0:T(8,128)(2,1)S(1)}, u32[]{:S(2)}, u32[]{:S(2)}) collective-permute-start(bf16[80,1280]{1,0:T(8,128)(2,1)S(1)} %get-tuple-element.76.refs_0_), channel_id=1, source_target_pairs={{0,8},{4,12},{8,0},{12,4},{1,9},{5,13},{9,1},{13,5},{2,10},{6,14},... | collective-permute-start | bytes 614408 | tf_op jit(solution)/shard_map/ppermute | solution.py:274
  19.8 13.6 %copy-start.2 = (bf16[1280,1280]{1,0:T(8,128)(2,1)S(1)}, bf16[1280,1280]{1,0:T(8,128)(2,1)}, u32[]{:S(2)}) copy-start(bf16[1280,1280]{1,0:T(8,128)(2,1)} %refs_1_.5) | copy-start | bytes 9830404
  23.3 5.9 %collective-permute-start.6 = (bf16[160,1280]{1,0:T(8,128)(2,1)S(1)}, bf16[160,1280]{1,0:T(8,128)(2,1)S(1)}, u32[]{:S(2)}, u32[]{:S(2)}) collective-permute-start(bf16[160,1280]{1,0:T(8,128)(2,1)S(1)} %get-tuple-element.84.refs_0_), channel_id=1, source_target_pairs={{0,4},{4,0},{8,12},{12,8},{1,5},{5,1},{9,13},{13,9},{2,6},{6,2},{1... | collective-permute-start | bytes 1228808 | tf_op jit(solution)/shard_map/ppermute | solution.py:274
  23.4 22.4 %collective-permute-start.7 = (bf16[160,2560]{1,0:T(8,128)(2,1)S(1)}, bf16[160,2560]{1,0:T(8,128)(2,1)S(1)}, u32[]{:S(2)}, u32[]{:S(2)}) collective-permute-start(bf16[160,2560]{1,0:T(8,128)(2,1)S(1)} %get-tuple-element.88), channel_id=1, source_target_pairs={{0,8},{4,12},{8,0},{12,4},{1,9},{5,13},{9,1},{13,5},{2,10},{6,14},... | collective-permute-start | bytes 2457608 | tf_op jit(solution)/shard_map/ppermute | solution.py:274
  25.0 14.0 %collective-permute-start.9 = (bf16[160,1280]{1,0:T(8,128)(2,1)S(1)}, bf16[160,1280]{1,0:T(8,128)(2,1)S(1)}, u32[]{:S(2)}, u32[]{:S(2)}) collective-permute-start(bf16[160,1280]{1,0:T(8,128)(2,1)S(1)} %get-tuple-element.92), channel_id=1, source_target_pairs={{0,1},{3,2},{4,5},{7,6},{8,9},{11,10},{12,13},{15,14},{16,17},{19,... | collective-permute-start | bytes 1228808 | tf_op jit(solution)/shard_map/ppermute | solution.py:310
  29.1 10.6 %collective-permute-start.8 = (bf16[160,1280]{1,0:T(8,128)(2,1)S(1)}, bf16[160,1280]{1,0:T(8,128)(2,1)S(1)}, u32[]{:S(2)}, u32[]{:S(2)}) collective-permute-start(bf16[160,1280]{1,0:T(8,128)(2,1)S(1)} %get-tuple-element.90), channel_id=1, source_target_pairs={{0,4},{1,2},{2,1},{3,7},{4,0},{5,6},{6,5},{7,3},{8,12},{9,10},{10,... | collective-permute-start | bytes 1228808 | tf_op jit(solution)/shard_map/ppermute | solution.py:291
  30.5 17.8 %collective-permute-start.14 = (bf16[160,1280]{1,0:T(8,128)(2,1)S(1)}, bf16[160,1280]{1,0:T(8,128)(2,1)S(1)}, u32[]{:S(2)}, u32[]{:S(2)}) collective-permute-start(bf16[160,1280]{1,0:T(8,128)(2,1)S(1)} %get-tuple-element.102), channel_id=1, source_target_pairs={{0,1},{3,2},{4,5},{7,6},{8,9},{11,10},{12,13},{15,14},{16,17},{19,... | collective-permute-start | bytes 1228808 | tf_op jit(solution)/shard_map/ppermute | solution.py:310
  39.1 11.0 %collective-permute-start.13 = (bf16[160,1280]{1,0:T(8,128)(2,1)S(1)}, bf16[160,1280]{1,0:T(8,128)(2,1)S(1)}, u32[]{:S(2)}, u32[]{:S(2)}) collective-permute-start(bf16[160,1280]{1,0:T(8,128)(2,1)S(1)} %get-tuple-element.101), channel_id=1, source_target_pairs={{0,4},{1,2},{2,1},{3,7},{4,0},{5,6},{6,5},{7,3},{8,12},{9,10},{10,... | collective-permute-start | bytes 1228808 | tf_op jit(solution)/shard_map/ppermute | solution.py:291
  39.2 14.1 %collective-permute-start.12 = (bf16[160,1280]{1,0:T(8,128)(2,1)S(1)}, bf16[160,1280]{1,0:T(8,128)(2,1)S(1)}, u32[]{:S(2)}, u32[]{:S(2)}) collective-permute-start(bf16[160,1280]{1,0:T(8,128)(2,1)S(1)} %get-tuple-element.99), channel_id=1, source_target_pairs={{0,8},{4,12},{8,0},{12,4},{1,9},{5,13},{9,1},{13,5},{2,10},{6,14},... | collective-permute-start | bytes 1228808 | tf_op jit(solution)/shard_map/ppermute | solution.py:274
  39.8 16.0 %collective-permute-start.11 = (bf16[160,1280]{1,0:T(8,128)(2,1)S(1)}, bf16[160,1280]{1,0:T(8,128)(2,1)S(1)}, u32[]{:S(2)}, u32[]{:S(2)}) collective-permute-start(bf16[160,1280]{1,0:T(8,128)(2,1)S(1)} %get-tuple-element.97), channel_id=1, source_target_pairs={{0,1},{3,2},{4,5},{7,6},{8,9},{11,10},{12,13},{15,14},{16,17},{19,... | collective-permute-start | bytes 1228808 | tf_op jit(solution)/shard_map/ppermute | solution.py:310
  45.8 11.2 %collective-permute-start.15 = (bf16[160,1280]{1,0:T(8,128)(2,1)S(1)}, bf16[160,1280]{1,0:T(8,128)(2,1)S(1)}, u32[]{:S(2)}, u32[]{:S(2)}) collective-permute-start(bf16[160,1280]{1,0:T(8,128)(2,1)S(1)} %get-tuple-element.108), channel_id=1, source_target_pairs={{1,0},{2,3},{5,4},{6,7},{9,8},{10,11},{13,12},{14,15},{17,16},{18,... | collective-permute-start | bytes 1228808 | tf_op jit(solution)/shard_map/ppermute | solution.py:299
  48.3 13.3 %collective-permute-start.10 = (bf16[160,1280]{1,0:T(8,128)(2,1)S(1)}, bf16[160,1280]{1,0:T(8,128)(2,1)S(1)}, u32[]{:S(2)}, u32[]{:S(2)}) collective-permute-start(bf16[160,1280]{1,0:T(8,128)(2,1)S(1)} %get-tuple-element.96), channel_id=1, source_target_pairs={{0,8},{4,12},{8,0},{12,4},{1,9},{5,13},{9,1},{13,5},{2,10},{6,14},... | collective-permute-start | bytes 1228808 | tf_op jit(solution)/shard_map/ppermute | solution.py:274
  50.1 11.7 %collective-permute-start.18 = (bf16[160,1280]{1,0:T(8,128)(2,1)S(1)}, bf16[160,1280]{1,0:T(8,128)(2,1)S(1)}, u32[]{:S(2)}, u32[]{:S(2)}) collective-permute-start(bf16[160,1280]{1,0:T(8,128)(2,1)S(1)} %get-tuple-element.114), channel_id=1, source_target_pairs={{0,4},{1,2},{2,1},{3,7},{4,0},{5,6},{6,5},{7,3},{8,12},{9,10},{10,... | collective-permute-start | bytes 1228808 | tf_op jit(solution)/shard_map/ppermute | solution.py:291
  53.3 12.5 %collective-permute-start.21 = (bf16[160,1280]{1,0:T(8,128)(2,1)S(1)}, bf16[160,1280]{1,0:T(8,128)(2,1)S(1)}, u32[]{:S(2)}, u32[]{:S(2)}) collective-permute-start(bf16[160,1280]{1,0:T(8,128)(2,1)S(1)} %get-tuple-element.119), channel_id=1, source_target_pairs={{1,0},{2,3},{5,4},{6,7},{9,8},{10,11},{13,12},{14,15},{17,16},{18,... | collective-permute-start | bytes 1228808 | tf_op jit(solution)/shard_map/ppermute | solution.py:299
  55.9 10.0 %collective-permute-start.20 = (bf16[160,1280]{1,0:T(8,128)(2,1)S(1)}, bf16[160,1280]{1,0:T(8,128)(2,1)S(1)}, u32[]{:S(2)}, u32[]{:S(2)}) collective-permute-start(bf16[160,1280]{1,0:T(8,128)(2,1)S(1)} %get-tuple-element.117), channel_id=1, source_target_pairs={{0,4},{1,2},{2,1},{3,7},{4,0},{5,6},{6,5},{7,3},{8,12},{9,10},{10,... | collective-permute-start | bytes 1228808 | tf_op jit(solution)/shard_map/ppermute | solution.py:291
  61.6 14.6 %copy-start.5 = (s32[640]{0:T(1024)S(1)}, s32[640]{0:T(1024)}, u32[]{:S(2)}) copy-start(s32[640]{0:T(1024)} %param.9) | copy-start | bytes 7684
  61.7 14.4 %collective-permute-start.16 = (bf16[160,1280]{1,0:T(8,128)(2,1)S(1)}, bf16[160,1280]{1,0:T(8,128)(2,1)S(1)}, u32[]{:S(2)}, u32[]{:S(2)}) collective-permute-start(bf16[160,1280]{1,0:T(8,128)(2,1)S(1)} %get-tuple-element.111.own), channel_id=1, source_target_pairs={{0,4},{4,0},{8,12},{12,8},{1,5},{5,1},{9,13},{13,9},{2,6},{6,2},{1... | collective-permute-start | bytes 1228808 | tf_op jit(solution)/shard_map/ppermute | solution.py:274
  61.9 14.2 %collective-permute-start.19 = (bf16[160,1280]{1,0:T(8,128)(2,1)S(1)}, bf16[160,1280]{1,0:T(8,128)(2,1)S(1)}, u32[]{:S(2)}, u32[]{:S(2)}) collective-permute-start(bf16[160,1280]{1,0:T(8,128)(2,1)S(1)} %get-tuple-element.116), channel_id=1, source_target_pairs={{1,0},{2,3},{5,4},{6,7},{9,8},{10,11},{13,12},{14,15},{17,16},{18,... | collective-permute-start | bytes 1228808 | tf_op jit(solution)/shard_map/ppermute | solution.py:299
  63.2 13.0 %collective-permute-start.17 = (bf16[160,1280]{1,0:T(8,128)(2,1)S(1)}, bf16[160,1280]{1,0:T(8,128)(2,1)S(1)}, u32[]{:S(2)}, u32[]{:S(2)}) collective-permute-start(bf16[160,1280]{1,0:T(8,128)(2,1)S(1)} %get-tuple-element.112.other_chip), channel_id=1, source_target_pairs={{0,4},{4,0},{8,12},{12,8},{1,5},{5,1},{9,13},{13,9},{2,6},{6,2},{1... | collective-permute-start | bytes 1228808 | tf_op jit(solution)/shard_map/ppermute | solution.py:274
  65.9 18.5 %collective-permute-start.22 = (bf16[160,1280]{1,0:T(8,128)(2,1)S(1)}, bf16[160,1280]{1,0:T(8,128)(2,1)S(1)}, u32[]{:S(2)}, u32[]{:S(2)}) collective-permute-start(bf16[160,1280]{1,0:T(8,128)(2,1)S(1)} %get-tuple-element.130), channel_id=1, source_target_pairs={{1,0},{2,3},{5,4},{6,7},{9,8},{10,11},{13,12},{14,15},{17,16},{18,... | collective-permute-start | bytes 1228808 | tf_op jit(solution)/shard_map/ppermute | solution.py:299
